TPU v7x, 128 devices: a whole 4x4x4 slice. The times are simulated.
128 devices in a mesh: outer: 32 (over z, y, core), sw: 4 (over x).
Axes of the slice: x: 4, y: 4, z: 4, core: 2. Of those that a mesh axis runs over, the one named last changes fastest.
Arguments:
- path_state: bfloat16 [65536, 256], P(('outer', 'sw')), may hold values from -6 to 6
- link_state: bfloat16 [262144, 256], P(('outer', 'sw')), may hold values from -6 to 6
- hop_slot: int32 [65536, 8], P(('outer', 'sw')), may hold values from 0 to 1023
- hop_count: int32 [65536], P(('outer', 'sw')), may hold values from 2 to 8
- send_rows: int32 [16384, 8], P(('outer', 'sw')), may hold values from 0 to 2047
- w_input: bfloat16 [256, 768], replicated, may hold values from -0.375 to 0.375
- w_state: bfloat16 [256, 768], replicated, may hold values from -0.375 to 0.375
- w_agg: bfloat16 [256, 256], replicated, may hold values from -0.375 to 0.375
- path_cot: bfloat16 [65536, 256], P(('outer', 'sw')), may hold values from -6 to 6
- link_cot: bfloat16 [262144, 256], P(('outer', 'sw')), may hold values from -6 to 6
Outputs:
- grad_path: float32 [65536, 256], P(('outer', 'sw'))
- grad_link: float32 [262144, 256], P(('outer', 'sw'))
- grad_w_input: float32 [256, 768], replicated
- grad_w_state: float32 [256, 768], replicated
- grad_w_agg: float32 [256, 256], replicated
Inputs may be any that keep to these rules, and one draw needn't show every extreme that they name: `hop_slot`: A slot s of a path on device q names row send_rows[(s // 8) * 128 + q, s % 8] of the links owned by device s // 8. `send_rows`: row q * 128 + d lists local link indices of device q sent to device d; an index may repeat.
All inputs are finite; a program needn't handle non-finite values.
Results may differ from a plain program's by a relative error of at most 0.0095.
Values may be sent and summed in bfloat16 or wider, within the bound.
No kernel may reach another device: no remote copies, remote signals or barrier semaphores. Data moves between devices by JAX's collectives and lax.ppermute only.
A program may use at most 192 MiB of HBM per device.

v0:
```python
import math

import jax
import jax.numpy as jnp
from jax import lax
from jax.sharding import PartitionSpec as P


def gru_path(start_state, hop_inputs, hop_valid, input_weight, state_weight):
    width = start_state.shape[1]

    def hop_step(carried, hop_item):
        link_rows, keep_mask = hop_item
        from_input = jnp.dot(
            link_rows, input_weight.astype(jnp.bfloat16), preferred_element_type=jnp.float32
        )
        from_state = jnp.dot(
            carried.astype(jnp.bfloat16),
            state_weight.astype(jnp.bfloat16),
            preferred_element_type=jnp.float32,
        )
        reset_gate = jax.nn.sigmoid(from_input[:, :width] + from_state[:, :width])
        update_gate = jax.nn.sigmoid(
            from_input[:, width : 2 * width] + from_state[:, width : 2 * width]
        )
        candidate = jnp.tanh(from_input[:, 2 * width :] + reset_gate * from_state[:, 2 * width :])
        proposed = (1.0 - update_gate) * candidate + update_gate * carried
        keep_col = keep_mask[:, None]
        carried = keep_col * proposed + (1.0 - keep_col) * carried
        message = (keep_col * carried).astype(jnp.bfloat16)
        return (carried, message)

    return lax.scan(hop_step, start_state, (hop_inputs, hop_valid))


def link_backward(agg_round, w_agg, link_cot):
    preact = jnp.dot(agg_round, w_agg, preferred_element_type=jnp.float32)
    activated = jnp.tanh(preact)
    grad_pre = link_cot.astype(jnp.float32) * (1.0 - activated * activated)
    d_agg = jnp.dot(grad_pre, w_agg.astype(jnp.float32).T, precision=lax.Precision.HIGHEST).astype(
        jnp.bfloat16
    )
    wgrad = jnp.dot(agg_round.astype(jnp.float32).T, grad_pre, precision=lax.Precision.HIGHEST)
    return (link_cot.astype(jnp.float32), d_agg, wgrad)


def to_paths(rows):
    return lax.all_to_all(rows, ("outer", "sw"), split_axis=0, concat_axis=0, tiled=True)


def to_owners(sums):
    return lax.all_to_all(sums, ("outer", "sw"), split_axis=0, concat_axis=0, tiled=True)


def per_device(
    path_state,
    link_state,
    hop_slot,
    hop_count,
    send_rows,
    w_input,
    w_state,
    w_agg,
    path_cot,
    link_cot,
):
    devices = lax.axis_size("outer") * lax.axis_size("sw")
    paths, width = path_state.shape
    links = link_state.shape[0]
    capacity = send_rows.shape[1]
    hop_slots = hop_slot.T
    flat_slots = hop_slots.reshape(-1)
    flat_rows = send_rows.reshape(-1)
    hop_valid = (
        jnp.arange(hop_slot.shape[1], dtype=jnp.int32)[:, None] < hop_count[None, :]
    ).astype(jnp.float32)
    row_table = to_paths(link_state[send_rows]).reshape(devices * capacity, width)
    hop_inputs = row_table[hop_slots]

    def path_fn(start_state, inputs_here, input_weight, state_weight):
        return gru_path(start_state, inputs_here, hop_valid, input_weight, state_weight)

    outputs, pullback = jax.vjp(
        path_fn,
        path_state.astype(jnp.float32),
        hop_inputs,
        w_input.astype(jnp.float32),
        w_state.astype(jnp.float32),
    )
    messages = outputs[1]
    slot_sums = (
        jnp.zeros((devices * capacity, width), jnp.float32)
        .at[flat_slots]
        .add(messages.reshape(-1, width).astype(jnp.float32))
    )
    arrived = to_owners(slot_sums.reshape(devices, capacity, width))
    aggregate = jnp.zeros((links, width), jnp.float32).at[flat_rows].add(arrived.reshape(-1, width))
    link_grad, d_agg, wagg_grad = link_backward(aggregate.astype(jnp.bfloat16), w_agg, link_cot)
    back_table = to_paths(d_agg[send_rows]).reshape(devices * capacity, width)
    d_messages = back_table[hop_slots]
    d_start, d_inputs, d_input_w, d_state_w = pullback((path_cot.astype(jnp.float32), d_messages))
    input_sums = (
        jnp.zeros((devices * capacity, width), jnp.float32)
        .at[flat_slots]
        .add(d_inputs.reshape(-1, width).astype(jnp.float32))
    )
    returned = to_owners(input_sums.reshape(devices, capacity, width))
    grad_link = link_grad + jnp.zeros((links, width), jnp.float32).at[flat_rows].add(
        returned.reshape(-1, width)
    )
    input_total, state_total, wagg_total = lax.psum(
        (d_input_w, d_state_w, wagg_grad), ("outer", "sw")
    )
    path_scale = 1.0 / math.sqrt(paths * devices)
    link_scale = 1.0 / math.sqrt(links * devices)
    return (
        d_start,
        grad_link,
        input_total * path_scale,
        state_total * path_scale,
        wagg_total * link_scale,
    )


def solution(mesh):
    return jax.shard_map(
        per_device,
        mesh=mesh,
        in_specs=(
            P(("outer", "sw"), None),
            P(("outer", "sw"), None),
            P(("outer", "sw"), None),
            P(("outer", "sw")),
            P(("outer", "sw"), None),
            P(),
            P(),
            P(),
            P(("outer", "sw"), None),
            P(("outer", "sw"), None),
        ),
        out_specs=(P(("outer", "sw"), None), P(("outer", "sw"), None), P(), P(), P()),
        check_vma=False,
    )
```

profile of v0, /device:TPU:1, one launch (start us, length us, event | category | flops | bytes accessed | tf_op | source)
XLA Modules:
  0.0 487.3 jit_solution(6531521434180947859)
XLA Ops:
  8.4 5.0 %gather_fusion = bf16[1024,256]{1,0:T(8,128)(2,1)} fusion(bf16[2048,256]{1,0:T(8,128)(2,1)S(1)} %copy-done, s32[1024]{0:T(1024)S(1)} %broadcast_clamp_fusion.1), kind=kCustom, calls=%fused_computation | custom fusion | bytes 1052672 | tf_op jit(solution)/shard_map/gather | solution.py:77
  13.4 11.5 %all-to-all-start = ((bf16[128,8,256]{2,1,0:T(8,128)(2,1)}), bf16[128,8,256]{2,1,0:T(8,128)(2,1)S(1)}, u32[]{:S(2)}, u32[]{:S(2)}) async-start(bf16[128,8,256]{2,1,0:T(8,128)(2,1)} %bitcast.14), calls=%async_computation | async-start | bytes 1048576 | tf_op jit(solution)/shard_map/all_to_all | solution.py:48
  26.3 12.6 %all-to-all-done = bf16[128,8,256]{2,1,0:T(8,128)(2,1)S(1)} async-done(((bf16[128,8,256]{2,1,0:T(8,128)(2,1)}), bf16[128,8,256]{2,1,0:T(8,128)(2,1)S(1)}, u32[]{:S(2)}, u32[]{:S(2)}) %all-to-all-start) | async-done | bytes 524320 | tf_op jit(solution)/shard_map/all_to_all | solution.py:48
  38.9 14.6 %gather_fusion.1 = bf16[4096,256]{1,0:T(8,128)(2,1)S(1)} fusion(bf16[1024,256]{1,0:T(8,128)(2,1)S(1)} %bitcast.178, s32[4096]{0:T(1024)S(1)} %broadcast_clamp_fusion), kind=kCustom, calls=%fused_computation.1 | custom fusion | bytes 4210688 | tf_op jit(solution)/shard_map/gather | solution.py:78
  56.5 67.6 %while.57 = (s32[]{:T(128)}, f32[512,256]{1,0:T(8,128)S(1)}, bf16[8,512,256]{2,1,0:T(8,128)(2,1)}, bf16[8,512,256]{2,1,0:T(8,128)(2,1)}, f32[8,512,256]{2,1,0:T(...) while((s32[]{:T(128)}, f32[512,256]{1,0:T(8,128)S(1)}, ...), condition=%wide.region_1.2_spmd, body=%wide.region_0.1_spmd.sunk | while | flops 406324224 | bytes 17847480 | solution.py:33
  124.1 22.1 %scatter_custom_fusion = f32[1024,256]{1,0:T(8,128)} fusion(s32[4096]{0:T(1024)} %bitcast.191, bf16[4096,256]{1,0:T(8,128)(2,1)} %bitcast.181, f32[]{:T(128)} %constant.105.clone.1), kind=kCustom, calls=%fused_computation.97 | custom fusion | flops 2097152 | bytes 3146240 | tf_op jit(solution)/shard_map/scatter-add | solution.py:94
  146.2 4.9 all-to-all-start.1
  151.3 19.1 %all-to-all-done.1 = f32[128,8,256]{2,1,0:T(8,128)} async-done(((f32[128,8,256]{2,1,0:T(8,128)}), f32[128,8,256]{2,1,0:T(8,128)}, u32[]{:S(2)}, u32[]{:S(2)}) %all-to-all-start.1) | async-done | bytes 1048608 | tf_op jit(solution)/shard_map/all_to_all | solution.py:52
  170.4 7.1 %scatter_custom_fusion.1 = f32[2048,256]{1,0:T(8,128)S(1)} fusion(s32[1024]{0:T(1024)S(1)} %bitcast.193, f32[128,8,256]{2,1,0:T(8,128)} %all-to-all-done.1, f32[]{:T(128)} %constant.105.clone.1), kind=kCustom, calls=%fused_computation.106 | custom fusion | flops 262144 | bytes 3145732 | tf_op jit(solution)/shard_map/scatter-add | solution.py:97
  181.7 5.0 %gather_fusion.2 = bf16[1024,256]{1,0:T(8,128)(2,1)} fusion(bf16[2048,256]{1,0:T(8,128)(2,1)S(1)} %convolution_convert_fusion.4, s32[1024]{0:T(1024)S(1)} %broadcast_clamp_fusion.1), kind=kCustom, calls=%fused_computation.2 | custom fusion | bytes 1052672 | tf_op jit(solution)/shard_map/gather | solution.py:99
  186.7 4.0 all-to-all-start.2
  191.6 4.4 fusion.59
  196.0 8.9 %all-to-all-done.2 = bf16[128,8,256]{2,1,0:T(8,128)(2,1)S(1)} async-done(((bf16[128,8,256]{2,1,0:T(8,128)(2,1)}), bf16[128,8,256]{2,1,0:T(8,128)(2,1)S(1)}, u32[]{:S(2)}, u32[]{:S(2)}) %all-to-all-start.2) | async-done | bytes 524320 | tf_op jit(solution)/shard_map/all_to_all | solution.py:48
  204.8 17.0 %gather_fusion.3 = bf16[4096,256]{1,0:T(8,128)(2,1)} fusion(bf16[1024,256]{1,0:T(8,128)(2,1)S(1)} %bitcast.179, s32[4096]{0:T(1024)S(1)} %copy-done.13), kind=kCustom, calls=%fused_computation.3 | custom fusion | bytes 4210688 | tf_op jit(solution)/shard_map/gather | solution.py:100
  223.3 95.7 %while.58 = (s32[]{:T(128)}, f32[256,768]{1,0:T(8,128)S(1)}, f32[256,768]{1,0:T(8,128)}, f32[512,256]{1,0:T(8,128)}, bf16[8,512,256]{2,1,0:T(8,128)(2,1)}, /*ind...) while((s32[]{:T(128)}, f32[256,768]{1,0:T(8,128)S(1)}, ...), condition=%wide.region_5.6_spmd.clone, body=%wide.region_4.5_spmd.clone.sunk | while | flops 813301760 | bytes 20461832 | solution.py:33
  228.7 2.6 fusion.107
  240.5 2.6 fusion.107
  243.1 2.5 fusion.106
  252.5 2.6 fusion.107
  255.1 2.5 fusion.106
  264.5 2.6 fusion.107
  276.4 2.6 fusion.107
  279.0 2.5 fusion.106
  288.5 2.6 fusion.107
  291.1 2.5 fusion.106
  300.5 2.6 fusion.107
  312.5 2.6 fusion.107
  319.9 22.0 %scatter_custom_fusion.2 = f32[1024,256]{1,0:T(8,128)} fusion(s32[4096]{0:T(1024)} %bitcast.192, bf16[4096,256]{1,0:T(8,128)(2,1)} %bitcast.45, f32[]{:T(128)} %constant.105.clone.1), kind=kCustom, calls=%fused_computation.95 | custom fusion | flops 2097152 | bytes 3146240 | tf_op jit(solution)/shard_map/scatter-add | solution.py:105
  341.9 3.8 all-to-all-start.3
  347.1 120.0 %all-reduce.7.cloned.1.call-done = (f32[256,768]{1,0:T(8,128)}, f32[256,768]{1,0:T(8,128)}, f32[256,256]{1,0:T(8,128)}) async-done(((f32[256,768]{1,0:T(8,128)}, f32[256,768]{1,0:T(8,128)}, f32[256,256]{1,0:T(8,128)}), (f32[256,768]{1,0:T(8,128)}, f32[256,768]{1,0:T(8,128)}, f32[256,256]{1,0:T(8,128)})) %all-reduce.7.cloned.1.call-update) | async-done | bytes 1835024 | tf_op jit(solution)/shard_map/psum | solution.py:111
  468.8 2.7 broadcast_multiply_fusion
  471.5 9.0 %scatter_custom_fusion.3 = f32[2048,256]{1,0:T(8,128)} fusion(f32[2048,256]{1,0:T(8,128)} %convert_element_type.121, s32[1024]{0:T(1024)S(1)} %bitcast.194, f32[128,8,256]{2,1,0:T(8,128)S(1)} %all-to-all-done.3), kind=kCustom, calls=%fused_computation.104 | custom fusion | flops 262144 | bytes 3145728 | tf_op jit(solution)/shard_map/scatter-add | solution.py:108
  (188 shorter events, 148.4 us)
Async XLA Ops:
  7.2 1.2 copy-start
  8.4 16.5 %copy-start.14 = (s32[512,8]{0,1:T(8,128)S(1)}, s32[512,8]{0,1:T(8,128)}, u32[]{:S(2)}) copy-start(s32[512,8]{0,1:T(8,128)} %param.16) | copy-start | bytes 49156
  8.4 17.2 %copy-start.10 = (bf16[512,256]{1,0:T(8,128)(2,1)S(1)}, bf16[512,256]{1,0:T(8,128)(2,1)}, u32[]{:S(2)}) copy-start(bf16[512,256]{1,0:T(8,128)(2,1)} %param.14) | copy-start | bytes 786436
  8.4 17.3 %copy-start.16 = (s32[512]{0:T(512)S(1)}, s32[512]{0:T(512)}, u32[]{:S(2)}) copy-start(s32[512]{0:T(512)} %param.17) | copy-start | bytes 6148
  13.4 25.5 %all-to-all-start = ((bf16[128,8,256]{2,1,0:T(8,128)(2,1)}), bf16[128,8,256]{2,1,0:T(8,128)(2,1)S(1)}, u32[]{:S(2)}, u32[]{:S(2)}) async-start(bf16[128,8,256]{2,1,0:T(8,128)(2,1)} %bitcast.14), calls=%async_computation | async-start | bytes 1048576 | tf_op jit(solution)/shard_map/all_to_all | solution.py:48
  26.3 27.2 %copy-start.12 = (s32[4096]{0:T(1024)}, s32[4096]{0:T(1024)S(1)}, u32[]{:S(2)}) copy-start(s32[4096]{0:T(1024)S(1)} %broadcast_clamp_fusion) | copy-start | bytes 49156
  53.5 3.0 copy-start.6
  124.0 22.1 %copy-start.5 = (bf16[8,512,256]{2,1,0:T(8,128)(2,1)}, bf16[8,512,256]{2,1,0:T(8,128)(2,1)S(1)}, u32[]{:S(2)}) copy-start(bf16[8,512,256]{2,1,0:T(8,128)(2,1)S(1)} %get-tuple-element.1141) | copy-start | bytes 6291460
  124.1 27.0 %copy-start.15 = (s32[128,8]{0,1:T(8,128)S(1)}, s32[128,8]{0,1:T(8,128)}, u32[]{:S(2)}) copy-start(s32[128,8]{0,1:T(8,128)} %param.18) | copy-start | bytes 12292
  146.2 24.3 %all-to-all-start.1 = ((f32[128,8,256]{2,1,0:T(8,128)}), f32[128,8,256]{2,1,0:T(8,128)}, u32[]{:S(2)}, u32[]{:S(2)}) async-start(f32[128,8,256]{2,1,0:T(8,128)} %bitcast.21), calls=%async_computation.1 | async-start | bytes 2097152 | tf_op jit(solution)/shard_map/all_to_all | solution.py:52
  151.0 26.5 %copy-start.7 = (bf16[2048,256]{1,0:T(8,128)(2,1)S(1)}, bf16[2048,256]{1,0:T(8,128)(2,1)}, u32[]{:S(2)}) copy-start(bf16[2048,256]{1,0:T(8,128)(2,1)} %param.23) | copy-start | bytes 3145732
  177.5 1.7 copy-start.3
  177.6 3.1 copy-start.9
  179.3 1.3 copy-start.4
  181.7 9.1 %copy-start.11 = (bf16[512,256]{1,0:T(8,128)(2,1)S(1)}, bf16[512,256]{1,0:T(8,128)(2,1)}, u32[]{:S(2)}) copy-start(bf16[512,256]{1,0:T(8,128)(2,1)} %param.22) | copy-start | bytes 786436
  186.7 18.1 %all-to-all-start.2 = ((bf16[128,8,256]{2,1,0:T(8,128)(2,1)}), bf16[128,8,256]{2,1,0:T(8,128)(2,1)S(1)}, u32[]{:S(2)}, u32[]{:S(2)}) async-start(bf16[128,8,256]{2,1,0:T(8,128)(2,1)} %bitcast.23), calls=%async_computation.2 | async-start | bytes 1048576 | tf_op jit(solution)/shard_map/all_to_all | solution.py:48
  190.7 276.4 %all-reduce.7.cloned.1.call-start = ((), (), s32[]{:S(2)}) async-start(), calls=%async_computation.4 | async-start | bytes 3670016 | tf_op jit(solution)/shard_map/psum | solution.py:111
  191.6 13.2 %copy-start.13 = (s32[4096]{0:T(1024)S(1)}, s32[4096]{0:T(1024)}, u32[]{:S(2)}) copy-start(s32[4096]{0:T(1024)} %copy-done.12) | copy-start | bytes 49156
  319.0 0.9 copy-start.2
  319.9 25.8 %copy-start.8 = (bf16[2048,256]{1,0:T(8,128)(2,1)S(1)}, bf16[2048,256]{1,0:T(8,128)(2,1)}, u32[]{:S(2)}) copy-start(bf16[2048,256]{1,0:T(8,128)(2,1)} %param.23) | copy-start | bytes 3145732
  341.9 129.6 %all-to-all-start.3 = ((f32[128,8,256]{2,1,0:T(8,128)}), f32[128,8,256]{2,1,0:T(8,128)S(1)}, u32[]{:S(2)}, u32[]{:S(2)}) async-start(f32[128,8,256]{2,1,0:T(8,128)} %bitcast.27), calls=%async_computation.3 | async-start | bytes 2097152 | tf_op jit(solution)/shard_map/all_to_all | solution.py:52
  468.8 11.7 %copy-start.1 = (bf16[2048,256]{1,0:T(8,128)(2,1)S(1)}, bf16[2048,256]{1,0:T(8,128)(2,1)}, u32[]{:S(2)}) copy-start(bf16[2048,256]{1,0:T(8,128)(2,1)} %param.15) | copy-start | bytes 3145732
Sparse Core Ops, SparseCore 0:
  320.0 147.0 all-reduce.6
where the time goes:
time: 490 us; the launch traced here: 487 us
  waiting for transfers between devices  161 us (33%)
  other arithmetic  147 us (30%)
  matrix products  81.7 us (17%)
  local copies, waits for them, and re-layouts  59.1 us (12%)
  starting transfers between devices  24.2 us (5%)
  between operations  14.4 us (3%)
    psum x1, waiting for transfers between devices, per_device(): lax.psum((d_input_w, d_state_w, wagg_grad), ('outer', 'sw'))  120 us
    dot_general x24, matrix products, hop_step(): jnp.dot(carried.astype(jnp.bfloat16), state_weight.astype(jnp.bfloat16),...  51.3 us
    dynamic_update_slice x40, other arithmetic, gru_path(): return lax.scan(hop_step, start_state, (hop_inputs, hop_valid))  49 us
    dot_general x24, matrix products, hop_step(): jnp.dot(link_rows, input_weight.astype(jnp.bfloat16), preferred_element_t...  23.3 us
    scatter-add x1, other arithmetic, per_device(): slot_sums = jnp.zeros((devices * capacity, width), jnp.float32).at[flat_s...  22.1 us
    scatter-add x1, other arithmetic, per_device(): input_sums = jnp.zeros((devices * capacity, width), jnp.float32).at[flat_...  22 us
    all_to_all x2, waiting for transfers between devices, to_paths(): lax.all_to_all(rows, ('outer', 'sw'), split_axis=0, concat_axis=0, tiled=...  21.4 us
    all_to_all x2, waiting for transfers between devices, to_owners(): lax.all_to_all(sums, ('outer', 'sw'), split_axis=0, concat_axis=0, tiled=...  19.1 us
  transfers between devices with their start and end apart: 5, of which 4 were waited for; matrix products, arithmetic and copies ran while one was open for 7% of the time, Pallas kernels for 0%

commit v1 on v0

v1 whole, which is shorter than its diff:
```python
import functools
import math

import jax
import jax.numpy as jnp
from jax import lax
from jax.experimental import pallas as pl
from jax.experimental.pallas import tpu as pltpu
from jax.sharding import PartitionSpec as P

F32 = jnp.float32
BF16 = jnp.bfloat16
AXES = ("outer", "sw")
VMEM_LIMIT = 56 * 1024 * 1024


def mm(a, b):
    return lax.dot_general(a, b, (((1,), (0,)), ((), ())), preferred_element_type=F32)


def mm_t(a, b):
    return lax.dot_general(a, b, (((1,), (1,)), ((), ())), preferred_element_type=F32)


def hot_rows(col, width):
    lanes = lax.broadcasted_iota(jnp.int32, (col.shape[0], width), 1)
    return jnp.where(col == lanes, 1.0, 0.0).astype(BF16)


def hot_cols(row, start, height):
    lines = lax.broadcasted_iota(jnp.int32, (height, row.shape[1]), 0) + start
    return jnp.where(row == lines, 1.0, 0.0).astype(BF16)


def call(kernel, outs, scratch, cost, *args):
    flops, moved = cost
    return pl.pallas_call(
        kernel,
        out_shape=outs,
        in_specs=[pl.BlockSpec(memory_space=pltpu.VMEM)] * len(args),
        out_specs=jax.tree.map(lambda _: pl.BlockSpec(memory_space=pltpu.VMEM), outs),
        scratch_shapes=scratch,
        compiler_params=pltpu.CompilerParams(vmem_limit_bytes=VMEM_LIMIT),
        cost_estimate=pl.CostEstimate(flops=flops, bytes_accessed=moved, transcendentals=0),
    )(*args)


def pick_kernel(rows_ref, link_ref, out_ref):
    links = link_ref.shape[0]
    tile = 256

    def body(i, carry):
        at = pl.ds(pl.multiple_of(i * tile, tile), tile)
        out_ref[at, :] = mm(hot_rows(rows_ref[at, :], links), link_ref[...]).astype(BF16)
        return carry

    lax.fori_loop(0, out_ref.shape[0] // tile, body, 0)


def halved(w_ref):
    width = w_ref.shape[0]
    lanes = lax.broadcasted_iota(jnp.int32, w_ref.shape, 1)
    w = w_ref[...].astype(F32)
    return jnp.where(lanes < 2 * width, 0.5 * w, w).astype(BF16)


def gates(a, b, width):
    r = 0.5 * jnp.tanh(a[:, :width] + b[:, :width]) + 0.5
    u = 0.5 * jnp.tanh(a[:, width : 2 * width] + b[:, width : 2 * width]) + 0.5
    bn = b[:, 2 * width :]
    n = jnp.tanh(a[:, 2 * width :] + r * bn)
    return r, u, n, bn


def forward_kernel(
    table_ref, col_ref, row_ref, start_ref, wi_ref, ws_ref,
    sums_ref, xs_ref, cs_ref, wi_s, ws_s, a_s, msg_s,
):
    hops, paths, width = xs_ref.shape
    slots = table_ref.shape[0]
    tile = 256
    wi_s[...] = halved(wi_ref)
    ws_s[...] = halved(ws_ref)

    for t in range(hops):
        for i in range(0, paths, tile):
            at = slice(i, i + tile)
            hot = hot_rows(col_ref[at, t : t + 1], slots)
            x = mm(hot, table_ref[...]).astype(BF16)
            xs_ref[t, at, :] = x
            a_s[t, at, :] = mm(x, wi_s[...])

    cs_ref[0] = start_ref[...].astype(F32)
    for t in range(hops):
        for i in range(0, paths, tile):
            at = slice(i, i + tile)
            c = cs_ref[t, at, :]
            b = mm(c.astype(BF16), ws_s[...])
            r, u, n, _ = gates(a_s[t, at, :], b, width)
            keep = col_ref[at, t : t + 1] >= 0
            c = jnp.where(keep, n + u * (c - n), c)
            if t + 1 < hops:
                cs_ref[t + 1, at, :] = c
            msg_s[t * paths + i : t * paths + i + tile, :] = c.astype(BF16)

    step = 256
    for i in range(0, slots, step):
        total = None
        for t in range(hops):
            hot = hot_cols(row_ref[t : t + 1, :], i, step)
            term = mm(hot, msg_s[t * paths : (t + 1) * paths, :])
            total = term if total is None else total + term
        sums_ref[i : i + step, :] = total.astype(BF16)


def factors_kernel(
    xs_ref, cs_ref, col_ref, wi_ref, ws_ref,
    fr_ref, fu_ref, fn_ref, fm_ref, fc_ref, xt_ref, ct_ref,
):
    t = pl.program_id(0)
    _, paths, width = xs_ref.shape
    wi = halved(wi_ref)
    ws = halved(ws_ref)
    tile = 256
    hop = lax.broadcasted_iota(jnp.int32, (1, col_ref.shape[1]), 1) == t
    for i in range(0, paths, tile):
        at = slice(i, i + tile)
        x = xs_ref[0, at, :]
        c = cs_ref[0, at, :]
        cb = c.astype(BF16)
        r, u, n, bn = gates(mm(x, wi), mm(cb, ws), width)
        slot = jnp.max(jnp.where(hop, col_ref[at, :], -1), axis=1, keepdims=True)
        keep = slot >= 0
        fn = jnp.where(keep, (1.0 - u) * (1.0 - n * n), 0.0)
        fm = fn * r
        fn_ref[0, at, :] = fn
        fm_ref[0, at, :] = fm
        fr_ref[0, at, :] = fm * bn * (1.0 - r)
        fu_ref[0, at, :] = jnp.where(keep, (c - n) * u * (1.0 - u), 0.0)
        fc_ref[0, at, :] = jnp.where(keep, u, 1.0)
        xt_ref[:, at] = x.astype(F32).T.astype(BF16)
        ct_ref[:, at] = c.T.astype(BF16)


def link_kernel(
    arrived_ref, row_ref, col_ref, w_ref, cot_ref, back_ref, agg_ref, pre_ref, d_s,
):
    links = cot_ref.shape[0]
    tile = 256

    def body(i, carry):
        start = pl.multiple_of(i * tile, tile)
        at = pl.ds(start, tile)
        agg = mm(hot_cols(row_ref[...], start, tile), arrived_ref[...]).astype(BF16)
        act = jnp.tanh(mm(agg, w_ref[...]))
        pre = cot_ref[at, :].astype(F32) * (1.0 - act * act)
        high = pre.astype(BF16)
        low = (pre - high.astype(F32)).astype(BF16)
        agg_ref[at, :] = agg
        pre_ref[at, :] = pre
        d_s[at, :] = (mm_t(high, w_ref[...]) + mm_t(low, w_ref[...])).astype(BF16)
        return carry

    lax.fori_loop(0, links // tile, body, 0)

    def pick(i, carry):
        at = pl.ds(pl.multiple_of(i * tile, tile), tile)
        back_ref[at, :] = mm(hot_rows(col_ref[at, :], links), d_s[...]).astype(BF16)
        return carry

    lax.fori_loop(0, back_ref.shape[0] // tile, pick, 0)


def link_grad_kernel(agg_ref, pre_ref, out_ref):
    links = agg_ref.shape[0]
    tile = 256
    out_ref[...] = jnp.zeros_like(out_ref)

    def body(i, carry):
        at = pl.ds(pl.multiple_of(i * tile, tile), tile)
        agg_t = agg_ref[at, :].astype(F32).T.astype(BF16)
        pre = pre_ref[at, :]
        high = pre.astype(BF16)
        low = (pre - high.astype(F32)).astype(BF16)
        out_ref[...] += mm(agg_t, high) + mm(agg_t, low)
        return carry

    lax.fori_loop(0, links // tile, body, 0)


def backward_kernel(
    table_ref, col_ref, row_ref, cot_ref, wi_ref, ws_ref,
    fr_ref, fu_ref, fn_ref, fm_ref, fc_ref, xt_ref, ct_ref,
    grad_ref, sums_ref, gi_ref, gs_ref, da_s, db_s, dx_s,
):
    step_id = pl.program_id(0)
    hops = pl.num_programs(0)
    t = hops - 1 - step_id
    paths, width = grad_ref.shape
    slots = table_ref.shape[0]
    tile = 256

    @pl.when(step_id == 0)
    def _():
        grad_ref[...] = cot_ref[...].astype(F32)
        gi_ref[...] = jnp.zeros_like(gi_ref)
        gs_ref[...] = jnp.zeros_like(gs_ref)

    hop = lax.broadcasted_iota(jnp.int32, (1, col_ref.shape[1]), 1) == t
    for i in range(0, paths, tile):
        at = slice(i, i + tile)
        slot = jnp.max(jnp.where(hop, col_ref[at, :], -1), axis=1, keepdims=True)
        d = grad_ref[at, :] + mm(hot_rows(slot, slots), table_ref[...])
        dr = (d * fr_ref[0, at, :]).astype(BF16)
        du = (d * fu_ref[0, at, :]).astype(BF16)
        dn = (d * fn_ref[0, at, :]).astype(BF16)
        dm = (d * fm_ref[0, at, :]).astype(BF16)
        da_s[at, :width] = dr
        da_s[at, width : 2 * width] = du
        da_s[at, 2 * width :] = dn
        db_s[at, :width] = dr
        db_s[at, width : 2 * width] = du
        db_s[at, 2 * width :] = dm
        back = mm_t(db_s[at, :], ws_ref[...]).astype(BF16).astype(F32)
        grad_ref[at, :] = d * fc_ref[0, at, :] + back
        dx = mm_t(da_s[at, :], wi_ref[...]).astype(BF16)
        dx_s[pl.ds(pl.multiple_of(t * paths + i, tile), tile), :] = dx
    gi_ref[...] += mm(xt_ref[...], da_s[...])
    gs_ref[...] += mm(ct_ref[...], db_s[...])

    @pl.when(step_id == hops - 1)
    def _():
        step = 256
        for i in range(0, slots, step):
            total = None
            for h in range(row_ref.shape[0]):
                hot = hot_cols(row_ref[h : h + 1, :], i, step)
                term = mm(hot, dx_s[h * paths : (h + 1) * paths, :])
                total = term if total is None else total + term
            sums_ref[i : i + step, :] = total.astype(BF16)


def share_kernel(parts_ref, out_ref):
    out_ref[...] = jnp.sum(parts_ref[...].astype(F32), axis=0)


def link_out_kernel(returned_ref, row_ref, cot_ref, out_ref):
    tile = 256

    def body(i, carry):
        start = pl.multiple_of(i * tile, tile)
        at = pl.ds(start, tile)
        total = mm(hot_cols(row_ref[...], start, tile), returned_ref[...])
        out_ref[at, :] = cot_ref[at, :].astype(F32) + total
        return carry

    lax.fori_loop(0, out_ref.shape[0] // tile, body, 0)


def exchange(rows):
    return lax.all_to_all(rows, AXES, split_axis=0, concat_axis=0, tiled=True)


def per_device(
    path_state, link_state, hop_slot, hop_count, send_rows,
    w_input, w_state, w_agg, path_cot, link_cot,
):
    devices = lax.axis_size("outer") * lax.axis_size("sw")
    paths, width = path_state.shape
    hops = hop_slot.shape[1]
    links = link_state.shape[0]
    capacity = send_rows.shape[1]
    slots = devices * capacity
    gate_cols = w_input.shape[1]
    shape = jax.ShapeDtypeStruct

    send_row = send_rows.reshape(1, slots)
    send_col = send_rows.reshape(slots, 1)
    rows = call(
        pick_kernel, shape((slots, width), BF16), [],
        (2 * slots * links * width, 2 * links * width), send_col, link_state,
    )
    table = exchange(rows.reshape(devices, capacity, width)).reshape(slots, width)

    valid = jnp.arange(hops, dtype=jnp.int32)[None, :] < hop_count[:, None]
    slot_col = jnp.where(valid, hop_slot, -1)
    slot_row = jnp.where(valid.T, hop_slot.T, -1)
    sums, xs, cs = call(
        forward_kernel,
        (
            shape((slots, width), BF16),
            shape((hops, paths, width), BF16),
            shape((hops, paths, width), F32),
        ),
        [
            pltpu.VMEM((width, gate_cols), BF16),
            pltpu.VMEM((width, gate_cols), BF16),
            pltpu.VMEM((hops, paths, gate_cols), F32),
            pltpu.VMEM((hops * paths, width), BF16),
        ],
        (4 * hops * paths * slots * width, 8 * hops * paths * width),
        table, slot_col, slot_row, path_state, w_input, w_state,
    )
    arrived = exchange(sums.reshape(devices, capacity, width)).reshape(slots, width)

    whole = lambda *dims: pl.BlockSpec(dims, lambda i: (0,) * len(dims))
    factor = shape((hops, paths, width), F32)
    turned = shape((width, hops * paths), BF16)
    hop_block = pl.BlockSpec((1, paths, width), lambda i: (i, 0, 0))
    turned_block = pl.BlockSpec((width, paths), lambda i: (0, i))
    factors = pl.pallas_call(
        factors_kernel,
        grid=(hops,),
        out_shape=(factor,) * 5 + (turned,) * 2,
        in_specs=[
            hop_block, hop_block, whole(paths, hops),
            whole(width, gate_cols), whole(width, gate_cols),
        ],
        out_specs=(hop_block,) * 5 + (turned_block,) * 2,
        compiler_params=pltpu.CompilerParams(vmem_limit_bytes=VMEM_LIMIT),
        cost_estimate=pl.CostEstimate(
            flops=4 * hops * paths * width * gate_cols,
            bytes_accessed=32 * hops * paths * width, transcendentals=0,
        ),
    )(xs, cs, slot_col, w_input, w_state)

    back, agg, pre = call(
        link_kernel,
        (shape((slots, width), BF16), shape((links, width), BF16), shape((links, width), F32)),
        [pltpu.VMEM((links, width), BF16)],
        (4 * slots * links * width, 8 * links * width),
        arrived, send_row, send_col, w_agg, link_cot,
    )
    back_table = exchange(back.reshape(devices, capacity, width)).reshape(slots, width)
    agg_grad = call(
        link_grad_kernel, shape((width, width), F32), [],
        (4 * links * width * width, 6 * links * width), agg, pre,
    )

    last = hops - 1
    hop_back = pl.BlockSpec((1, paths, width), lambda i: (last - i, 0, 0))
    turned_back = pl.BlockSpec((width, paths), lambda i: (0, last - i))
    grad_path, input_sums, input_grad, state_grad = pl.pallas_call(
        backward_kernel,
        grid=(hops,),
        out_shape=(
            shape((paths, width), F32),
            shape((slots, width), BF16),
            shape((width, gate_cols), F32),
            shape((width, gate_cols), F32),
        ),
        in_specs=[
            whole(slots, width), whole(paths, hops), whole(hops, paths), whole(paths, width),
            whole(width, gate_cols), whole(width, gate_cols),
        ] + [hop_back] * 5 + [turned_back] * 2,
        out_specs=(
            whole(paths, width), whole(slots, width),
            whole(width, gate_cols), whole(width, gate_cols),
        ),
        scratch_shapes=[
            pltpu.VMEM((paths, gate_cols), BF16),
            pltpu.VMEM((paths, gate_cols), BF16),
            pltpu.VMEM((hops * paths, width), BF16),
        ],
        compiler_params=pltpu.CompilerParams(vmem_limit_bytes=VMEM_LIMIT),
        cost_estimate=pl.CostEstimate(
            flops=12 * hops * paths * width * gate_cols,
            bytes_accessed=32 * hops * paths * width, transcendentals=0,
        ),
    )(back_table, slot_col, slot_row, path_cot, w_input, w_state, *factors)

    grads = jnp.concatenate(
        [
            input_grad.reshape(-1, width), state_grad.reshape(-1, width), agg_grad,
        ],
        axis=0,
    ).astype(BF16)
    share = grads.shape[0] // devices
    both = jnp.concatenate(
        [input_sums.reshape(devices, capacity, width), grads.reshape(devices, share, width)],
        axis=1,
    )
    got = exchange(both)
    returned = got[:, :capacity].reshape(slots, width)
    mine = call(
        share_kernel, shape((share, width), F32), [],
        (devices * share * width, 2 * devices * share * width), got[:, capacity:],
    )
    spread = jnp.broadcast_to(mine.astype(BF16)[None], (devices, share, width))
    total = exchange(spread).reshape(devices * share, width).astype(F32)
    grad_link = call(
        link_out_kernel, shape((links, width), F32), [],
        (2 * slots * links * width, 6 * links * width), returned, send_row, link_cot,
    )
    span = width * gate_cols // width
    path_scale = 1.0 / math.sqrt(paths * devices)
    link_scale = 1.0 / math.sqrt(links * devices)
    return (
        grad_path,
        grad_link,
        total[:span].reshape(width, gate_cols) * path_scale,
        total[span : 2 * span].reshape(width, gate_cols) * path_scale,
        total[2 * span :] * link_scale,
    )


def solution(mesh):
    split = P(AXES, None)
    return jax.shard_map(
        per_device,
        mesh=mesh,
        in_specs=(split, split, split, P(AXES), split, P(), P(), P(), split, split),
        out_specs=(split, split, P(), P(), P()),
        check_vma=False,
    )
```

time: 490 us -> 193 us (0.39)
  other arithmetic: 147 us -> 5.45 us
  waiting for transfers between devices: 161 us -> 39.6 us
  matrix products: 81.7 us -> 0 us
  Pallas kernels: 0 us -> 76.7 us
  local copies, waits for them, and re-layouts: 59.1 us -> 11.6 us
  blocking collectives: 0 us -> 34.9 us
  between operations: 14.4 us -> 0.8 us
    psum x1 -> x0, waiting for transfers between devices: 120 us -> none  [per_device(): lax.psum((d_input_w, d_state_w, wagg_grad), ('outer', 'sw'))]
    dot_general x51 -> x0, matrix products: 81.7 us -> none  [the longest x24 51.3 us: hop_step(): jnp.dot(carried.astype(jnp.bfloat16), state_weight.astype(jnp.bfloat16),...]
    pallas_call x0 -> x8, Pallas kernels: none -> 76.7 us  [the longest x6 42.5 us: call(): pl.pallas_call(kernel, out_shape=outs, in_specs=[pl.BlockSpec(memory_spac...]
    scatter-add x4 -> x0, other arithmetic: 60.1 us -> none  [the longest x1 22.1 us: per_device(): slot_sums = jnp.zeros((devices * capacity, width), jnp.float32).at[flat_s...]
    dynamic_update_slice x40 -> x0, other arithmetic: 49 us -> none  [gru_path(): return lax.scan(hop_step, start_state, (hop_inputs, hop_valid))]
    gather x4 -> x0, local copies, waits for them, and re-layouts: 41.6 us -> none  [the longest x1 17 us: per_device(): d_messages = back_table[hop_slots]]
    all_to_all x0 -> x1, blocking collectives: none -> 34.9 us  [exchange(): return lax.all_to_all(rows, AXES, split_axis=0, concat_axis=0, tiled=True)]
    mul x18 -> x2, other arithmetic: 33.5 us -> 0.83 us  [the longest x1 0.72 us: per_device(): total[2 * span:] * link_scale]
  transfers between devices with their start and end apart: 5 -> 4, of which waited for: 4 -> 3; matrix products, arithmetic and copies ran while one was open for 7% -> 2% of each run, Pallas kernels for 0% -> 12%
where the time goes in v1:
time: 193 us; the launch traced here: 192 us
  Pallas kernels  76.7 us (40%)
  waiting for transfers between devices  39.6 us (21%)
  blocking collectives  34.9 us (18%)
  starting transfers between devices  22.9 us (12%)
  local copies, waits for them, and re-layouts  11.6 us (6%)
  other arithmetic  5.45 us (3%)
    pallas_call x6, Pallas kernels, call(): pl.pallas_call(kernel, out_shape=outs, in_specs=[pl.BlockSpec(memory_spac...  42.5 us
    all_to_all x4, waiting for transfers between devices, exchange(): return lax.all_to_all(rows, AXES, split_axis=0, concat_axis=0, tiled=True)  39.6 us
    all_to_all x1, blocking collectives, exchange(): return lax.all_to_all(rows, AXES, split_axis=0, concat_axis=0, tiled=True)  34.9 us
    all_to_all x4, starting transfers between devices, exchange(): return lax.all_to_all(rows, AXES, split_axis=0, concat_axis=0, tiled=True)  22.9 us
    pallas_call x1, Pallas kernels, per_device(): pl.pallas_call(backward_kernel, grid=(hops,), out_shape=(shape((paths, wi...  20.7 us
    pallas_call x1, Pallas kernels, per_device(): pl.pallas_call(factors_kernel, grid=(hops,), out_shape=(factor,) * 5 + (t...  13.5 us
    unnamed x16, local copies, waits for them, and re-layouts  3.99 us
  transfers between devices with their start and end apart: 4, of which 3 were waited for; matrix products, arithmetic and copies ran while one was open for 2% of the time, Pallas kernels for 12%

profile of v1, /device:TPU:1, one launch (start us, length us, event | category | flops | bytes accessed | tf_op | source)
XLA Modules:
  0.0 192.0 jit_solution(6373220139523226115)
XLA Ops:
  0.6 0.8 copy.18
  1.4 1.0 reshape.75.rows_ref.col_ref
  2.4 4.1 %shard_map.137 = bf16[1024,256]{1,0:T(8,128)(2,1)} custom-call(s32[1024,1]{1,0:T(8,128)} %reshape.75.rows_ref.col_ref, bf16[2048,256]{1,0:T(8,128)(2,1)} %link_ref.1), custom_call_target="tpu_custom_call" | custom-call | flops 1073741824 | bytes 1048576 | tf_op jit(solution)/shard_map/pallas_call | solution.py:37
  6.5 11.5 %all-to-all-start = ((bf16[128,8,256]{2,1,0:T(8,128)(2,1)}), bf16[128,8,256]{2,1,0:T(8,128)(2,1)S(1)}, u32[]{:S(2)}, u32[]{:S(2)}) async-start(bf16[128,8,256]{2,1,0:T(8,128)(2,1)} %bitcast.16), calls=%async_computation | async-start | bytes 1048576 | tf_op jit(solution)/shard_map/all_to_all | solution.py:261
  18.8 0.8 fusion.col_ref
  19.6 12.4 %all-to-all-done = bf16[128,8,256]{2,1,0:T(8,128)(2,1)S(1)} async-done(((bf16[128,8,256]{2,1,0:T(8,128)(2,1)}), bf16[128,8,256]{2,1,0:T(8,128)(2,1)S(1)}, u32[]{:S(2)}, u32[]{:S(2)}) %all-to-all-start) | async-done | bytes 524320 | tf_op jit(solution)/shard_map/all_to_all | solution.py:261
  32.0 0.8 copy-done.2
  32.8 15.7 %shard_map.138 = (bf16[1024,256]{1,0:T(8,128)(2,1)}, bf16[8,512,256]{2,1,0:T(8,128)(2,1)}, f32[8,512,256]{2,1,0:T(8,128)}) custom-call(bf16[1024,256]{1,0:T(8,128)(2,1)} %bitcast.13, s32[512,8]{1,0:T(8,128)} %fusion.col_ref, s32[8,512]{1,0:T(8,128)} %bitcast_select_fusion.row_ref, bf16[512,256]{1,0:T(8,128)(2,1)} %start_ref.1, bf16[256,768]{1,0:T(8,128)(2,1)} %wi_ref.5, ...), custom_call_target="tpu_custom_call" | custom-call | flops 4294967296 | bytes 8388608 | tf_op jit(solution)/shard_map/pallas_call | solution.py:37
  48.5 3.8 %all-to-all-start.1 = ((bf16[128,8,256]{2,1,0:T(8,128)(2,1)}), bf16[128,8,256]{2,1,0:T(8,128)(2,1)S(1)}, u32[]{:S(2)}, u32[]{:S(2)}) async-start(bf16[128,8,256]{2,1,0:T(8,128)(2,1)} %bitcast.15), calls=%async_computation.1 | async-start | bytes 1048576 | tf_op jit(solution)/shard_map/all_to_all | solution.py:261
  53.1 13.4 %all-to-all-done.1 = bf16[128,8,256]{2,1,0:T(8,128)(2,1)S(1)} async-done(((bf16[128,8,256]{2,1,0:T(8,128)(2,1)}), bf16[128,8,256]{2,1,0:T(8,128)(2,1)S(1)}, u32[]{:S(2)}, u32[]{:S(2)}) %all-to-all-start.1) | async-done | bytes 524320 | tf_op jit(solution)/shard_map/all_to_all | solution.py:261
  66.5 0.8 copy-done.3
  67.3 10.6 %shard_map.139 = (bf16[1024,256]{1,0:T(8,128)(2,1)}, bf16[2048,256]{1,0:T(8,128)(2,1)}, f32[2048,256]{1,0:T(8,128)}) custom-call(bf16[1024,256]{1,0:T(8,128)(2,1)} %bitcast.14, s32[1,1024]{1,0:T(1,128)} %reshape.67.row_ref, s32[1024,1]{1,0:T(8,128)} %reshape.75.rows_ref.col_ref, bf16[256,256]{1,0:T(8,128)(2,1)} %w_ref.1, bf16[2048,256]{1,0:T(8,128)(2,1)} %cot_ref.5), custom_call_target="tpu_custom_call" | custom-call | flops 2147483648 | bytes 4194304 | tf_op jit(solution)/shard_map/pallas_call | solution.py:37
  77.8 3.8 %all-to-all-start.2 = ((bf16[128,8,256]{2,1,0:T(8,128)(2,1)}), bf16[128,8,256]{2,1,0:T(8,128)(2,1)S(1)}, u32[]{:S(2)}, u32[]{:S(2)}) async-start(bf16[128,8,256]{2,1,0:T(8,128)(2,1)} %bitcast.12), calls=%async_computation.2 | async-start | bytes 1048576 | tf_op jit(solution)/shard_map/all_to_all | solution.py:261
  81.6 13.5 %shard_map.140 = (f32[8,512,256]{2,1,0:T(8,128)}, f32[8,512,256]{2,1,0:T(8,128)}, f32[8,512,256]{2,1,0:T(8,128)}, f32[8,512,256]{2,1,0:T(8,128)}, f32[8,512,256]...) custom-call(bf16[8,512,256]{2,1,0:T(8,128)(2,1)} %get-tuple-element.24.xs_ref, ...), custom_call_target="tpu_custom_call" | custom-call | flops 3221225472 | bytes 33554432 | tf_op jit(solution)/shard_map/pallas_call | solution.py:311
  95.1 4.9 %shard_map.142 = f32[256,256]{1,0:T(8,128)} custom-call(bf16[2048,256]{1,0:T(8,128)(2,1)} %get-tuple-element.37.agg_ref, f32[2048,256]{1,0:T(8,128)} %get-tuple-element.38.pre_ref), custom_call_target="tpu_custom_call" | custom-call | flops 536870912 | bytes 3145728 | tf_op jit(solution)/shard_map/pallas_call | solution.py:37
  100.0 1.0 convert.14
  101.0 0.8 copy-done.1
  101.8 20.7 %shard_map.141 = (f32[512,256]{1,0:T(8,128)}, bf16[1024,256]{1,0:T(8,128)(2,1)}, f32[256,768]{1,0:T(8,128)}, f32[256,768]{1,0:T(8,128)}) custom-call(bf16[1024,256]{1,0:T(8,128)(2,1)} %bitcast.11, s32[512,8]{1,0:T(8,128)} %fusion.col_ref, s32[8,512]{1,0:T(8,128)} %bitcast_select_fusion.row_ref, bf16[512,256]{1,0:T(8,128)(2,1)} %cot_ref.4, ...), custom_call_target="tpu_custom_call" | custom-call | flops 9663676416 | bytes 33554432 | tf_op jit(solution)/shard_map/pallas_call | solution.py:343
  122.5 1.2 convert.12
  124.6 0.7 copy-done.4
  125.4 34.9 %all_to_all.25 = bf16[128,22,256]{2,1,0:T(8,128)(2,1)S(1)} all-to-all(bf16[128,22,256]{2,1,0:T(8,128)(2,1)S(1)} %pad_maximum_fusion), channel_id=1, replica_groups=mesh['outer'=32,'sw'=4] {'outer','sw'}, dimensions={0} | all-to-all | bytes 2883584 | tf_op jit(solution)/shard_map/all_to_all | solution.py:261
  160.3 1.1 slice.21.parts_ref
  161.4 2.1 %shard_map.144 = f32[14,256]{1,0:T(8,128)} custom-call(bf16[128,14,256]{2,1,0:T(8,128)(2,1)} %slice.21.parts_ref), custom_call_target="tpu_custom_call" | custom-call | flops 458752 | bytes 917504 | tf_op jit(solution)/shard_map/pallas_call | solution.py:37
  163.4 0.7 convert_element_type.15
  164.2 1.0 broadcast_in_dim.18
  165.2 3.8 %all-to-all-start.4 = ((bf16[128,14,256]{2,1,0:T(8,128)(2,1)}), bf16[128,14,256]{2,1,0:T(8,128)(2,1)S(1)}, u32[]{:S(2)}, u32[]{:S(2)}) async-start(bf16[128,14,256]{2,1,0:T(8,128)(2,1)} %broadcast_in_dim.18), calls=%async_computation.4 | async-start | bytes 2097152 | tf_op jit(solution)/shard_map/all_to_all | solution.py:261
  169.0 0.8 slice_bitcast_fusion.returned_ref
  169.9 5.2 %shard_map.143 = f32[2048,256]{1,0:T(8,128)} custom-call(bf16[1024,256]{1,0:T(8,128)(2,1)} %slice_bitcast_fusion.returned_ref, s32[1,1024]{1,0:T(1,128)} %reshape.67.row_ref, bf16[2048,256]{1,0:T(8,128)(2,1)} %cot_ref.5), custom_call_target="tpu_custom_call" | custom-call | flops 1073741824 | bytes 3145728 | tf_op jit(solution)/shard_map/pallas_call | solution.py:37
  175.0 13.7 %all-to-all-done.4 = bf16[128,14,256]{2,1,0:T(8,128)(2,1)S(1)} async-done(((bf16[128,14,256]{2,1,0:T(8,128)(2,1)}), bf16[128,14,256]{2,1,0:T(8,128)(2,1)S(1)}, u32[]{:S(2)}, u32[]{:S(2)}) %all-to-all-start.4) | async-done | bytes 917536 | tf_op jit(solution)/shard_map/all_to_all | solution.py:261
  189.0 0.7 slice_multiply_fusion.2
  189.8 1.1 mul.21
  190.9 1.1 mul.19
  (22 shorter events, 2.6 us)
Async XLA Ops:
  2.4 15.6 %copy-start.5 = (s32[512,8]{0,1:T(8,128)S(1)}, s32[512,8]{0,1:T(8,128)}, u32[]{:S(2)}) copy-start(s32[512,8]{0,1:T(8,128)} %param.12) | copy-start | bytes 49156
  2.4 15.8 %copy-start.6 = (s32[512]{0:T(512)S(1)}, s32[512]{0:T(512)}, u32[]{:S(2)}) copy-start(s32[512]{0:T(512)} %param.13) | copy-start | bytes 6148
  6.5 25.5 %all-to-all-start = ((bf16[128,8,256]{2,1,0:T(8,128)(2,1)}), bf16[128,8,256]{2,1,0:T(8,128)(2,1)S(1)}, u32[]{:S(2)}, u32[]{:S(2)}) async-start(bf16[128,8,256]{2,1,0:T(8,128)(2,1)} %bitcast.16), calls=%async_computation | async-start | bytes 1048576 | tf_op jit(solution)/shard_map/all_to_all | solution.py:261
  32.0 0.8 copy-start.2
  48.5 17.9 %all-to-all-start.1 = ((bf16[128,8,256]{2,1,0:T(8,128)(2,1)}), bf16[128,8,256]{2,1,0:T(8,128)(2,1)S(1)}, u32[]{:S(2)}, u32[]{:S(2)}) async-start(bf16[128,8,256]{2,1,0:T(8,128)(2,1)} %bitcast.15), calls=%async_computation.1 | async-start | bytes 1048576 | tf_op jit(solution)/shard_map/all_to_all | solution.py:261
  66.5 0.8 copy-start.3
  77.8 23.1 %all-to-all-start.2 = ((bf16[128,8,256]{2,1,0:T(8,128)(2,1)}), bf16[128,8,256]{2,1,0:T(8,128)(2,1)S(1)}, u32[]{:S(2)}, u32[]{:S(2)}) async-start(bf16[128,8,256]{2,1,0:T(8,128)(2,1)} %bitcast.12), calls=%async_computation.2 | async-start | bytes 1048576 | tf_op jit(solution)/shard_map/all_to_all | solution.py:261
  101.0 0.8 copy-start.1
  122.5 1.5 copy-start
  124.2 1.0 copy-start.4
  165.2 23.6 %all-to-all-start.4 = ((bf16[128,14,256]{2,1,0:T(8,128)(2,1)}), bf16[128,14,256]{2,1,0:T(8,128)(2,1)S(1)}, u32[]{:S(2)}, u32[]{:S(2)}) async-start(bf16[128,14,256]{2,1,0:T(8,128)(2,1)} %broadcast_in_dim.18), calls=%async_computation.4 | async-start | bytes 2097152 | tf_op jit(solution)/shard_map/all_to_all | solution.py:261

commit v2 on v1

v2 whole, which is shorter than its diff:
```python
import functools
import math

import jax
import jax.numpy as jnp
from jax import lax
from jax.experimental import pallas as pl
from jax.experimental.pallas import tpu as pltpu
from jax.sharding import PartitionSpec as P

F32 = jnp.float32
BF16 = jnp.bfloat16
AXES = ("outer", "sw")
VMEM_LIMIT = 56 * 1024 * 1024


def mm(a, b):
    return lax.dot_general(a, b, (((1,), (0,)), ((), ())), preferred_element_type=F32)


def mm_t(a, b):
    return lax.dot_general(a, b, (((1,), (1,)), ((), ())), preferred_element_type=F32)


def hot_rows(col, width):
    lanes = lax.broadcasted_iota(jnp.int32, (col.shape[0], width), 1)
    return jnp.where(col == lanes, 1.0, 0.0).astype(BF16)


def hot_cols(row, start, height):
    lines = lax.broadcasted_iota(jnp.int32, (height, row.shape[1]), 0) + start
    return jnp.where(row == lines, 1.0, 0.0).astype(BF16)


VMEM = pl.BlockSpec(memory_space=pltpu.VMEM)
ANY = pl.BlockSpec(memory_space=pl.ANY)


def call(kernel, outs, scratch, cost, *args, in_specs=None, out_specs=None):
    flops, moved = cost
    return pl.pallas_call(
        kernel,
        out_shape=outs,
        in_specs=in_specs or [VMEM] * len(args),
        out_specs=out_specs or jax.tree.map(lambda _: VMEM, outs),
        scratch_shapes=scratch,
        compiler_params=pltpu.CompilerParams(vmem_limit_bytes=VMEM_LIMIT),
        cost_estimate=pl.CostEstimate(flops=flops, bytes_accessed=moved, transcendentals=0),
    )(*args)


def pick_kernel(rows_ref, link_ref, out_ref):
    links = link_ref.shape[0]
    tile = 256

    def body(i, carry):
        at = pl.ds(pl.multiple_of(i * tile, tile), tile)
        out_ref[at, :] = mm(hot_rows(rows_ref[at, :], links), link_ref[...]).astype(BF16)
        return carry

    lax.fori_loop(0, out_ref.shape[0] // tile, body, 0)


def halved(w_ref):
    width = w_ref.shape[0]
    lanes = lax.broadcasted_iota(jnp.int32, w_ref.shape, 1)
    w = w_ref[...].astype(F32)
    return jnp.where(lanes < 2 * width, 0.5 * w, w).astype(BF16)


def gates(a, b, width):
    r = 0.5 * jnp.tanh(a[:, :width] + b[:, :width]) + 0.5
    u = 0.5 * jnp.tanh(a[:, width : 2 * width] + b[:, width : 2 * width]) + 0.5
    bn = b[:, 2 * width :]
    n = jnp.tanh(a[:, 2 * width :] + r * bn)
    return r, u, n, bn


def forward_kernel(
    table_ref, col_ref, row_ref, start_ref, wi_ref, ws_ref,
    sums_ref, xs_ref, cs_ref, wi_s, ws_s, a_s, x_s, c_s, msg_s, sem,
):
    hops, paths, width = x_s.shape
    slots = table_ref.shape[0]
    tile = 256
    wi_s[...] = halved(wi_ref)
    ws_s[...] = halved(ws_ref)

    def saves(t):
        return (
            pltpu.make_async_copy(x_s.at[t], xs_ref.at[t], sem.at[0, t]),
            pltpu.make_async_copy(c_s.at[t], cs_ref.at[t], sem.at[1, t]),
        )

    def enter(t, i):
        at = slice(i, i + tile)
        x = mm(hot_rows(col_ref[at, t : t + 1], slots), table_ref[...]).astype(BF16)
        x_s[t, at, :] = x
        a_s[t, at, :] = mm(x, wi_s[...])

    c_s[0] = start_ref[...].astype(F32)
    for i in range(0, paths, tile):
        enter(0, i)
    for t in range(hops):
        for i in range(0, paths, tile):
            at = slice(i, i + tile)
            if t + 1 < hops:
                enter(t + 1, i)
            c = c_s[t, at, :]
            b = mm(c.astype(BF16), ws_s[...])
            r, u, n, _ = gates(a_s[t, at, :], b, width)
            keep = col_ref[at, t : t + 1] >= 0
            c = jnp.where(keep, n + u * (c - n), c)
            if t + 1 < hops:
                c_s[t + 1, at, :] = c
            msg_s[t * paths + i : t * paths + i + tile, :] = c.astype(BF16)
    for t in range(hops):
        for copy in saves(t):
            copy.start()

    step = 256
    for i in range(0, slots, step):
        total = None
        for t in range(hops):
            hot = hot_cols(row_ref[t : t + 1, :], i, step)
            term = mm(hot, msg_s[t * paths : (t + 1) * paths, :])
            total = term if total is None else total + term
        sums_ref[i : i + step, :] = total.astype(BF16)
    for t in range(hops):
        for copy in saves(t):
            copy.wait()


def factors_kernel(
    xs_ref, cs_ref, col_ref, wi_ref, ws_ref,
    fr_ref, fu_ref, fn_ref, fm_ref, fc_ref, xt_ref, ct_ref,
):
    t = pl.program_id(0)
    _, paths, width = xs_ref.shape
    wi = halved(wi_ref)
    ws = halved(ws_ref)
    tile = 256
    hop = lax.broadcasted_iota(jnp.int32, (1, col_ref.shape[1]), 1) == t
    for i in range(0, paths, tile):
        at = slice(i, i + tile)
        x = xs_ref[0, at, :]
        c = cs_ref[0, at, :]
        cb = c.astype(BF16)
        r, u, n, bn = gates(mm(x, wi), mm(cb, ws), width)
        slot = jnp.max(jnp.where(hop, col_ref[at, :], -1), axis=1, keepdims=True)
        keep = slot >= 0
        fn = jnp.where(keep, (1.0 - u) * (1.0 - n * n), 0.0)
        fm = fn * r
        fn_ref[0, at, :] = fn
        fm_ref[0, at, :] = fm
        fr_ref[0, at, :] = fm * bn * (1.0 - r)
        fu_ref[0, at, :] = jnp.where(keep, (c - n) * u * (1.0 - u), 0.0)
        fc_ref[0, at, :] = jnp.where(keep, u, 1.0)
        xt_ref[:, at] = x.astype(F32).T.astype(BF16)
        ct_ref[:, at] = c.T.astype(BF16)


def link_tile(arrived_ref, row_ref, w_ref, cot_ref, start, tile):
    at = pl.ds(start, tile)
    agg = mm(hot_cols(row_ref[...], start, tile), arrived_ref[...]).astype(BF16)
    act = jnp.tanh(mm(agg, w_ref[...]))
    pre = cot_ref[at, :].astype(F32) * (1.0 - act * act)
    high = pre.astype(BF16)
    low = (pre - high.astype(F32)).astype(BF16)
    return agg, high, low


def link_kernel(arrived_ref, row_ref, col_ref, w_ref, cot_ref, back_ref, d_s):
    links = cot_ref.shape[0]
    tile = 256
    for i in range(0, links, tile):
        _, high, low = link_tile(arrived_ref, row_ref, w_ref, cot_ref, i, tile)
        d_s[i : i + tile, :] = (mm_t(high, w_ref[...]) + mm_t(low, w_ref[...])).astype(BF16)
    for i in range(0, back_ref.shape[0], tile):
        at = slice(i, i + tile)
        back_ref[at, :] = mm(hot_rows(col_ref[at, :], links), d_s[...]).astype(BF16)


def link_grad_kernel(arrived_ref, row_ref, w_ref, cot_ref, out_ref):
    tile = 256
    out_ref[...] = jnp.zeros_like(out_ref)

    def body(i, carry):
        start = pl.multiple_of(i * tile, tile)
        agg, high, low = link_tile(arrived_ref, row_ref, w_ref, cot_ref, start, tile)
        agg_t = agg.astype(F32).T.astype(BF16)
        out_ref[...] += mm(agg_t, high) + mm(agg_t, low)
        return carry

    lax.fori_loop(0, cot_ref.shape[0] // tile, body, 0)


def backward_kernel(
    table_ref, col_ref, cot_ref, wi_ref, ws_ref, agg_grad_ref,
    fr_ref, fu_ref, fn_ref, fm_ref, fc_ref, xt_ref, ct_ref,
    grad_ref, da_ref, grads_ref,
    f_s, xt_s, ct_s, m_s, da_s, db_s, gi_s, gs_s, sem, da_sem,
):
    _, hops, paths, width = f_s.shape
    slots = table_ref.shape[0]
    tile = 256

    def loads(t):
        at = pl.ds(t * paths, paths)
        pairs = [(ref.at[t], f_s.at[k, t]) for k, ref in enumerate(
            (fr_ref, fu_ref, fn_ref, fm_ref, fc_ref))]
        pairs += [(xt_ref.at[:, at], xt_s.at[:, at]), (ct_ref.at[:, at], ct_s.at[:, at])]
        return [
            pltpu.make_async_copy(source, target, sem.at[k, t])
            for k, (source, target) in enumerate(pairs)
        ]

    def save(t):
        return pltpu.make_async_copy(da_s.at[t], da_ref.at[t], da_sem.at[t])

    order = list(range(hops))[::-1]
    for t in order:
        for copy in loads(t):
            copy.start()

    grad_ref[...] = cot_ref[...].astype(F32)

    def fetch(t, i):
        at = slice(i, i + tile)
        m_s[t, at, :] = mm(hot_rows(col_ref[at, t : t + 1], slots), table_ref[...])

    def weigh(t):
        at = slice(t * paths, (t + 1) * paths)
        gi = mm(xt_s[:, at], da_s[t])
        gs = mm(ct_s[:, at], db_s[t])
        if t == hops - 1:
            gi_s[...] = gi
            gs_s[...] = gs
        else:
            gi_s[...] += gi
            gs_s[...] += gs

    for i in range(0, paths, tile):
        fetch(hops - 1, i)
    for t in order:
        for copy in loads(t):
            copy.wait()
        for i in range(0, paths, tile):
            at = slice(i, i + tile)
            if t > 0:
                fetch(t - 1, i)
            d = grad_ref[at, :] + m_s[t, at, :]
            dr = (d * f_s[0, t, at, :]).astype(BF16)
            du = (d * f_s[1, t, at, :]).astype(BF16)
            da_s[t, at, :width] = dr
            da_s[t, at, width : 2 * width] = du
            da_s[t, at, 2 * width :] = (d * f_s[2, t, at, :]).astype(BF16)
            db_s[t, at, :width] = dr
            db_s[t, at, width : 2 * width] = du
            db_s[t, at, 2 * width :] = (d * f_s[3, t, at, :]).astype(BF16)
            back = mm_t(db_s[t, at, :], ws_ref[...]).astype(BF16).astype(F32)
            grad_ref[at, :] = d * f_s[4, t, at, :] + back
        if t < hops - 1:
            weigh(t + 1)
    for t in order:
        save(t).start()
    weigh(0)
    for k in range(3):
        part = slice(k * width, (k + 1) * width)
        grads_ref[part, :] = gi_s[:, part].astype(BF16)
        grads_ref[3 * width + k * width : 3 * width + (k + 1) * width, :] = gs_s[:, part].astype(BF16)
    grads_ref[6 * width : 7 * width, :] = agg_grad_ref[...].astype(BF16)
    grads_ref[7 * width :, :] = jnp.zeros_like(agg_grad_ref).astype(BF16)
    for t in order:
        save(t).wait()


def input_kernel(da_ref, row_ref, wi_ref, sums_ref, dx_s):
    hops, paths, _ = da_ref.shape
    slots = sums_ref.shape[0]
    for t in range(hops):
        dx_s[t * paths : (t + 1) * paths, :] = mm_t(da_ref[t], wi_ref[...]).astype(BF16)
    step = 256
    for i in range(0, slots, step):
        total = None
        for t in range(hops):
            hot = hot_cols(row_ref[t : t + 1, :], i, step)
            term = mm(hot, dx_s[t * paths : (t + 1) * paths, :])
            total = term if total is None else total + term
        sums_ref[i : i + step, :] = total.astype(BF16)


def share_kernel(parts_ref, out_ref):
    total = jnp.sum(parts_ref[...].astype(F32), axis=0).astype(BF16)
    out_ref[...] = jnp.broadcast_to(total[None], out_ref.shape)


def link_out_kernel(returned_ref, row_ref, cot_ref, out_ref):
    tile = 256
    for i in range(0, out_ref.shape[0], tile):
        at = slice(i, i + tile)
        total = mm(hot_cols(row_ref[...], i, tile), returned_ref[...])
        out_ref[at, :] = cot_ref[at, :].astype(F32) + total


def final_kernel(path_scale, link_scale, total_ref, gi_ref, gs_ref, ga_ref):
    width = ga_ref.shape[0]
    for k in range(3):
        part = slice(k * width, (k + 1) * width)
        other = slice((k + 3) * width, (k + 4) * width)
        gi_ref[:, part] = total_ref[part, :].astype(F32) * path_scale
        gs_ref[:, part] = total_ref[other, :].astype(F32) * path_scale
    ga_ref[...] = total_ref[6 * width : 7 * width, :].astype(F32) * link_scale


def exchange(rows):
    return lax.all_to_all(rows, AXES, split_axis=0, concat_axis=0, tiled=True)


def per_device(
    path_state, link_state, hop_slot, hop_count, send_rows,
    w_input, w_state, w_agg, path_cot, link_cot,
):
    devices = lax.axis_size("outer") * lax.axis_size("sw")
    paths, width = path_state.shape
    hops = hop_slot.shape[1]
    links = link_state.shape[0]
    capacity = send_rows.shape[1]
    slots = devices * capacity
    gate_cols = w_input.shape[1]
    shape = jax.ShapeDtypeStruct

    send_row = send_rows.reshape(1, slots)
    send_col = send_rows.reshape(slots, 1)
    rows = call(
        pick_kernel, shape((slots, width), BF16), [],
        (2 * slots * links * width, 2 * links * width), send_col, link_state,
    )
    table = exchange(rows.reshape(devices, capacity, width)).reshape(slots, width)

    valid = jnp.arange(hops, dtype=jnp.int32)[None, :] < hop_count[:, None]
    slot_col = jnp.where(valid, hop_slot, -1)
    slot_row = jnp.where(valid.T, hop_slot.T, -1)
    sums, xs, cs = call(
        forward_kernel,
        (
            shape((slots, width), BF16),
            shape((hops, paths, width), BF16),
            shape((hops, paths, width), F32),
        ),
        [
            pltpu.VMEM((width, gate_cols), BF16),
            pltpu.VMEM((width, gate_cols), BF16),
            pltpu.VMEM((hops, paths, gate_cols), F32),
            pltpu.VMEM((hops, paths, width), BF16),
            pltpu.VMEM((hops, paths, width), F32),
            pltpu.VMEM((hops * paths, width), BF16),
            pltpu.SemaphoreType.DMA((2, hops)),
        ],
        (4 * hops * paths * slots * width, 8 * hops * paths * width),
        table, slot_col, slot_row, path_state, w_input, w_state,
        out_specs=(VMEM, ANY, ANY),
    )
    arrived = exchange(sums.reshape(devices, capacity, width)).reshape(slots, width)

    whole = lambda *dims: pl.BlockSpec(dims, lambda i: (0,) * len(dims))
    factor = shape((hops, paths, width), F32)
    turned = shape((width, hops * paths), BF16)
    hop_block = pl.BlockSpec((1, paths, width), lambda i: (i, 0, 0))
    turned_block = pl.BlockSpec((width, paths), lambda i: (0, i))
    factors = pl.pallas_call(
        factors_kernel,
        grid=(hops,),
        out_shape=(factor,) * 5 + (turned,) * 2,
        in_specs=[
            hop_block, hop_block, whole(paths, hops),
            whole(width, gate_cols), whole(width, gate_cols),
        ],
        out_specs=(hop_block,) * 5 + (turned_block,) * 2,
        compiler_params=pltpu.CompilerParams(vmem_limit_bytes=VMEM_LIMIT),
        cost_estimate=pl.CostEstimate(
            flops=4 * hops * paths * width * gate_cols,
            bytes_accessed=32 * hops * paths * width, transcendentals=0,
        ),
    )(xs, cs, slot_col, w_input, w_state)
    arrived, factors = lax.optimization_barrier((arrived, factors))

    back = call(
        link_kernel, shape((slots, width), BF16), [pltpu.VMEM((links, width), BF16)],
        (4 * slots * links * width, 8 * links * width),
        arrived, send_row, send_col, w_agg, link_cot,
    )
    back_table = exchange(back.reshape(devices, capacity, width)).reshape(slots, width)
    agg_grad = call(
        link_grad_kernel, shape((width, width), F32), [],
        (4 * links * width * width, 6 * links * width), arrived, send_row, w_agg, link_cot,
    )
    back_table, agg_grad = lax.optimization_barrier((back_table, agg_grad))

    grad_path, da, grads = call(
        backward_kernel,
        (
            shape((paths, width), F32),
            shape((hops, paths, gate_cols), BF16),
            shape((8 * width, width), BF16),
        ),
        [
            pltpu.VMEM((5, hops, paths, width), F32),
            pltpu.VMEM((width, hops * paths), BF16),
            pltpu.VMEM((width, hops * paths), BF16),
            pltpu.VMEM((hops, paths, width), F32),
            pltpu.VMEM((hops, paths, gate_cols), BF16),
            pltpu.VMEM((hops, paths, gate_cols), BF16),
            pltpu.VMEM((width, gate_cols), F32),
            pltpu.VMEM((width, gate_cols), F32),
            pltpu.SemaphoreType.DMA((7, hops)),
            pltpu.SemaphoreType.DMA((hops,)),
        ],
        (10 * hops * paths * width * gate_cols, 32 * hops * paths * width),
        back_table, slot_col, path_cot, w_input, w_state, agg_grad, *factors,
        in_specs=[VMEM] * 6 + [ANY] * 7,
        out_specs=(VMEM, ANY, VMEM),
    )
    share = grads.shape[0] // devices
    parts = exchange(grads.reshape(devices, share, width))
    input_sums = call(
        input_kernel, shape((slots, width), BF16), [pltpu.VMEM((hops * paths, width), BF16)],
        (2 * hops * paths * (gate_cols + slots) * width, 2 * hops * paths * gate_cols),
        da, slot_row, w_input,
    )
    returned = exchange(input_sums.reshape(devices, capacity, width)).reshape(slots, width)
    mine = call(
        share_kernel, shape((devices, share, width), BF16), [],
        (devices * share * width, 4 * devices * share * width), parts,
    )
    total = exchange(mine).reshape(devices * share, width)
    grad_link = call(
        link_out_kernel, shape((links, width), F32), [],
        (2 * slots * links * width, 6 * links * width), returned, send_row, link_cot,
    )
    path_scale = 1.0 / math.sqrt(paths * devices)
    link_scale = 1.0 / math.sqrt(links * devices)
    wide = shape((width, gate_cols), F32)
    input_grad, state_grad, agg_total = call(
        functools.partial(final_kernel, path_scale, link_scale),
        (wide, wide, shape((width, width), F32)), [],
        (8 * width * width, 40 * width * width), total,
    )
    return grad_path, grad_link, input_grad, state_grad, agg_total


def solution(mesh):
    split = P(AXES, None)
    return jax.shard_map(
        per_device,
        mesh=mesh,
        in_specs=(split, split, split, P(AXES), split, P(), P(), P(), split, split),
        out_specs=(split, split, P(), P(), P()),
        check_vma=False,
    )
```

time: 193 us -> 184 us (0.953)
  blocking collectives: 34.9 us -> 0 us
  waiting for transfers between devices: 39.6 us -> 57.4 us
  starting transfers between devices: 22.9 us -> 37.2 us
  local copies, waits for them, and re-layouts: 11.6 us -> 5.98 us
  other arithmetic: 5.45 us -> 1.44 us
  Pallas kernels: 76.7 us -> 80 us
    all_to_all x1 -> x0, blocking collectives: 34.9 us -> none  [exchange(): return lax.all_to_all(rows, AXES, split_axis=0, concat_axis=0, tiled=True)]
    all_to_all x4 -> x6, waiting for transfers between devices: 39.6 us -> 57.4 us  [exchange(): return lax.all_to_all(rows, AXES, split_axis=0, concat_axis=0, tiled=True)]
    all_to_all x4 -> x6, starting transfers between devices: 22.9 us -> 37.2 us  [exchange(): return lax.all_to_all(rows, AXES, split_axis=0, concat_axis=0, tiled=True)]
    pallas_call x7 -> x9, Pallas kernels: 63.2 us -> 66.4 us  [call(): pl.pallas_call(kernel, out_shape=outs, in_specs=in_specs or [VMEM] * len(...]
    another operation x3 -> x0, other arithmetic: 2.25 us -> none
    mul x2 -> x0, local copies, waits for them, and re-layouts: 2.2 us -> none  [the longest x1 1.1 us: per_device(): total[span:2 * span].reshape(width, gate_cols) * path_scale]
    unnamed x16 -> x18, local copies, waits for them, and re-layouts: 3.99 us -> 4.3 us
  transfers between devices with their start and end apart: 4 -> 6, of which waited for: 3 -> 5; matrix products, arithmetic and copies ran while one was open for 2% -> 1% of each run, Pallas kernels for 12% -> 20%
where the time goes in v2:
time: 184 us; the launch traced here: 183 us
  Pallas kernels  80 us (43%)
  waiting for transfers between devices  57.4 us (31%)
  starting transfers between devices  37.2 us (20%)
  local copies, waits for them, and re-layouts  5.98 us (3%)
    pallas_call x9, Pallas kernels, call(): pl.pallas_call(kernel, out_shape=outs, in_specs=in_specs or [VMEM] * len(...  66.4 us
    all_to_all x6, waiting for transfers between devices, exchange(): return lax.all_to_all(rows, AXES, split_axis=0, concat_axis=0, tiled=True)  57.4 us
    all_to_all x6, starting transfers between devices, exchange(): return lax.all_to_all(rows, AXES, split_axis=0, concat_axis=0, tiled=True)  37.2 us
    pallas_call x1, Pallas kernels, per_device(): pl.pallas_call(factors_kernel, grid=(hops,), out_shape=(factor,) * 5 + (t...  13.6 us
    unnamed x18, local copies, waits for them, and re-layouts  4.3 us
  transfers between devices with their start and end apart: 6, of which 5 were waited for; matrix products, arithmetic and copies ran while one was open for 1% of the time, Pallas kernels for 20%

profile of v2, /device:TPU:1, one launch (start us, length us, event | category | flops | bytes accessed | tf_op | source)
XLA Modules:
  0.0 182.8 jit_solution(15031178890666873537)
XLA Ops:
  0.7 0.8 copy.18
  1.5 1.0 reshape.59.rows_ref.col_ref
  2.4 4.1 %shard_map.137 = bf16[1024,256]{1,0:T(8,128)(2,1)} custom-call(s32[1024,1]{1,0:T(8,128)} %reshape.59.rows_ref.col_ref, bf16[2048,256]{1,0:T(8,128)(2,1)} %link_ref.1), custom_call_target="tpu_custom_call" | custom-call | flops 1073741824 | bytes 1048576 | tf_op jit(solution)/shard_map/pallas_call | solution.py:41
  6.5 11.5 %all-to-all-start = ((bf16[128,8,256]{2,1,0:T(8,128)(2,1)}), bf16[128,8,256]{2,1,0:T(8,128)(2,1)S(1)}, u32[]{:S(2)}, u32[]{:S(2)}) async-start(bf16[128,8,256]{2,1,0:T(8,128)(2,1)} %bitcast.21), calls=%async_computation | async-start | bytes 1048576 | tf_op jit(solution)/shard_map/all_to_all | solution.py:317
  18.1 0.1 copy.20
  18.2 0.6 bitcast_select_fusion.row_ref
  18.8 0.8 fusion.col_ref
  19.6 12.4 %all-to-all-done = bf16[128,8,256]{2,1,0:T(8,128)(2,1)S(1)} async-done(((bf16[128,8,256]{2,1,0:T(8,128)(2,1)}), bf16[128,8,256]{2,1,0:T(8,128)(2,1)S(1)}, u32[]{:S(2)}, u32[]{:S(2)}) %all-to-all-start) | async-done | bytes 524320 | tf_op jit(solution)/shard_map/all_to_all | solution.py:317
  32.0 0.8 copy-done.5
  32.8 13.5 %shard_map.138 = (bf16[1024,256]{1,0:T(8,128)(2,1)}, bf16[8,512,256]{2,1,0:T(8,128)(2,1)}, f32[8,512,256]{2,1,0:T(8,128)}) custom-call(bf16[1024,256]{1,0:T(8,128)(2,1)} %bitcast.19, s32[512,8]{1,0:T(8,128)} %fusion.col_ref, s32[8,512]{1,0:T(8,128)} %bitcast_select_fusion.row_ref, bf16[512,256]{1,0:T(8,128)(2,1)} %start_ref.1, bf16[256,768]{1,0:T(8,128)(2,1)} %wi_ref.7, ...), custom_call_target="tpu_custom_call" | custom-call | flops 4294967296 | bytes 8388608 | tf_op jit(solution)/shard_map/pallas_call | solution.py:41
  46.3 3.8 %all-to-all-start.1 = ((bf16[128,8,256]{2,1,0:T(8,128)(2,1)}), bf16[128,8,256]{2,1,0:T(8,128)(2,1)S(1)}, u32[]{:S(2)}, u32[]{:S(2)}) async-start(bf16[128,8,256]{2,1,0:T(8,128)(2,1)} %bitcast.17), calls=%async_computation.1 | async-start | bytes 1048576 | tf_op jit(solution)/shard_map/all_to_all | solution.py:317
  50.2 0.7 reshape.52.row_ref
  50.9 13.6 %shard_map.139 = (f32[8,512,256]{2,1,0:T(8,128)}, f32[8,512,256]{2,1,0:T(8,128)}, f32[8,512,256]{2,1,0:T(8,128)}, f32[8,512,256]{2,1,0:T(8,128)}, f32[8,512,256]...) custom-call(bf16[8,512,256]{2,1,0:T(8,128)(2,1)} %get-tuple-element.32.xs_ref, ...), custom_call_target="tpu_custom_call" | custom-call | flops 3221225472 | bytes 33554432 | tf_op jit(solution)/shard_map/pallas_call | solution.py:371
  64.5 0.0 copy-start.2
  64.5 0.8 copy-done.2
  65.3 8.4 %shard_map.140 = bf16[1024,256]{1,0:T(8,128)(2,1)} custom-call(bf16[1024,256]{1,0:T(8,128)(2,1)} %bitcast.14, s32[1,1024]{1,0:T(1,128)} %reshape.52.row_ref, s32[1024,1]{1,0:T(8,128)} %reshape.59.rows_ref.col_ref, bf16[256,256]{1,0:T(8,128)(2,1)} %w_ref.3, bf16[2048,256]{1,0:T(8,128)(2,1)} %cot_ref.7), custom_call_target="tpu_custom_call" | custom-call | flops 2147483648 | bytes 4194304 | tf_op jit(solution)/shard_map/pallas_call | solution.py:41
  73.6 9.9 %all-to-all-start.2 = ((bf16[128,8,256]{2,1,0:T(8,128)(2,1)}), bf16[128,8,256]{2,1,0:T(8,128)(2,1)S(1)}, u32[]{:S(2)}, u32[]{:S(2)}) async-start(bf16[128,8,256]{2,1,0:T(8,128)(2,1)} %bitcast.22), calls=%async_computation.2 | async-start | bytes 1048576 | tf_op jit(solution)/shard_map/all_to_all | solution.py:317
  83.6 8.3 %shard_map.141.agg_grad_ref = f32[256,256]{1,0:T(8,128)} custom-call(bf16[1024,256]{1,0:T(8,128)(2,1)} %bitcast.15, s32[1,1024]{1,0:T(1,128)} %reshape.52.row_ref, bf16[256,256]{1,0:T(8,128)(2,1)} %w_ref.3, bf16[2048,256]{1,0:T(8,128)(2,1)} %cot_ref.7), custom_call_target="tpu_custom_call" | custom-call | flops 536870912 | bytes 3145728 | tf_op jit(solution)/shard_map/pallas_call | solution.py:41
  91.9 5.6 %all-to-all-done.2 = bf16[128,8,256]{2,1,0:T(8,128)(2,1)S(1)} async-done(((bf16[128,8,256]{2,1,0:T(8,128)(2,1)}), bf16[128,8,256]{2,1,0:T(8,128)(2,1)S(1)}, u32[]{:S(2)}, u32[]{:S(2)}) %all-to-all-start.2) | async-done | bytes 524320 | tf_op jit(solution)/shard_map/all_to_all | solution.py:317
  97.5 0.8 copy-done.3
  98.3 15.5 %shard_map.142 = (f32[512,256]{1,0:T(8,128)}, bf16[8,512,768]{2,1,0:T(8,128)(2,1)}, bf16[2048,256]{1,0:T(8,128)(2,1)}) custom-call(bf16[1024,256]{1,0:T(8,128)(2,1)} %bitcast.16, s32[512,8]{1,0:T(8,128)} %fusion.col_ref, bf16[512,256]{1,0:T(8,128)(2,1)} %cot_ref.6, bf16[256,768]{1,0:T(8,128)(2,1)} %wi_ref.7, bf16[256,768]{1,0:T(8,128)(2,1)} %ws_ref.5, ...), custom_call_target="tpu_custom_call" | custom-call | flops 8053063680 | bytes 33554432 | tf_op jit(solution)/shard_map/pallas_call | solution.py:41
  113.9 4.1 %all-to-all-start.4 = ((bf16[128,16,256]{2,1,0:T(8,128)(2,1)}), bf16[128,16,256]{2,1,0:T(8,128)(2,1)S(1)}, u32[]{:S(2)}, u32[]{:S(2)}) async-start(bf16[128,16,256]{2,1,0:T(8,128)(2,1)} %bitcast.13), calls=%async_computation.4 | async-start | bytes 2097152 | tf_op jit(solution)/shard_map/all_to_all | solution.py:317
  118.0 7.6 %shard_map.143 = bf16[1024,256]{1,0:T(8,128)(2,1)} custom-call(bf16[8,512,768]{2,1,0:T(8,128)(2,1)} %get-tuple-element.52.da_ref, s32[8,512]{1,0:T(8,128)} %bitcast_select_fusion.row_ref, bf16[256,768]{1,0:T(8,128)(2,1)} %wi_ref.7), custom_call_target="tpu_custom_call" | custom-call | flops 3758096384 | bytes 6291456 | tf_op jit(solution)/shard_map/pallas_call | solution.py:41
  125.6 12.0 %all-to-all-done.4.parts_ref = bf16[128,16,256]{2,1,0:T(8,128)(2,1)S(1)} async-done(((bf16[128,16,256]{2,1,0:T(8,128)(2,1)}), bf16[128,16,256]{2,1,0:T(8,128)(2,1)S(1)}, u32[]{:S(2)}, u32[]{:S(2)}) %all-to-all-start.4) | async-done | bytes 1048608 | tf_op jit(solution)/shard_map/all_to_all | solution.py:317
  137.6 4.0 %all-to-all-start.3 = ((bf16[128,8,256]{2,1,0:T(8,128)(2,1)}), bf16[128,8,256]{2,1,0:T(8,128)(2,1)S(1)}, u32[]{:S(2)}, u32[]{:S(2)}) async-start(bf16[128,8,256]{2,1,0:T(8,128)(2,1)} %bitcast.20), calls=%async_computation.3 | async-start | bytes 1048576 | tf_op jit(solution)/shard_map/all_to_all | solution.py:317
  141.7 2.4 %shard_map.145 = bf16[128,16,256]{2,1,0:T(8,128)(2,1)} custom-call(bf16[128,16,256]{2,1,0:T(8,128)(2,1)} %copy-done), custom_call_target="tpu_custom_call" | custom-call | flops 524288 | bytes 2097152 | tf_op jit(solution)/shard_map/pallas_call | solution.py:41
  144.1 11.7 %all-to-all-done.3 = bf16[128,8,256]{2,1,0:T(8,128)(2,1)S(1)} async-done(((bf16[128,8,256]{2,1,0:T(8,128)(2,1)}), bf16[128,8,256]{2,1,0:T(8,128)(2,1)S(1)}, u32[]{:S(2)}, u32[]{:S(2)}) %all-to-all-start.3) | async-done | bytes 524320 | tf_op jit(solution)/shard_map/all_to_all | solution.py:317
  155.8 3.8 %all-to-all-start.5 = ((bf16[128,16,256]{2,1,0:T(8,128)(2,1)}), bf16[128,16,256]{2,1,0:T(8,128)(2,1)S(1)}, u32[]{:S(2)}, u32[]{:S(2)}) async-start(bf16[128,16,256]{2,1,0:T(8,128)(2,1)} %shard_map.145), calls=%async_computation.5 | async-start | bytes 2097152 | tf_op jit(solution)/shard_map/all_to_all | solution.py:317
  159.6 4.0 %shard_map.144 = f32[2048,256]{1,0:T(8,128)} custom-call(bf16[1024,256]{1,0:T(8,128)(2,1)} %bitcast.18, s32[1,1024]{1,0:T(1,128)} %reshape.52.row_ref, bf16[2048,256]{1,0:T(8,128)(2,1)} %cot_ref.7), custom_call_target="tpu_custom_call" | custom-call | flops 1073741824 | bytes 3145728 | tf_op jit(solution)/shard_map/pallas_call | solution.py:41
  163.6 15.8 %all-to-all-done.5 = bf16[128,16,256]{2,1,0:T(8,128)(2,1)S(1)} async-done(((bf16[128,16,256]{2,1,0:T(8,128)(2,1)}), bf16[128,16,256]{2,1,0:T(8,128)(2,1)S(1)}, u32[]{:S(2)}, u32[]{:S(2)}) %all-to-all-start.5) | async-done | bytes 1048608 | tf_op jit(solution)/shard_map/all_to_all | solution.py:317
  179.3 1.0 copy-done.1
  180.3 2.5 %shard_map.146 = (f32[256,768]{1,0:T(8,128)}, f32[256,768]{1,0:T(8,128)}, f32[256,256]{1,0:T(8,128)}) custom-call(bf16[2048,256]{1,0:T(8,128)(2,1)} %bitcast.12), custom_call_target="tpu_custom_call" | custom-call | flops 524288 | bytes 2621440 | tf_op jit(solution)/shard_map/pallas_call | solution.py:41
  (12 shorter events, 0.0 us)
Async XLA Ops:
  0.6 17.4 %copy-start.6 = (s32[512,8]{0,1:T(8,128)S(1)}, s32[512,8]{0,1:T(8,128)}, u32[]{:S(2)}) copy-start(s32[512,8]{0,1:T(8,128)} %param.12) | copy-start | bytes 49156
  0.6 17.5 %copy-start.7 = (s32[512]{0:T(512)S(1)}, s32[512]{0:T(512)}, u32[]{:S(2)}) copy-start(s32[512]{0:T(512)} %param.13) | copy-start | bytes 6148
  6.5 25.5 %all-to-all-start = ((bf16[128,8,256]{2,1,0:T(8,128)(2,1)}), bf16[128,8,256]{2,1,0:T(8,128)(2,1)S(1)}, u32[]{:S(2)}, u32[]{:S(2)}) async-start(bf16[128,8,256]{2,1,0:T(8,128)(2,1)} %bitcast.21), calls=%async_computation | async-start | bytes 1048576 | tf_op jit(solution)/shard_map/all_to_all | solution.py:317
  32.0 0.8 copy-start.5
  46.3 18.2 %all-to-all-start.1 = ((bf16[128,8,256]{2,1,0:T(8,128)(2,1)}), bf16[128,8,256]{2,1,0:T(8,128)(2,1)S(1)}, u32[]{:S(2)}, u32[]{:S(2)}) async-start(bf16[128,8,256]{2,1,0:T(8,128)(2,1)} %bitcast.17), calls=%async_computation.1 | async-start | bytes 1048576 | tf_op jit(solution)/shard_map/all_to_all | solution.py:317
  64.5 0.8 copy-start.2
  73.6 23.9 %all-to-all-start.2 = ((bf16[128,8,256]{2,1,0:T(8,128)(2,1)}), bf16[128,8,256]{2,1,0:T(8,128)(2,1)S(1)}, u32[]{:S(2)}, u32[]{:S(2)}) async-start(bf16[128,8,256]{2,1,0:T(8,128)(2,1)} %bitcast.22), calls=%async_computation.2 | async-start | bytes 1048576 | tf_op jit(solution)/shard_map/all_to_all | solution.py:317
  97.5 0.8 copy-start.3
  113.9 23.7 %all-to-all-start.4 = ((bf16[128,16,256]{2,1,0:T(8,128)(2,1)}), bf16[128,16,256]{2,1,0:T(8,128)(2,1)S(1)}, u32[]{:S(2)}, u32[]{:S(2)}) async-start(bf16[128,16,256]{2,1,0:T(8,128)(2,1)} %bitcast.13), calls=%async_computation.4 | async-start | bytes 2097152 | tf_op jit(solution)/shard_map/all_to_all | solution.py:317
  137.6 4.0 %copy-start = (bf16[128,16,256]{2,1,0:T(8,128)(2,1)}, bf16[128,16,256]{2,1,0:T(8,128)(2,1)S(1)}, u32[]{:S(2)}) copy-start(bf16[128,16,256]{2,1,0:T(8,128)(2,1)S(1)} %all-to-all-done.4.parts_ref) | copy-start | bytes 3145732
  137.6 18.2 %all-to-all-start.3 = ((bf16[128,8,256]{2,1,0:T(8,128)(2,1)}), bf16[128,8,256]{2,1,0:T(8,128)(2,1)S(1)}, u32[]{:S(2)}, u32[]{:S(2)}) async-start(bf16[128,8,256]{2,1,0:T(8,128)(2,1)} %bitcast.20), calls=%async_computation.3 | async-start | bytes 1048576 | tf_op jit(solution)/shard_map/all_to_all | solution.py:317
  155.8 3.8 %copy-start.4 = (bf16[128,8,256]{2,1,0:T(8,128)(2,1)}, bf16[128,8,256]{2,1,0:T(8,128)(2,1)S(1)}, u32[]{:S(2)}) copy-start(bf16[128,8,256]{2,1,0:T(8,128)(2,1)S(1)} %all-to-all-done.3) | copy-start | bytes 1572868
  155.8 23.6 %all-to-all-start.5 = ((bf16[128,16,256]{2,1,0:T(8,128)(2,1)}), bf16[128,16,256]{2,1,0:T(8,128)(2,1)S(1)}, u32[]{:S(2)}, u32[]{:S(2)}) async-start(bf16[128,16,256]{2,1,0:T(8,128)(2,1)} %shard_map.145), calls=%async_computation.5 | async-start | bytes 2097152 | tf_op jit(solution)/shard_map/all_to_all | solution.py:317
  179.3 1.0 copy-start.1

commit v3 on v2

v3 whole, which is shorter than its diff:
```python
import functools
import math

import jax
import jax.numpy as jnp
from jax import lax
from jax.experimental import pallas as pl
from jax.experimental.pallas import tpu as pltpu
from jax.sharding import PartitionSpec as P

F32 = jnp.float32
BF16 = jnp.bfloat16
AXES = ("outer", "sw")
MIB = 1024 * 1024
VMEM = pl.BlockSpec(memory_space=pltpu.VMEM)
ANY = pl.BlockSpec(memory_space=pl.ANY)


def mm(a, b):
    return lax.dot_general(a, b, (((1,), (0,)), ((), ())), preferred_element_type=F32)


def mm_t(a, b):
    return lax.dot_general(a, b, (((1,), (1,)), ((), ())), preferred_element_type=F32)


def t_mm(a, b):
    return lax.dot_general(a, b, (((0,), (0,)), ((), ())), preferred_element_type=F32)


def hot_cols(row, start, height):
    lines = lax.broadcasted_iota(jnp.int32, (height, row.shape[1]), 0) + start
    return jnp.where(row == lines, 1.0, 0.0).astype(BF16)


def call(kernel, outs, scratch, cost, *args, in_specs=None, out_specs=None):
    flops, moved, room = cost
    return pl.pallas_call(
        kernel,
        out_shape=outs,
        in_specs=in_specs or [VMEM] * len(args),
        out_specs=out_specs or jax.tree.map(lambda _: VMEM, outs),
        scratch_shapes=scratch,
        compiler_params=pltpu.CompilerParams(vmem_limit_bytes=room * MIB),
        cost_estimate=pl.CostEstimate(flops=flops, bytes_accessed=moved, transcendentals=0),
    )(*args)


def pick_kernel(turned_ref, link_ref, out_ref, row_ref):
    capacity, devices = turned_ref.shape
    slots = capacity * devices
    links = link_ref.shape[0]
    listed = turned_ref[...]
    high = (listed >> 8).astype(F32).astype(BF16)
    low = (listed & 255).astype(F32).astype(BF16)
    owner = lax.broadcasted_iota(jnp.int32, (devices, slots), 0)
    place = lax.broadcasted_iota(jnp.int32, (devices, slots), 1)
    spread = jnp.where(place // capacity == owner, 1.0, 0.0).astype(BF16)
    wide = mm(high, spread) * 256.0 + mm(low, spread)
    line = lax.broadcasted_iota(jnp.int32, (capacity, slots), 0)
    at = lax.broadcasted_iota(jnp.int32, (capacity, slots), 1)
    row = jnp.sum(jnp.where(at % capacity == line, wide, 0.0), axis=0, keepdims=True)
    row_ref[...] = row.astype(jnp.int32)
    step = 512
    total = None
    for i in range(0, links, step):
        term = t_mm(hot_cols(row_ref[...], i, step), link_ref[i : i + step, :])
        total = term if total is None else total + term
    out_ref[...] = total.astype(BF16)


def pick_again_kernel(row_ref, link_ref, out_ref):
    step = 512
    total = None
    for i in range(0, link_ref.shape[0], step):
        term = t_mm(hot_cols(row_ref[...], i, step), link_ref[i : i + step, :])
        total = term if total is None else total + term
    out_ref[...] = total.astype(BF16)


def halved(w_ref):
    width = w_ref.shape[0]
    lanes = lax.broadcasted_iota(jnp.int32, w_ref.shape, 1)
    w = w_ref[...].astype(F32)
    return jnp.where(lanes < 2 * width, 0.5 * w, w).astype(BF16)


def gates(a, b, width):
    r = 0.5 * jnp.tanh(a[:, :width] + b[:, :width]) + 0.5
    u = 0.5 * jnp.tanh(a[:, width : 2 * width] + b[:, width : 2 * width]) + 0.5
    bn = b[:, 2 * width :]
    n = jnp.tanh(a[:, 2 * width :] + r * bn)
    return r, u, n, bn


def forward_kernel(
    table_ref, count_ref, row_ref, start_ref, wi_ref, ws_ref,
    sums_ref, xs_ref, cs_ref, table_s, wi_s, ws_s, a_s, x_s, c_s, msg_s, sem, table_sem,
):
    hops, paths, width = x_s.shape
    slots = table_ref.shape[0]
    tile = 256
    arrival = pltpu.make_async_copy(table_ref, table_s, table_sem)
    arrival.start()
    wi_s[...] = halved(wi_ref)
    ws_s[...] = halved(ws_ref)
    c_s[0] = start_ref[...].astype(F32)
    arrival.wait()

    def saves(t):
        return (
            pltpu.make_async_copy(x_s.at[t], xs_ref.at[t], sem.at[0, t]),
            pltpu.make_async_copy(c_s.at[t], cs_ref.at[t], sem.at[1, t]),
        )

    def enter(t, i):
        at = slice(i, i + tile)
        hot = hot_cols(row_ref[t : t + 1, at], 0, slots)
        x = t_mm(hot, table_s[...]).astype(BF16)
        x_s[t, at, :] = x
        a_s[t, at, :] = mm(x, wi_s[...])

    for i in range(0, paths, tile):
        enter(0, i)
    for t in range(hops):
        for i in range(0, paths, tile):
            at = slice(i, i + tile)
            if t + 1 < hops:
                enter(t + 1, i)
            c = c_s[t, at, :]
            b = mm(c.astype(BF16), ws_s[...])
            r, u, n, _ = gates(a_s[t, at, :], b, width)
            c = jnp.where(count_ref[at, :] > t, n + u * (c - n), c)
            if t + 1 < hops:
                c_s[t + 1, at, :] = c
            msg_s[t * paths + i : t * paths + i + tile, :] = c.astype(BF16)
    for t in range(hops):
        for copy in saves(t):
            copy.start()

    add_up(row_ref, msg_s, sums_ref)
    for t in range(hops):
        for copy in saves(t):
            copy.wait()


def add_up(row_ref, values, sums_ref):
    hops, paths = row_ref.shape
    step = 256
    for i in range(0, sums_ref.shape[0], step):
        total = None
        for t in range(hops):
            hot = hot_cols(row_ref[t : t + 1, :], i, step)
            term = mm(hot, values[t * paths : (t + 1) * paths, :])
            total = term if total is None else total + term
        sums_ref[i : i + step, :] = total.astype(BF16)


def factors_kernel(
    xs_ref, cs_ref, count_ref, wi_ref, ws_ref,
    fr_ref, fu_ref, fn_ref, fm_ref, fc_ref, cb_ref, wi_s, ws_s,
):
    t = pl.program_id(0)
    _, paths, width = xs_ref.shape
    tile = 256

    @pl.when(t == 0)
    def _():
        wi_s[...] = halved(wi_ref)
        ws_s[...] = halved(ws_ref)

    for i in range(0, paths, tile):
        at = slice(i, i + tile)
        c = cs_ref[0, at, :]
        cb = c.astype(BF16)
        cb_ref[0, at, :] = cb
        r, u, n, bn = gates(mm(xs_ref[0, at, :], wi_s[...]), mm(cb, ws_s[...]), width)
        keep = count_ref[at, :] > t
        fn = jnp.where(keep, (1.0 - u) * (1.0 - n * n), 0.0)
        fm = fn * r
        fn_ref[0, at, :] = fn
        fm_ref[0, at, :] = fm
        fr_ref[0, at, :] = fm * bn * (1.0 - r)
        fu_ref[0, at, :] = jnp.where(keep, (c - n) * u * (1.0 - u), 0.0)
        fc_ref[0, at, :] = jnp.where(keep, u, 1.0)


def turn_back(agg, w, cot):
    act = jnp.tanh(mm(agg, w))
    pre = cot.astype(F32) * (1.0 - act * act)
    high = pre.astype(BF16)
    low = (pre - high.astype(F32)).astype(BF16)
    return high, low


def link_kernel(arrived_ref, row_ref, col_ref, w_ref, cot_ref, back_ref, arrived_s, sem):
    slots = back_ref.shape[0]
    tile = 256
    arrival = pltpu.make_async_copy(arrived_ref, arrived_s, sem)
    arrival.start()
    arrival.wait()
    for i in range(0, slots, tile):
        at = slice(i, i + tile)
        same = jnp.where(col_ref[at, :] == row_ref[...], 1.0, 0.0).astype(BF16)
        agg = mm(same, arrived_s[...]).astype(BF16)
        high, low = turn_back(agg, w_ref[...], cot_ref[at, :])
        back_ref[at, :] = (mm_t(high, w_ref[...]) + mm_t(low, w_ref[...])).astype(BF16)


def link_grad_kernel(arrived_ref, row_ref, w_ref, cot_ref, out_ref):
    tile = 256
    total = None
    for i in range(0, cot_ref.shape[0], tile):
        at = slice(i, i + tile)
        agg = mm(hot_cols(row_ref[...], i, tile), arrived_ref[...]).astype(BF16)
        high, low = turn_back(agg, w_ref[...], cot_ref[at, :])
        term = t_mm(agg, high) + t_mm(agg, low)
        total = term if total is None else total + term
    out_ref[...] = total


def backward_kernel(
    table_ref, row_ref, cot_ref, wi_ref, ws_ref, agg_grad_ref,
    fr_ref, fu_ref, fn_ref, fm_ref, fc_ref, xs_ref, cb_ref,
    grad_ref, da_ref, grads_ref,
    table_s, f_s, x_s, c_s, m_s, da_s, db_s, gi_s, gs_s, sem, da_sem, table_sem,
):
    _, hops, paths, width = f_s.shape
    slots = table_ref.shape[0]
    tile = 256
    arrival = pltpu.make_async_copy(table_ref, table_s, table_sem)
    arrival.start()

    def loads(t):
        pairs = [(ref.at[t], f_s.at[k, t]) for k, ref in enumerate(
            (fr_ref, fu_ref, fn_ref, fm_ref, fc_ref))]
        pairs += [(xs_ref.at[t], x_s.at[t]), (cb_ref.at[t], c_s.at[t])]
        return [
            pltpu.make_async_copy(source, target, sem.at[k, t])
            for k, (source, target) in enumerate(pairs)
        ]

    def save(t):
        return pltpu.make_async_copy(da_s.at[t], da_ref.at[t], da_sem.at[t])

    order = list(range(hops))[::-1]
    for t in order:
        for copy in loads(t):
            copy.start()

    grad_ref[...] = cot_ref[...].astype(F32)
    arrival.wait()

    def fetch(t, i):
        at = slice(i, i + tile)
        m_s[t, at, :] = t_mm(hot_cols(row_ref[t : t + 1, at], 0, slots), table_s[...])

    def weigh(t):
        gi = t_mm(x_s[t], da_s[t])
        gs = t_mm(c_s[t], db_s[t])
        if t == hops - 1:
            gi_s[...] = gi
            gs_s[...] = gs
        else:
            gi_s[...] += gi
            gs_s[...] += gs

    for i in range(0, paths, tile):
        fetch(hops - 1, i)
    for t in order:
        for copy in loads(t):
            copy.wait()
        for i in range(0, paths, tile):
            at = slice(i, i + tile)
            if t > 0:
                fetch(t - 1, i)
            d = grad_ref[at, :] + m_s[t, at, :]
            dr = (d * f_s[0, t, at, :]).astype(BF16)
            du = (d * f_s[1, t, at, :]).astype(BF16)
            da_s[t, at, :width] = dr
            da_s[t, at, width : 2 * width] = du
            da_s[t, at, 2 * width :] = (d * f_s[2, t, at, :]).astype(BF16)
            db_s[t, at, :width] = dr
            db_s[t, at, width : 2 * width] = du
            db_s[t, at, 2 * width :] = (d * f_s[3, t, at, :]).astype(BF16)
            back = mm_t(db_s[t, at, :], ws_ref[...]).astype(BF16).astype(F32)
            grad_ref[at, :] = d * f_s[4, t, at, :] + back
        if t < hops - 1:
            weigh(t + 1)
    for t in order:
        save(t).start()
    weigh(0)
    two = 2 * width
    grads_ref[:width, :] = gi_s[:, :two].astype(BF16)
    grads_ref[width:two, :] = gs_s[:, :two].astype(BF16)
    grads_ref[two : 3 * width, :width] = gi_s[:, two:].astype(BF16)
    grads_ref[two : 3 * width, width:] = gs_s[:, two:].astype(BF16)
    grads_ref[3 * width :, :width] = agg_grad_ref[...].astype(BF16)
    grads_ref[3 * width :, width:] = jnp.zeros_like(agg_grad_ref).astype(BF16)
    for t in order:
        save(t).wait()


def input_kernel(da_ref, row_ref, wi_ref, sums_ref, dx_s):
    hops, paths, _ = da_ref.shape
    for t in range(hops):
        dx_s[t * paths : (t + 1) * paths, :] = mm_t(da_ref[t], wi_ref[...]).astype(BF16)
    add_up(row_ref, dx_s, sums_ref)


def share_kernel(devices, parts_ref, sums_ref, out_ref):
    slots, wide = parts_ref.shape
    width = sums_ref.shape[1]
    lines = slots // devices
    total = jnp.sum(parts_ref[...].reshape(devices // 2, 2 * lines, wide).astype(F32), axis=0)
    total = total[:lines] + total[lines:]
    pair = jnp.concatenate([total, total], axis=0).astype(BF16)
    out_ref[:, :width] = sums_ref[...]
    out_ref[:, width:] = jnp.broadcast_to(pair[None], (devices // 2, 2 * lines, wide)).reshape(slots, wide)


def final_kernel(
    path_scale, link_scale, got_ref, row_ref, cot_ref,
    link_ref, gi_ref, gs_ref, ga_ref, got_s, out_s, sem, out_sem,
):
    width = ga_ref.shape[0]
    links = cot_ref.shape[0]
    two = 2 * width
    tile = 512
    arrival = pltpu.make_async_copy(got_ref, got_s, sem)
    arrival.start()
    arrival.wait()

    def save(k):
        at = pl.ds(k * tile, tile)
        return pltpu.make_async_copy(out_s.at[at, :], link_ref.at[at, :], out_sem.at[k])

    for k in range(links // tile):
        at = slice(k * tile, (k + 1) * tile)
        total = mm(hot_cols(row_ref[...], k * tile, tile), got_s[:, :width])
        out_s[at, :] = cot_ref[at, :].astype(F32) + total
        save(k).start()
    gi_ref[:, :two] = got_s[:width, width:].astype(F32) * path_scale
    gs_ref[:, :two] = got_s[width:two, width:].astype(F32) * path_scale
    gi_ref[:, two:] = got_s[two : 3 * width, width:two].astype(F32) * path_scale
    gs_ref[:, two:] = got_s[two : 3 * width, two:].astype(F32) * path_scale
    ga_ref[...] = got_s[3 * width :, width:two].astype(F32) * link_scale
    for k in range(links // tile):
        save(k).wait()


def exchange(rows, devices):
    lines, width = rows.shape
    chunks = rows.reshape(devices, lines // devices, width)
    got = lax.all_to_all(chunks, AXES, split_axis=0, concat_axis=0, tiled=True)
    return got.reshape(lines, width)


def per_device(
    path_state, link_state, hop_slot, hop_count, send_rows,
    w_input, w_state, w_agg, path_cot, link_cot,
):
    devices = lax.axis_size("outer") * lax.axis_size("sw")
    paths, width = path_state.shape
    hops = hop_slot.shape[1]
    links = link_state.shape[0]
    slots = devices * send_rows.shape[1]
    gate_cols = w_input.shape[1]
    shape = jax.ShapeDtypeStruct

    slot_rows = shape((slots, width), BF16)
    rows, send_row = call(
        pick_kernel, (slot_rows, shape((1, slots), jnp.int32)), [],
        (2 * slots * links * width, 2 * links * width, 16), send_rows.T, link_state,
    )
    table = exchange(rows, devices)

    valid = jnp.arange(hops, dtype=jnp.int32)[:, None] < hop_count[None, :]
    slot_row = jnp.where(valid, hop_slot.T, -1)
    count = hop_count[:, None]
    send_col = send_rows.reshape(slots, 1)
    cot_rows = call(
        pick_again_kernel, slot_rows, [],
        (2 * slots * links * width, 2 * links * width, 16), send_row, link_cot,
    )
    table, cot_rows, send_col, count, slot_row = lax.optimization_barrier(
        (table, cot_rows, send_col, count, slot_row)
    )
    sums, xs, cs = call(
        forward_kernel,
        (slot_rows, shape((hops, paths, width), BF16), shape((hops, paths, width), F32)),
        [
            pltpu.VMEM((slots, width), BF16),
            pltpu.VMEM((width, gate_cols), BF16),
            pltpu.VMEM((width, gate_cols), BF16),
            pltpu.VMEM((hops, paths, gate_cols), F32),
            pltpu.VMEM((hops, paths, width), BF16),
            pltpu.VMEM((hops, paths, width), F32),
            pltpu.VMEM((hops * paths, width), BF16),
            pltpu.SemaphoreType.DMA((2, hops)),
            pltpu.SemaphoreType.DMA,
        ],
        (4 * hops * paths * slots * width, 8 * hops * paths * width, 58),
        table, count, slot_row, path_state, w_input, w_state,
        in_specs=[ANY] + [VMEM] * 5,
        out_specs=(VMEM, ANY, ANY),
    )
    arrived = exchange(sums, devices)

    whole = lambda *dims: pl.BlockSpec(dims, lambda i: (0,) * len(dims))
    factor = shape((hops, paths, width), F32)
    hop_block = pl.BlockSpec((1, paths, width), lambda i: (i, 0, 0))
    factors = pl.pallas_call(
        factors_kernel,
        grid=(hops,),
        out_shape=(factor,) * 5 + (shape((hops, paths, width), BF16),),
        in_specs=[
            hop_block, hop_block, whole(paths, 1),
            whole(width, gate_cols), whole(width, gate_cols),
        ],
        out_specs=(hop_block,) * 6,
        scratch_shapes=[pltpu.VMEM((width, gate_cols), BF16)] * 2,
        compiler_params=pltpu.CompilerParams(vmem_limit_bytes=58 * MIB),
        cost_estimate=pl.CostEstimate(
            flops=4 * hops * paths * width * gate_cols,
            bytes_accessed=32 * hops * paths * width, transcendentals=0,
        ),
    )(xs, cs, count, w_input, w_state)
    arrived, factors = lax.optimization_barrier((arrived, factors))

    back = call(
        link_kernel, slot_rows,
        [pltpu.VMEM((slots, width), BF16), pltpu.SemaphoreType.DMA],
        (2 * slots * slots * width, 8 * slots * width, 16),
        arrived, send_row, send_col, w_agg, cot_rows,
        in_specs=[ANY] + [VMEM] * 4,
    )
    back_table = exchange(back, devices)
    agg_grad = call(
        link_grad_kernel, shape((width, width), F32), [],
        (4 * links * width * width, 6 * links * width, 16), arrived, send_row, w_agg, link_cot,
    )
    back_table, agg_grad = lax.optimization_barrier((back_table, agg_grad))

    grad_path, da, grads = call(
        backward_kernel,
        (
            shape((paths, width), F32),
            shape((hops, paths, gate_cols), BF16),
            shape((4 * width, 2 * width), BF16),
        ),
        [
            pltpu.VMEM((slots, width), BF16),
            pltpu.VMEM((5, hops, paths, width), F32),
            pltpu.VMEM((hops, paths, width), BF16),
            pltpu.VMEM((hops, paths, width), BF16),
            pltpu.VMEM((hops, paths, width), F32),
            pltpu.VMEM((hops, paths, gate_cols), BF16),
            pltpu.VMEM((hops, paths, gate_cols), BF16),
            pltpu.VMEM((width, gate_cols), F32),
            pltpu.VMEM((width, gate_cols), F32),
            pltpu.SemaphoreType.DMA((7, hops)),
            pltpu.SemaphoreType.DMA((hops,)),
            pltpu.SemaphoreType.DMA,
        ],
        (10 * hops * paths * width * gate_cols, 32 * hops * paths * width, 52),
        back_table, slot_row, path_cot, w_input, w_state, agg_grad,
        *factors[:5], xs, factors[5],
        in_specs=[ANY] + [VMEM] * 5 + [ANY] * 7,
        out_specs=(VMEM, ANY, VMEM),
    )
    parts = exchange(grads, devices)
    input_sums = call(
        input_kernel, slot_rows, [pltpu.VMEM((hops * paths, width), BF16)],
        (2 * hops * paths * (gate_cols + slots) * width, 2 * hops * paths * gate_cols, 24),
        da, slot_row, w_input,
    )
    parts, input_sums = lax.optimization_barrier((parts, input_sums))
    last = call(
        functools.partial(share_kernel, devices), shape((slots, 3 * width), BF16), [],
        (slots * width, 10 * slots * width, 16), parts, input_sums,
    )
    got = exchange(last, devices)
    wide = shape((width, gate_cols), F32)
    grad_link, input_grad, state_grad, agg_total = call(
        functools.partial(
            final_kernel, 1.0 / math.sqrt(paths * devices), 1.0 / math.sqrt(links * devices)
        ),
        (shape((links, width), F32), wide, wide, shape((width, width), F32)),
        [
            pltpu.VMEM((slots, 3 * width), BF16),
            pltpu.VMEM((links, width), F32),
            pltpu.SemaphoreType.DMA,
            pltpu.SemaphoreType.DMA((links // 512,)),
        ],
        (2 * slots * links * width, 8 * links * width, 16),
        got, send_row, link_cot,
        in_specs=[ANY, VMEM, VMEM],
        out_specs=(ANY, VMEM, VMEM, VMEM),
    )
    return grad_path, grad_link, input_grad, state_grad, agg_total


def solution(mesh):
    split = P(AXES, None)
    return jax.shard_map(
        per_device,
        mesh=mesh,
        in_specs=(split, split, split, P(AXES), split, P(), P(), P(), split, split),
        out_specs=(split, split, P(), P(), P()),
        check_vma=False,
    )
```

time: 184 us -> 163 us (0.89)
  blocking collectives: 0 us -> 28.7 us
  waiting for transfers between devices: 57.4 us -> 34.2 us
  Pallas kernels: 80 us -> 61.2 us
  starting transfers between devices: 37.2 us -> 28.7 us
  local copies, waits for them, and re-layouts: 5.98 us -> 8.01 us
    all_to_all x0 -> x1, blocking collectives: none -> 28.7 us  [exchange(): got = lax.all_to_all(chunks, AXES, split_axis=0, concat_axis=0, tiled=True)]
    all_to_all x6 -> x4, waiting for transfers between devices: 57.4 us -> 34.2 us  [exchange(): got = lax.all_to_all(chunks, AXES, split_axis=0, concat_axis=0, tiled=True)]
    pallas_call x9, Pallas kernels: 66.4 us -> 47.9 us  [call(): pl.pallas_call(kernel, out_shape=outs, in_specs=in_specs or [VMEM] * len(...]
    all_to_all x6 -> x4, starting transfers between devices: 37.2 us -> 28.7 us  [exchange(): got = lax.all_to_all(chunks, AXES, split_axis=0, concat_axis=0, tiled=True)]
    unnamed x18 -> x29, local copies, waits for them, and re-layouts: 4.3 us -> 6.82 us
  transfers between devices with their start and end apart: 6 -> 4, of which waited for: 5 -> 4; matrix products, arithmetic and copies ran while one was open for 1% -> 1% of each run, Pallas kernels for 20% -> 14%
where the time goes in v3:
time: 163 us; the launch traced here: 162 us
  Pallas kernels  61.2 us (38%)
  waiting for transfers between devices  34.2 us (21%)
  starting transfers between devices  28.7 us (18%)
  blocking collectives  28.7 us (18%)
  local copies, waits for them, and re-layouts  8.01 us (5%)
    pallas_call x9, Pallas kernels, call(): pl.pallas_call(kernel, out_shape=outs, in_specs=in_specs or [VMEM] * len(...  47.9 us
    all_to_all x4, waiting for transfers between devices, exchange(): got = lax.all_to_all(chunks, AXES, split_axis=0, concat_axis=0, tiled=True)  34.2 us
    all_to_all x4, starting transfers between devices, exchange(): got = lax.all_to_all(chunks, AXES, split_axis=0, concat_axis=0, tiled=True)  28.7 us
    all_to_all x1, blocking collectives, exchange(): got = lax.all_to_all(chunks, AXES, split_axis=0, concat_axis=0, tiled=True)  28.7 us
    pallas_call x1, Pallas kernels, per_device(): pl.pallas_call(factors_kernel, grid=(hops,), out_shape=(factor,) * 5 + (s...  13.3 us
    unnamed x29, local copies, waits for them, and re-layouts  6.82 us
  transfers between devices with their start and end apart: 4, of which 4 were waited for; matrix products, arithmetic and copies ran while one was open for 1% of the time, Pallas kernels for 14%

profile of v3, /device:TPU:1, one launch (start us, length us, event | category | flops | bytes accessed | tf_op | source)
XLA Modules:
  0.0 162.5 jit_solution(6245558686520656637)
XLA Ops:
  0.6 0.7 copy-done.2
  1.3 1.2 copy-done.4
  2.6 2.3 %shard_map.137 = (bf16[1024,256]{1,0:T(8,128)(2,1)}, s32[1,1024]{1,0:T(1,128)S(1)}) custom-call(s32[8,128]{1,0:T(8,128)S(1)} %bitcast.20, bf16[2048,256]{1,0:T(8,128)(2,1)S(1)} %copy-done.4), custom_call_target="tpu_custom_call" | custom-call | flops 1073741824 | bytes 1048576 | tf_op jit(solution)/shard_map/pallas_call | solution.py:38
  4.8 11.5 %all-to-all-start = ((bf16[128,8,256]{2,1,0:T(8,128)(2,1)}), bf16[128,8,256]{2,1,0:T(8,128)(2,1)S(1)}, u32[]{:S(2)}, u32[]{:S(2)}) async-start(bf16[128,8,256]{2,1,0:T(8,128)(2,1)} %bitcast.1), calls=%async_computation | async-start | bytes 1048576 | tf_op jit(solution)/shard_map/all_to_all | solution.py:355
  16.3 0.1 copy.16
  16.5 0.1 reshape.46
  16.6 1.3 shard_map.138.cot_ref
  17.9 0.6 bitcast_select_fusion.row_ref
  18.5 11.8 %all-to-all-done = bf16[128,8,256]{2,1,0:T(8,128)(2,1)S(1)} async-done(((bf16[128,8,256]{2,1,0:T(8,128)(2,1)}), bf16[128,8,256]{2,1,0:T(8,128)(2,1)S(1)}, u32[]{:S(2)}, u32[]{:S(2)}) %all-to-all-start) | async-done | bytes 524320 | tf_op jit(solution)/shard_map/all_to_all | solution.py:355
  30.3 0.9 copy.17.count_ref
  31.2 14.4 %shard_map.139 = (bf16[1024,256]{1,0:T(8,128)(2,1)}, bf16[8,512,256]{2,1,0:T(8,128)(2,1)}, f32[8,512,256]{2,1,0:T(8,128)}) custom-call(bf16[1024,256]{1,0:T(8,128)(2,1)} %bitcast.22, s32[512,1]{1,0:T(8,128)} %copy.17.count_ref, s32[8,512]{1,0:T(8,128)} %bitcast_select_fusion.row_ref, bf16[512,256]{1,0:T(8,128)(2,1)} %start_ref.1, bf16[256,768]{1,0:T(8,128)(2,1)} %wi_ref.7, ...), custom_call_target="tpu_custom_call" | custom-call | flops 4294967296 | bytes 8388608 | tf_op jit(solution)/shard_map/pallas_call | solution.py:38
  45.6 4.0 %all-to-all-start.1 = ((bf16[128,8,256]{2,1,0:T(8,128)(2,1)}), bf16[128,8,256]{2,1,0:T(8,128)(2,1)S(1)}, u32[]{:S(2)}, u32[]{:S(2)}) async-start(bf16[128,8,256]{2,1,0:T(8,128)(2,1)} %bitcast.23), calls=%async_computation.1 | async-start | bytes 1048576 | tf_op jit(solution)/shard_map/all_to_all | solution.py:355
  49.6 0.2 copy.19.col_ref
  49.9 0.0 copy-start
  49.9 13.3 %shard_map.140 = (f32[8,512,256]{2,1,0:T(8,128)}, f32[8,512,256]{2,1,0:T(8,128)}, f32[8,512,256]{2,1,0:T(8,128)}, f32[8,512,256]{2,1,0:T(8,128)}, f32[8,512,256]{2,1,0:T(8,128)}, /*index=5*/bf16[8,512,256]{2,1,0:T(8,128)(2,1)}) custom-call(bf16[8,512,256]{2,1,0:T(8,128)(2,1)} %get-tuple-element.45.xs_ref, f32[8,512,256]{2,1,0:T(8,128)} %get-tuple-element.46.cs_ref, ...), custom_call_target="tpu_custom_call" | custom-call | flops 3221225472 | bytes 33554432 | tf_op jit(solution)/shard_map/pallas_call | solution.py:413
  63.2 0.0 copy-start.1
  63.2 0.0 copy-start.9
  63.2 0.6 all-to-all-done.1
  63.8 3.4 %shard_map.141 = bf16[1024,256]{1,0:T(8,128)(2,1)} custom-call(bf16[1024,256]{1,0:T(8,128)(2,1)S(1)} %bitcast.16, s32[1,1024]{1,0:T(1,128)S(1)} %get-tuple-element.40.row_ref, s32[1024,1]{1,0:T(8,128)S(1)} %copy.19.col_ref, bf16[256,256]{1,0:T(8,128)(2,1)S(1)} %copy-done, bf16[1024,256]{1,0:T(8,128)(2,1)S(1)} %shard_map.138.cot_ref), custom_call_target="tpu_custom_call" | custom-call | flops 536870912 | bytes 2097152 | tf_op jit(solution)/shard_map/pallas_call | solution.py:38
  67.2 9.4 %all-to-all-start.2 = ((bf16[128,8,256]{2,1,0:T(8,128)(2,1)}), bf16[128,8,256]{2,1,0:T(8,128)(2,1)S(1)}, u32[]{:S(2)}, u32[]{:S(2)}) async-start(bf16[128,8,256]{2,1,0:T(8,128)(2,1)} %bitcast.7), calls=%async_computation.2 | async-start | bytes 1048576 | tf_op jit(solution)/shard_map/all_to_all | solution.py:355
  76.5 4.1 %shard_map.142.agg_grad_ref = f32[256,256]{1,0:T(8,128)S(1)} custom-call(bf16[1024,256]{1,0:T(8,128)(2,1)S(1)} %bitcast.17, s32[1,1024]{1,0:T(1,128)S(1)} %get-tuple-element.40.row_ref, bf16[256,256]{1,0:T(8,128)(2,1)S(1)} %copy-done, bf16[2048,256]{1,0:T(8,128)(2,1)S(1)} %copy-done.5), custom_call_target="tpu_custom_call" | custom-call | flops 536870912 | bytes 3145728 | tf_op jit(solution)/shard_map/pallas_call | solution.py:38
  80.6 9.9 %all-to-all-done.2 = bf16[128,8,256]{2,1,0:T(8,128)(2,1)S(1)} async-done(((bf16[128,8,256]{2,1,0:T(8,128)(2,1)}), bf16[128,8,256]{2,1,0:T(8,128)(2,1)S(1)}, u32[]{:S(2)}, u32[]{:S(2)}) %all-to-all-start.2) | async-done | bytes 524320 | tf_op jit(solution)/shard_map/all_to_all | solution.py:355
  90.5 1.0 copy-done.7
  91.5 14.4 %shard_map.143 = (f32[512,256]{1,0:T(8,128)}, bf16[8,512,768]{2,1,0:T(8,128)(2,1)}, bf16[1024,512]{1,0:T(8,128)(2,1)}) custom-call(bf16[1024,256]{1,0:T(8,128)(2,1)S(1)} %bitcast.19, s32[8,512]{1,0:T(8,128)S(1)} %copy-done.1, bf16[512,256]{1,0:T(8,128)(2,1)S(1)} %copy-done.9, bf16[256,768]{1,0:T(8,128)(2,1)S(1)} %copy-done.7, ...), custom_call_target="tpu_custom_call" | custom-call | flops 8053063680 | bytes 33554432 | tf_op jit(solution)/shard_map/pallas_call | solution.py:38
  106.0 3.8 %all-to-all-start.3 = ((bf16[128,8,512]{2,1,0:T(8,128)(2,1)}), bf16[128,8,512]{2,1,0:T(8,128)(2,1)S(1)}, u32[]{:S(2)}, u32[]{:S(2)}) async-start(bf16[128,8,512]{2,1,0:T(8,128)(2,1)} %bitcast.21), calls=%async_computation.3 | async-start | bytes 2097152 | tf_op jit(solution)/shard_map/all_to_all | solution.py:355
  109.8 1.0 copy-done.8
  110.8 2.8 %copy-done.10 = bf16[8,512,768]{2,1,0:T(8,128)(2,1)S(1)} copy-done((bf16[8,512,768]{2,1,0:T(8,128)(2,1)S(1)}, bf16[8,512,768]{2,1,0:T(8,128)(2,1)}, u32[]{:S(2)}) %copy-start.10) | copy-done | bytes 6291480
  113.6 4.0 %shard_map.144.sums_ref = bf16[1024,256]{1,0:T(8,128)(2,1)S(1)} custom-call(bf16[8,512,768]{2,1,0:T(8,128)(2,1)S(1)} %copy-done.10, s32[8,512]{1,0:T(8,128)S(1)} %copy-done.1, bf16[256,768]{1,0:T(8,128)(2,1)S(1)} %copy-done.8), custom_call_target="tpu_custom_call" | custom-call | flops 3758096384 | bytes 6291456 | tf_op jit(solution)/shard_map/pallas_call | solution.py:38
  117.6 12.0 %all-to-all-done.3 = bf16[128,8,512]{2,1,0:T(8,128)(2,1)S(1)} async-done(((bf16[128,8,512]{2,1,0:T(8,128)(2,1)}), bf16[128,8,512]{2,1,0:T(8,128)(2,1)S(1)}, u32[]{:S(2)}, u32[]{:S(2)}) %all-to-all-start.3) | async-done | bytes 1048608 | tf_op jit(solution)/shard_map/all_to_all | solution.py:355
  129.6 0.2 shard_map.145
  129.8 28.7 %all_to_all.25 = bf16[128,8,768]{2,1,0:T(8,128)(2,1)S(1)} all-to-all(bf16[128,8,768]{2,1,0:T(8,128)(2,1)S(1)} %bitcast.14), channel_id=1, replica_groups=mesh['outer'=32,'sw'=4] {'outer','sw'}, dimensions={0} | all-to-all | bytes 3145728 | tf_op jit(solution)/shard_map/all_to_all | solution.py:355
  158.4 3.8 %shard_map.146 = (f32[2048,256]{1,0:T(8,128)}, f32[256,768]{1,0:T(8,128)}, f32[256,768]{1,0:T(8,128)}, f32[256,256]{1,0:T(8,128)}) custom-call(bf16[1024,768]{1,0:T(8,128)(2,1)S(1)} %bitcast.18, s32[1,1024]{1,0:T(1,128)S(1)} %get-tuple-element.40.row_ref, bf16[2048,256]{1,0:T(8,128)(2,1)S(1)} %copy-done.5), custom_call_target="tpu_custom_call" | custom-call | flops 1073741824 | bytes 4194304 | tf_op jit(solution)/shard_map/pallas_call | solution.py:38
  (20 shorter events, 0.0 us)
Async XLA Ops:
  0.6 0.7 copy-start.2
  1.3 1.2 copy-start.4
  2.5 13.8 %copy-start.3 = (s32[128,8]{0,1:T(8,128)S(1)}, s32[128,8]{0,1:T(8,128)}, u32[]{:S(2)}) copy-start(s32[128,8]{0,1:T(8,128)} %param.14) | copy-start | bytes 12292
  2.5 14.0 %copy-start.5 = (bf16[2048,256]{1,0:T(8,128)(2,1)S(1)}, bf16[2048,256]{1,0:T(8,128)(2,1)}, u32[]{:S(2)}) copy-start(bf16[2048,256]{1,0:T(8,128)(2,1)} %cot_ref.5) | copy-start | bytes 3145732
  2.6 15.3 %copy-start.12 = (s32[512,8]{0,1:T(8,128)S(1)}, s32[512,8]{0,1:T(8,128)}, u32[]{:S(2)}) copy-start(s32[512,8]{0,1:T(8,128)} %param.12) | copy-start | bytes 49156
  2.6 15.3 %copy-start.13 = (s32[512]{0:T(512)S(1)}, s32[512]{0:T(512)}, u32[]{:S(2)}) copy-start(s32[512]{0:T(512)} %param.13) | copy-start | bytes 6148
  4.8 25.5 %all-to-all-start = ((bf16[128,8,256]{2,1,0:T(8,128)(2,1)}), bf16[128,8,256]{2,1,0:T(8,128)(2,1)S(1)}, u32[]{:S(2)}, u32[]{:S(2)}) async-start(bf16[128,8,256]{2,1,0:T(8,128)(2,1)} %bitcast.1), calls=%async_computation | async-start | bytes 1048576 | tf_op jit(solution)/shard_map/all_to_all | solution.py:355
  30.3 0.9 copy-start.11
  45.6 18.1 %all-to-all-start.1 = ((bf16[128,8,256]{2,1,0:T(8,128)(2,1)}), bf16[128,8,256]{2,1,0:T(8,128)(2,1)S(1)}, u32[]{:S(2)}, u32[]{:S(2)}) async-start(bf16[128,8,256]{2,1,0:T(8,128)(2,1)} %bitcast.23), calls=%async_computation.1 | async-start | bytes 1048576 | tf_op jit(solution)/shard_map/all_to_all | solution.py:355
  49.9 13.9 %copy-start = (bf16[256,256]{1,0:T(8,128)(2,1)S(1)}, bf16[256,256]{1,0:T(8,128)(2,1)}, u32[]{:S(2)}) copy-start(bf16[256,256]{1,0:T(8,128)(2,1)} %w_ref.3) | copy-start | bytes 393220
  63.2 27.4 %copy-start.1 = (s32[8,512]{1,0:T(8,128)S(1)}, s32[8,512]{1,0:T(8,128)}, u32[]{:S(2)}) copy-start(s32[8,512]{1,0:T(8,128)} %bitcast_select_fusion.row_ref) | copy-start | bytes 49156
  63.2 27.4 %copy-start.6 = (bf16[256,768]{1,0:T(8,128)(2,1)S(1)}, bf16[256,768]{1,0:T(8,128)(2,1)}, u32[]{:S(2)}) copy-start(bf16[256,768]{1,0:T(8,128)(2,1)} %ws_ref.5) | copy-start | bytes 1179652
  63.2 27.3 %copy-start.9 = (bf16[512,256]{1,0:T(8,128)(2,1)S(1)}, bf16[512,256]{1,0:T(8,128)(2,1)}, u32[]{:S(2)}) copy-start(bf16[512,256]{1,0:T(8,128)(2,1)} %cot_ref.4) | copy-start | bytes 786436
  67.2 23.4 %all-to-all-start.2 = ((bf16[128,8,256]{2,1,0:T(8,128)(2,1)}), bf16[128,8,256]{2,1,0:T(8,128)(2,1)S(1)}, u32[]{:S(2)}, u32[]{:S(2)}) async-start(bf16[128,8,256]{2,1,0:T(8,128)(2,1)} %bitcast.7), calls=%async_computation.2 | async-start | bytes 1048576 | tf_op jit(solution)/shard_map/all_to_all | solution.py:355
  90.5 1.0 copy-start.7
  106.0 23.6 %all-to-all-start.3 = ((bf16[128,8,512]{2,1,0:T(8,128)(2,1)}), bf16[128,8,512]{2,1,0:T(8,128)(2,1)S(1)}, u32[]{:S(2)}, u32[]{:S(2)}) async-start(bf16[128,8,512]{2,1,0:T(8,128)(2,1)} %bitcast.21), calls=%async_computation.3 | async-start | bytes 2097152 | tf_op jit(solution)/shard_map/all_to_all | solution.py:355
  109.8 1.0 copy-start.8
  110.8 2.8 %copy-start.10 = (bf16[8,512,768]{2,1,0:T(8,128)(2,1)S(1)}, bf16[8,512,768]{2,1,0:T(8,128)(2,1)}, u32[]{:S(2)}) copy-start(bf16[8,512,768]{2,1,0:T(8,128)(2,1)} %get-tuple-element.66.da_ref) | copy-start | bytes 18874372

commit v4 on v3

--- a/solution.py
+++ b/solution.py
@@ -113,20 +113,16 @@
             pltpu.make_async_copy(c_s.at[t], cs_ref.at[t], sem.at[1, t]),
         )
 
-    def enter(t, i):
-        at = slice(i, i + tile)
-        hot = hot_cols(row_ref[t : t + 1, at], 0, slots)
-        x = t_mm(hot, table_s[...]).astype(BF16)
-        x_s[t, at, :] = x
-        a_s[t, at, :] = mm(x, wi_s[...])
-
-    for i in range(0, paths, tile):
-        enter(0, i)
     for t in range(hops):
+        hot = hot_cols(row_ref[t : t + 1, :], 0, slots)
+        x_s[t] = t_mm(hot, table_s[...]).astype(BF16)
+
+    a_s[0] = mm(x_s[0], wi_s[...])
+    for t in range(hops):
+        if t + 1 < hops:
+            a_s[t + 1] = mm(x_s[t + 1], wi_s[...])
         for i in range(0, paths, tile):
             at = slice(i, i + tile)
-            if t + 1 < hops:
-                enter(t + 1, i)
             c = c_s[t, at, :]
             b = mm(c.astype(BF16), ws_s[...])
             r, u, n, _ = gates(a_s[t, at, :], b, width)
@@ -178,10 +174,10 @@
         keep = count_ref[at, :] > t
         fn = jnp.where(keep, (1.0 - u) * (1.0 - n * n), 0.0)
         fm = fn * r
-        fn_ref[0, at, :] = fn
-        fm_ref[0, at, :] = fm
-        fr_ref[0, at, :] = fm * bn * (1.0 - r)
-        fu_ref[0, at, :] = jnp.where(keep, (c - n) * u * (1.0 - u), 0.0)
+        fn_ref[0, at, :] = fn.astype(BF16)
+        fm_ref[0, at, :] = fm.astype(BF16)
+        fr_ref[0, at, :] = (fm * bn * (1.0 - r)).astype(BF16)
+        fu_ref[0, at, :] = jnp.where(keep, (c - n) * u * (1.0 - u), 0.0).astype(BF16)
         fc_ref[0, at, :] = jnp.where(keep, u, 1.0)
 
 
@@ -223,7 +219,7 @@
     table_ref, row_ref, cot_ref, wi_ref, ws_ref, agg_grad_ref,
     fr_ref, fu_ref, fn_ref, fm_ref, fc_ref, xs_ref, cb_ref,
     grad_ref, da_ref, grads_ref,
-    table_s, f_s, x_s, c_s, m_s, da_s, db_s, gi_s, gs_s, sem, da_sem, table_sem,
+    table_s, f_s, fc_s, x_s, c_s, m_s, da_s, db_s, gi_s, gs_s, sem, da_sem, table_sem,
 ):
     _, hops, paths, width = f_s.shape
     slots = table_ref.shape[0]
@@ -233,8 +229,10 @@
 
     def loads(t):
         pairs = [(ref.at[t], f_s.at[k, t]) for k, ref in enumerate(
-            (fr_ref, fu_ref, fn_ref, fm_ref, fc_ref))]
-        pairs += [(xs_ref.at[t], x_s.at[t]), (cb_ref.at[t], c_s.at[t])]
+            (fr_ref, fu_ref, fn_ref, fm_ref))]
+        pairs += [
+            (fc_ref.at[t], fc_s.at[t]), (xs_ref.at[t], x_s.at[t]), (cb_ref.at[t], c_s.at[t]),
+        ]
         return [
             pltpu.make_async_copy(source, target, sem.at[k, t])
             for k, (source, target) in enumerate(pairs)
@@ -251,29 +249,13 @@
     grad_ref[...] = cot_ref[...].astype(F32)
     arrival.wait()
 
-    def fetch(t, i):
-        at = slice(i, i + tile)
-        m_s[t, at, :] = t_mm(hot_cols(row_ref[t : t + 1, at], 0, slots), table_s[...])
-
-    def weigh(t):
-        gi = t_mm(x_s[t], da_s[t])
-        gs = t_mm(c_s[t], db_s[t])
-        if t == hops - 1:
-            gi_s[...] = gi
-            gs_s[...] = gs
-        else:
-            gi_s[...] += gi
-            gs_s[...] += gs
-
-    for i in range(0, paths, tile):
-        fetch(hops - 1, i)
+    for t in order:
+        m_s[t] = t_mm(hot_cols(row_ref[t : t + 1, :], 0, slots), table_s[...])
     for t in order:
         for copy in loads(t):
             copy.wait()
         for i in range(0, paths, tile):
             at = slice(i, i + tile)
-            if t > 0:
-                fetch(t - 1, i)
             d = grad_ref[at, :] + m_s[t, at, :]
             dr = (d * f_s[0, t, at, :]).astype(BF16)
             du = (d * f_s[1, t, at, :]).astype(BF16)
@@ -284,12 +266,10 @@
             db_s[t, at, width : 2 * width] = du
             db_s[t, at, 2 * width :] = (d * f_s[3, t, at, :]).astype(BF16)
             back = mm_t(db_s[t, at, :], ws_ref[...]).astype(BF16).astype(F32)
-            grad_ref[at, :] = d * f_s[4, t, at, :] + back
-        if t < hops - 1:
-            weigh(t + 1)
-    for t in order:
+            grad_ref[at, :] = d * fc_s[t, at, :] + back
         save(t).start()
-    weigh(0)
+    gi_s[...] = t_mm(flat(x_s), flat(da_s))
+    gs_s[...] = t_mm(flat(c_s), flat(db_s))
     two = 2 * width
     grads_ref[:width, :] = gi_s[:, :two].astype(BF16)
     grads_ref[width:two, :] = gs_s[:, :two].astype(BF16)
@@ -299,6 +279,11 @@
     grads_ref[3 * width :, width:] = jnp.zeros_like(agg_grad_ref).astype(BF16)
     for t in order:
         save(t).wait()
+
+
+def flat(ref):
+    hops, paths, width = ref.shape
+    return ref[...].reshape(hops * paths, width)
 
 
 def input_kernel(da_ref, row_ref, wi_ref, sums_ref, dx_s):
@@ -409,11 +394,12 @@
 
     whole = lambda *dims: pl.BlockSpec(dims, lambda i: (0,) * len(dims))
     factor = shape((hops, paths, width), F32)
+    short = shape((hops, paths, width), BF16)
     hop_block = pl.BlockSpec((1, paths, width), lambda i: (i, 0, 0))
     factors = pl.pallas_call(
         factors_kernel,
         grid=(hops,),
-        out_shape=(factor,) * 5 + (shape((hops, paths, width), BF16),),
+        out_shape=(short,) * 4 + (factor, short),
         in_specs=[
             hop_block, hop_block, whole(paths, 1),
             whole(width, gate_cols), whole(width, gate_cols),
@@ -451,7 +437,8 @@
         ),
         [
             pltpu.VMEM((slots, width), BF16),
-            pltpu.VMEM((5, hops, paths, width), F32),
+            pltpu.VMEM((4, hops, paths, width), BF16),
+            pltpu.VMEM((hops, paths, width), F32),
             pltpu.VMEM((hops, paths, width), BF16),
             pltpu.VMEM((hops, paths, width), BF16),
             pltpu.VMEM((hops, paths, width), F32),

time: 163 us -> 158 us (0.969)
  Pallas kernels: 61.2 us -> 55.7 us
    pallas_call x9, Pallas kernels: 47.9 us -> 43.6 us  [call(): pl.pallas_call(kernel, out_shape=outs, in_specs=in_specs or [VMEM] * len(...]
    unnamed x29 -> x33, local copies, waits for them, and re-layouts: 6.82 us -> 6.48 us
where the time goes in v4:
time: 158 us; the launch traced here: 157 us
  Pallas kernels  55.7 us (35%)
  waiting for transfers between devices  35.7 us (23%)
  blocking collectives  28.7 us (18%)
  starting transfers between devices  27.5 us (17%)
  local copies, waits for them, and re-layouts  7.67 us (5%)
    pallas_call x9, Pallas kernels, call(): pl.pallas_call(kernel, out_shape=outs, in_specs=in_specs or [VMEM] * len(...  43.6 us
    all_to_all x4, waiting for transfers between devices, exchange(): got = lax.all_to_all(chunks, AXES, split_axis=0, concat_axis=0, tiled=True)  35.7 us
    all_to_all x1, blocking collectives, exchange(): got = lax.all_to_all(chunks, AXES, split_axis=0, concat_axis=0, tiled=True)  28.7 us
    all_to_all x4, starting transfers between devices, exchange(): got = lax.all_to_all(chunks, AXES, split_axis=0, concat_axis=0, tiled=True)  27.5 us
    pallas_call x1, Pallas kernels, per_device(): pl.pallas_call(factors_kernel, grid=(hops,), out_shape=(short,) * 4 + (fa...  12.1 us
    unnamed x33, local copies, waits for them, and re-layouts  6.48 us
  transfers between devices with their start and end apart: 4, of which 4 were waited for; matrix products, arithmetic and copies ran while one was open for 1% of the time, Pallas kernels for 14%

profile of v4, /device:TPU:1, one launch (start us, length us, event | category | flops | bytes accessed | tf_op | source)
XLA Modules:
  0.0 156.9 jit_solution(17234506492729124705)
XLA Ops:
  0.6 0.7 copy-done.2
  1.3 1.2 copy-done.4
  2.5 2.3 %shard_map.137 = (bf16[1024,256]{1,0:T(8,128)(2,1)}, s32[1,1024]{1,0:T(1,128)S(1)}) custom-call(s32[8,128]{1,0:T(8,128)S(1)} %bitcast.20, bf16[2048,256]{1,0:T(8,128)(2,1)S(1)} %copy-done.4), custom_call_target="tpu_custom_call" | custom-call | flops 1073741824 | bytes 1048576 | tf_op jit(solution)/shard_map/pallas_call | solution.py:38
  4.8 11.5 %all-to-all-start = ((bf16[128,8,256]{2,1,0:T(8,128)(2,1)}), bf16[128,8,256]{2,1,0:T(8,128)(2,1)S(1)}, u32[]{:S(2)}, u32[]{:S(2)}) async-start(bf16[128,8,256]{2,1,0:T(8,128)(2,1)} %bitcast.1), calls=%async_computation | async-start | bytes 1048576 | tf_op jit(solution)/shard_map/all_to_all | solution.py:340
  16.3 0.0 copy-start.14
  16.4 0.0 copy-start.15
  16.4 0.1 copy.16
  16.5 0.1 reshape.46
  16.6 1.3 shard_map.138.cot_ref
  17.9 0.6 bitcast_select_fusion.row_ref
  18.5 11.8 %all-to-all-done = bf16[128,8,256]{2,1,0:T(8,128)(2,1)S(1)} async-done(((bf16[128,8,256]{2,1,0:T(8,128)(2,1)}), bf16[128,8,256]{2,1,0:T(8,128)(2,1)S(1)}, u32[]{:S(2)}, u32[]{:S(2)}) %all-to-all-start) | async-done | bytes 524320 | tf_op jit(solution)/shard_map/all_to_all | solution.py:340
  30.3 0.9 copy.17.count_ref
  31.2 11.5 %shard_map.139 = (bf16[1024,256]{1,0:T(8,128)(2,1)}, bf16[8,512,256]{2,1,0:T(8,128)(2,1)}, f32[8,512,256]{2,1,0:T(8,128)}) custom-call(bf16[1024,256]{1,0:T(8,128)(2,1)} %bitcast.22, s32[512,1]{1,0:T(8,128)} %copy.17.count_ref, s32[8,512]{1,0:T(8,128)} %bitcast_select_fusion.row_ref, bf16[512,256]{1,0:T(8,128)(2,1)} %start_ref.1, bf16[256,768]{1,0:T(8,128)(2,1)} %wi_ref.7, ...), custom_call_target="tpu_custom_call" | custom-call | flops 4294967296 | bytes 8388608 | tf_op jit(solution)/shard_map/pallas_call | solution.py:38
  42.7 3.8 %all-to-all-start.1 = ((bf16[128,8,256]{2,1,0:T(8,128)(2,1)}), bf16[128,8,256]{2,1,0:T(8,128)(2,1)S(1)}, u32[]{:S(2)}, u32[]{:S(2)}) async-start(bf16[128,8,256]{2,1,0:T(8,128)(2,1)} %bitcast.23), calls=%async_computation.1 | async-start | bytes 1048576 | tf_op jit(solution)/shard_map/all_to_all | solution.py:340
  46.6 0.2 copy.19.col_ref
  46.8 12.1 %shard_map.140 = (bf16[8,512,256]{2,1,0:T(8,128)(2,1)}, bf16[8,512,256]{2,1,0:T(8,128)(2,1)}, bf16[8,512,256]{2,1,0:T(8,128)(2,1)}, bf16[8,512,256]{2,1,0:T(8,12...) custom-call(bf16[8,512,256]{2,1,0:T(8,128)(2,1)} %get-tuple-element.45.xs_ref, ...), custom_call_target="tpu_custom_call" | custom-call | flops 3221225472 | bytes 33554432 | tf_op jit(solution)/shard_map/pallas_call | solution.py:399
  58.9 1.8 %all-to-all-done.1 = bf16[128,8,256]{2,1,0:T(8,128)(2,1)S(1)} async-done(((bf16[128,8,256]{2,1,0:T(8,128)(2,1)}), bf16[128,8,256]{2,1,0:T(8,128)(2,1)S(1)}, u32[]{:S(2)}, u32[]{:S(2)}) %all-to-all-start.1) | async-done | bytes 524320 | tf_op jit(solution)/shard_map/all_to_all | solution.py:340
  60.7 3.4 %shard_map.141 = bf16[1024,256]{1,0:T(8,128)(2,1)} custom-call(bf16[1024,256]{1,0:T(8,128)(2,1)S(1)} %bitcast.16, s32[1,1024]{1,0:T(1,128)S(1)} %get-tuple-element.40.row_ref, s32[1024,1]{1,0:T(8,128)S(1)} %copy.19.col_ref, bf16[256,256]{1,0:T(8,128)(2,1)S(1)} %copy-done, bf16[1024,256]{1,0:T(8,128)(2,1)S(1)} %shard_map.138.cot_ref), custom_call_target="tpu_custom_call" | custom-call | flops 536870912 | bytes 2097152 | tf_op jit(solution)/shard_map/pallas_call | solution.py:38
  64.1 8.2 %all-to-all-start.2 = ((bf16[128,8,256]{2,1,0:T(8,128)(2,1)}), bf16[128,8,256]{2,1,0:T(8,128)(2,1)S(1)}, u32[]{:S(2)}, u32[]{:S(2)}) async-start(bf16[128,8,256]{2,1,0:T(8,128)(2,1)} %bitcast.7), calls=%async_computation.2 | async-start | bytes 1048576 | tf_op jit(solution)/shard_map/all_to_all | solution.py:340
  72.3 4.1 %shard_map.142.agg_grad_ref = f32[256,256]{1,0:T(8,128)S(1)} custom-call(bf16[1024,256]{1,0:T(8,128)(2,1)S(1)} %bitcast.17, s32[1,1024]{1,0:T(1,128)S(1)} %get-tuple-element.40.row_ref, bf16[256,256]{1,0:T(8,128)(2,1)S(1)} %copy-done, bf16[2048,256]{1,0:T(8,128)(2,1)S(1)} %copy-done.5), custom_call_target="tpu_custom_call" | custom-call | flops 536870912 | bytes 3145728 | tf_op jit(solution)/shard_map/pallas_call | solution.py:38
  76.4 0.7 copy-done.10
  77.1 9.2 %all-to-all-done.2 = bf16[128,8,256]{2,1,0:T(8,128)(2,1)S(1)} async-done(((bf16[128,8,256]{2,1,0:T(8,128)(2,1)}), bf16[128,8,256]{2,1,0:T(8,128)(2,1)S(1)}, u32[]{:S(2)}, u32[]{:S(2)}) %all-to-all-start.2) | async-done | bytes 524320 | tf_op jit(solution)/shard_map/all_to_all | solution.py:340
  86.3 0.9 copy-done.11
  87.3 13.0 %shard_map.143 = (f32[512,256]{1,0:T(8,128)}, bf16[8,512,768]{2,1,0:T(8,128)(2,1)}, bf16[1024,512]{1,0:T(8,128)(2,1)}) custom-call(bf16[1024,256]{1,0:T(8,128)(2,1)S(1)} %bitcast.19, s32[8,512]{1,0:T(8,128)S(1)} %copy-done.1, bf16[512,256]{1,0:T(8,128)(2,1)S(1)} %copy-done.9, bf16[256,768]{1,0:T(8,128)(2,1)S(1)} %copy-done.7, ...), custom_call_target="tpu_custom_call" | custom-call | flops 8053063680 | bytes 33554432 | tf_op jit(solution)/shard_map/pallas_call | solution.py:38
  100.2 0.0 copy-start.8
  100.2 4.0 %all-to-all-start.3 = ((bf16[128,8,512]{2,1,0:T(8,128)(2,1)}), bf16[128,8,512]{2,1,0:T(8,128)(2,1)S(1)}, u32[]{:S(2)}, u32[]{:S(2)}) async-start(bf16[128,8,512]{2,1,0:T(8,128)(2,1)} %bitcast.21), calls=%async_computation.3 | async-start | bytes 2097152 | tf_op jit(solution)/shard_map/all_to_all | solution.py:340
  104.2 2.8 %copy-done.12 = bf16[8,512,768]{2,1,0:T(8,128)(2,1)S(1)} copy-done((bf16[8,512,768]{2,1,0:T(8,128)(2,1)S(1)}, bf16[8,512,768]{2,1,0:T(8,128)(2,1)}, u32[]{:S(2)}) %copy-start.12) | copy-done | bytes 6291480
  107.0 4.0 %shard_map.144.sums_ref = bf16[1024,256]{1,0:T(8,128)(2,1)S(1)} custom-call(bf16[8,512,768]{2,1,0:T(8,128)(2,1)S(1)} %copy-done.12, s32[8,512]{1,0:T(8,128)S(1)} %copy-done.1, bf16[256,768]{1,0:T(8,128)(2,1)S(1)} %copy-done.8), custom_call_target="tpu_custom_call" | custom-call | flops 3758096384 | bytes 6291456 | tf_op jit(solution)/shard_map/pallas_call | solution.py:38
  111.0 12.9 %all-to-all-done.3 = bf16[128,8,512]{2,1,0:T(8,128)(2,1)S(1)} async-done(((bf16[128,8,512]{2,1,0:T(8,128)(2,1)}), bf16[128,8,512]{2,1,0:T(8,128)(2,1)S(1)}, u32[]{:S(2)}, u32[]{:S(2)}) %all-to-all-start.3) | async-done | bytes 1048608 | tf_op jit(solution)/shard_map/all_to_all | solution.py:340
  123.9 0.2 shard_map.145
  124.2 28.7 %all_to_all.25 = bf16[128,8,768]{2,1,0:T(8,128)(2,1)S(1)} all-to-all(bf16[128,8,768]{2,1,0:T(8,128)(2,1)S(1)} %bitcast.14), channel_id=1, replica_groups=mesh['outer'=32,'sw'=4] {'outer','sw'}, dimensions={0} | all-to-all | bytes 3145728 | tf_op jit(solution)/shard_map/all_to_all | solution.py:340
  152.8 3.8 %shard_map.146 = (f32[2048,256]{1,0:T(8,128)}, f32[256,768]{1,0:T(8,128)}, f32[256,768]{1,0:T(8,128)}, f32[256,256]{1,0:T(8,128)}) custom-call(bf16[1024,768]{1,0:T(8,128)(2,1)S(1)} %bitcast.18, s32[1,1024]{1,0:T(1,128)S(1)} %get-tuple-element.40.row_ref, bf16[2048,256]{1,0:T(8,128)(2,1)S(1)} %copy-done.5), custom_call_target="tpu_custom_call" | custom-call | flops 1073741824 | bytes 4194304 | tf_op jit(solution)/shard_map/pallas_call | solution.py:38
  (24 shorter events, 0.1 us)
Async XLA Ops:
  0.6 0.7 copy-start.2
  1.3 1.2 copy-start.4
  2.5 13.8 %copy-start.3 = (s32[128,8]{0,1:T(8,128)S(1)}, s32[128,8]{0,1:T(8,128)}, u32[]{:S(2)}) copy-start(s32[128,8]{0,1:T(8,128)} %param.14) | copy-start | bytes 12292
  2.5 14.0 %copy-start.5 = (bf16[2048,256]{1,0:T(8,128)(2,1)S(1)}, bf16[2048,256]{1,0:T(8,128)(2,1)}, u32[]{:S(2)}) copy-start(bf16[2048,256]{1,0:T(8,128)(2,1)} %cot_ref.5) | copy-start | bytes 3145732
  4.8 25.5 %all-to-all-start = ((bf16[128,8,256]{2,1,0:T(8,128)(2,1)}), bf16[128,8,256]{2,1,0:T(8,128)(2,1)S(1)}, u32[]{:S(2)}, u32[]{:S(2)}) async-start(bf16[128,8,256]{2,1,0:T(8,128)(2,1)} %bitcast.1), calls=%async_computation | async-start | bytes 1048576 | tf_op jit(solution)/shard_map/all_to_all | solution.py:340
  16.3 1.5 copy-start.14
  16.4 1.5 copy-start.15
  30.3 0.9 copy-start.13
  42.7 18.0 %all-to-all-start.1 = ((bf16[128,8,256]{2,1,0:T(8,128)(2,1)}), bf16[128,8,256]{2,1,0:T(8,128)(2,1)S(1)}, u32[]{:S(2)}, u32[]{:S(2)}) async-start(bf16[128,8,256]{2,1,0:T(8,128)(2,1)} %bitcast.23), calls=%async_computation.1 | async-start | bytes 1048576 | tf_op jit(solution)/shard_map/all_to_all | solution.py:340
  46.8 13.9 %copy-start = (bf16[256,256]{1,0:T(8,128)(2,1)S(1)}, bf16[256,256]{1,0:T(8,128)(2,1)}, u32[]{:S(2)}) copy-start(bf16[256,256]{1,0:T(8,128)(2,1)} %w_ref.3) | copy-start | bytes 393220
  60.7 25.6 %copy-start.1 = (s32[8,512]{1,0:T(8,128)S(1)}, s32[8,512]{1,0:T(8,128)}, u32[]{:S(2)}) copy-start(s32[8,512]{1,0:T(8,128)} %bitcast_select_fusion.row_ref) | copy-start | bytes 49156
  60.7 25.6 %copy-start.6 = (bf16[256,768]{1,0:T(8,128)(2,1)S(1)}, bf16[256,768]{1,0:T(8,128)(2,1)}, u32[]{:S(2)}) copy-start(bf16[256,768]{1,0:T(8,128)(2,1)} %ws_ref.5) | copy-start | bytes 1179652
  60.7 25.6 %copy-start.9 = (bf16[512,256]{1,0:T(8,128)(2,1)S(1)}, bf16[512,256]{1,0:T(8,128)(2,1)}, u32[]{:S(2)}) copy-start(bf16[512,256]{1,0:T(8,128)(2,1)} %cot_ref.4) | copy-start | bytes 786436
  64.1 22.2 %copy-start.7 = (bf16[256,768]{1,0:T(8,128)(2,1)S(1)}, bf16[256,768]{1,0:T(8,128)(2,1)}, u32[]{:S(2)}) copy-start(bf16[256,768]{1,0:T(8,128)(2,1)} %wi_ref.7) | copy-start | bytes 1179652
  64.1 22.2 %all-to-all-start.2 = ((bf16[128,8,256]{2,1,0:T(8,128)(2,1)}), bf16[128,8,256]{2,1,0:T(8,128)(2,1)S(1)}, u32[]{:S(2)}, u32[]{:S(2)}) async-start(bf16[128,8,256]{2,1,0:T(8,128)(2,1)} %bitcast.7), calls=%async_computation.2 | async-start | bytes 1048576 | tf_op jit(solution)/shard_map/all_to_all | solution.py:340
  76.4 0.7 copy-start.10
  86.3 1.0 copy-start.11
  100.2 4.0 %copy-start.8 = (bf16[256,768]{1,0:T(8,128)(2,1)S(1)}, bf16[256,768]{1,0:T(8,128)(2,1)}, u32[]{:S(2)}) copy-start(bf16[256,768]{1,0:T(8,128)(2,1)} %wi_ref.7) | copy-start | bytes 1179652
  100.2 23.7 %all-to-all-start.3 = ((bf16[128,8,512]{2,1,0:T(8,128)(2,1)}), bf16[128,8,512]{2,1,0:T(8,128)(2,1)S(1)}, u32[]{:S(2)}, u32[]{:S(2)}) async-start(bf16[128,8,512]{2,1,0:T(8,128)(2,1)} %bitcast.21), calls=%async_computation.3 | async-start | bytes 2097152 | tf_op jit(solution)/shard_map/all_to_all | solution.py:340
  104.2 2.8 %copy-start.12 = (bf16[8,512,768]{2,1,0:T(8,128)(2,1)S(1)}, bf16[8,512,768]{2,1,0:T(8,128)(2,1)}, u32[]{:S(2)}) copy-start(bf16[8,512,768]{2,1,0:T(8,128)(2,1)} %get-tuple-element.66.da_ref) | copy-start | bytes 18874372

commit v5 on v4

--- a/solution.py
+++ b/solution.py
@@ -6,14 +6,17 @@
 from jax import lax
 from jax.experimental import pallas as pl
 from jax.experimental.pallas import tpu as pltpu
+from jax.sharding import Mesh
 from jax.sharding import PartitionSpec as P
 
 F32 = jnp.float32
 BF16 = jnp.bfloat16
-AXES = ("outer", "sw")
+AXES = ("group", "core", "sw")
+CHIPS = ("group", "sw")
 MIB = 1024 * 1024
 VMEM = pl.BlockSpec(memory_space=pltpu.VMEM)
 ANY = pl.BlockSpec(memory_space=pl.ANY)
+SMEM = pl.BlockSpec(memory_space=pltpu.SMEM)
 
 
 def mm(a, b):
@@ -216,10 +219,10 @@
 
 
 def backward_kernel(
-    table_ref, row_ref, cot_ref, wi_ref, ws_ref, agg_grad_ref,
+    core_ref, table_ref, row_ref, cot_ref, wi_ref, ws_ref, agg_grad_ref,
     fr_ref, fu_ref, fn_ref, fm_ref, fc_ref, xs_ref, cb_ref,
-    grad_ref, da_ref, grads_ref,
-    table_s, f_s, fc_s, x_s, c_s, m_s, da_s, db_s, gi_s, gs_s, sem, da_sem, table_sem,
+    grad_ref, da_ref, mine_ref, other_ref,
+    table_s, f_s, fc_s, x_s, c_s, m_s, da_s, db_s, gi_s, gs_s, grads_s, sem, da_sem, table_sem,
 ):
     _, hops, paths, width = f_s.shape
     slots = table_ref.shape[0]
@@ -271,14 +274,21 @@
     gi_s[...] = t_mm(flat(x_s), flat(da_s))
     gs_s[...] = t_mm(flat(c_s), flat(db_s))
     two = 2 * width
-    grads_ref[:width, :] = gi_s[:, :two].astype(BF16)
-    grads_ref[width:two, :] = gs_s[:, :two].astype(BF16)
-    grads_ref[two : 3 * width, :width] = gi_s[:, two:].astype(BF16)
-    grads_ref[two : 3 * width, width:] = gs_s[:, two:].astype(BF16)
-    grads_ref[3 * width :, :width] = agg_grad_ref[...].astype(BF16)
-    grads_ref[3 * width :, width:] = jnp.zeros_like(agg_grad_ref).astype(BF16)
+    grads_s[:width, :] = gi_s[:, :two]
+    grads_s[width:two, :] = gs_s[:, :two]
+    grads_s[two : 3 * width, :width] = gi_s[:, two:]
+    grads_s[two : 3 * width, width:] = gs_s[:, two:]
+    grads_s[3 * width :, :width] = agg_grad_ref[...]
+    grads_s[3 * width :, width:] = jnp.zeros_like(agg_grad_ref)
+    core = core_ref[0]
+    mine_ref[...] = grads_s[half_of(core, two), :]
+    other_ref[...] = grads_s[half_of(1 - core, two), :].astype(BF16)
     for t in order:
         save(t).wait()
+
+
+def half_of(core, lines):
+    return pl.ds(pl.multiple_of(core * lines, lines), lines)
 
 
 def flat(ref):
@@ -286,31 +296,35 @@
     return ref[...].reshape(hops * paths, width)
 
 
-def input_kernel(da_ref, row_ref, wi_ref, sums_ref, dx_s):
+def input_kernel(groups, core_ref, da_ref, row_ref, wi_ref, mine_ref, other_ref, dx_s, sums_s):
     hops, paths, _ = da_ref.shape
     for t in range(hops):
         dx_s[t * paths : (t + 1) * paths, :] = mm_t(da_ref[t], wi_ref[...]).astype(BF16)
-    add_up(row_ref, dx_s, sums_ref)
-
-
-def share_kernel(devices, parts_ref, sums_ref, out_ref):
-    slots, wide = parts_ref.shape
-    width = sums_ref.shape[1]
-    lines = slots // devices
-    total = jnp.sum(parts_ref[...].reshape(devices // 2, 2 * lines, wide).astype(F32), axis=0)
+    add_up(row_ref, dx_s, sums_s)
+    run = mine_ref.shape[0] // groups
+    core = core_ref[0]
+    for g in range(groups):
+        at = slice(g * run, (g + 1) * run)
+        mine_ref[at, :] = sums_s[pl.ds(pl.multiple_of((2 * g + core) * run, run), run), :]
+        other_ref[at, :] = sums_s[pl.ds(pl.multiple_of((2 * g + 1 - core) * run, run), run), :]
+
+
+def share_kernel(chips, parts_ref, mine_ref, pair_ref, out_ref):
+    rows, wide = parts_ref.shape
+    width = mine_ref.shape[1]
+    lines = rows // chips
+    total = jnp.sum(parts_ref[...].reshape(chips // 2, 2 * lines, wide).astype(F32), axis=0)
     total = total[:lines] + total[lines:]
-    pair = jnp.concatenate([total, total], axis=0).astype(BF16)
-    out_ref[:, :width] = sums_ref[...]
-    out_ref[:, width:] = jnp.broadcast_to(pair[None], (devices // 2, 2 * lines, wide)).reshape(slots, wide)
-
-
-def final_kernel(
-    path_scale, link_scale, got_ref, row_ref, cot_ref,
-    link_ref, gi_ref, gs_ref, ga_ref, got_s, out_s, sem, out_sem,
-):
-    width = ga_ref.shape[0]
-    links = cot_ref.shape[0]
-    two = 2 * width
+    both = jnp.concatenate([total, total], axis=0).astype(BF16)
+    out_ref[:, :width] = mine_ref[...]
+    out_ref[:, width : 2 * width] = pair_ref[...]
+    out_ref[:, 2 * width :] = jnp.broadcast_to(
+        both[None], (chips // 2, 2 * lines, wide)
+    ).reshape(rows, wide)
+
+
+def link_out_kernel(got_ref, mine_ref, pair_ref, cot_ref, link_ref, got_s, out_s, sem, out_sem):
+    links, width = cot_ref.shape
     tile = 512
     arrival = pltpu.make_async_copy(got_ref, got_s, sem)
     arrival.start()
@@ -322,22 +336,37 @@
 
     for k in range(links // tile):
         at = slice(k * tile, (k + 1) * tile)
-        total = mm(hot_cols(row_ref[...], k * tile, tile), got_s[:, :width])
+        total = mm(hot_cols(mine_ref[...], k * tile, tile), got_s[:, :width])
+        total += mm(hot_cols(pair_ref[...], k * tile, tile), got_s[:, width : 2 * width])
         out_s[at, :] = cot_ref[at, :].astype(F32) + total
         save(k).start()
-    gi_ref[:, :two] = got_s[:width, width:].astype(F32) * path_scale
-    gs_ref[:, :two] = got_s[width:two, width:].astype(F32) * path_scale
-    gi_ref[:, two:] = got_s[two : 3 * width, width:two].astype(F32) * path_scale
-    gs_ref[:, two:] = got_s[two : 3 * width, two:].astype(F32) * path_scale
-    ga_ref[...] = got_s[3 * width :, width:two].astype(F32) * link_scale
     for k in range(links // tile):
         save(k).wait()
 
 
-def exchange(rows, devices):
+def grads_kernel(
+    path_scale, link_scale, core_ref, mine_ref, other_ref, gi_ref, gs_ref, ga_ref, all_s,
+):
+    width = ga_ref.shape[0]
+    two = 2 * width
+    core = core_ref[0]
+    all_s[half_of(core, two), :] = mine_ref[...].astype(F32)
+    all_s[half_of(1 - core, two), :] = other_ref[...].astype(F32)
+    gi_ref[:, :two] = all_s[:width, :] * path_scale
+    gs_ref[:, :two] = all_s[width:two, :] * path_scale
+    gi_ref[:, two:] = all_s[two : 3 * width, :width] * path_scale
+    gs_ref[:, two:] = all_s[two : 3 * width, width:] * path_scale
+    ga_ref[...] = all_s[3 * width :, :width] * link_scale
+
+
+def to_pair(rows):
+    return lax.ppermute(rows, "core", [(0, 1), (1, 0)])
+
+
+def exchange(rows, devices, axes=AXES):
     lines, width = rows.shape
     chunks = rows.reshape(devices, lines // devices, width)
-    got = lax.all_to_all(chunks, AXES, split_axis=0, concat_axis=0, tiled=True)
+    got = lax.all_to_all(chunks, axes, split_axis=0, concat_axis=0, tiled=True)
     return got.reshape(lines, width)
 
 
@@ -345,7 +374,11 @@
     path_state, link_state, hop_slot, hop_count, send_rows,
     w_input, w_state, w_agg, path_cot, link_cot,
 ):
-    devices = lax.axis_size("outer") * lax.axis_size("sw")
+    groups = lax.axis_size("group")
+    chips = groups * lax.axis_size("sw")
+    devices = 2 * chips
+    core = lax.axis_index("core")
+    core_at = core.astype(jnp.int32).reshape(1)
     paths, width = path_state.shape
     hops = hop_slot.shape[1]
     links = link_state.shape[0]
@@ -428,12 +461,13 @@
     )
     back_table, agg_grad = lax.optimization_barrier((back_table, agg_grad))
 
-    grad_path, da, grads = call(
+    grad_path, da, mine, other = call(
         backward_kernel,
         (
             shape((paths, width), F32),
             shape((hops, paths, gate_cols), BF16),
-            shape((4 * width, 2 * width), BF16),
+            shape((2 * width, 2 * width), F32),
+            shape((2 * width, 2 * width), BF16),
         ),
         [
             pltpu.VMEM((slots, width), BF16),
@@ -446,53 +480,73 @@
             pltpu.VMEM((hops, paths, gate_cols), BF16),
             pltpu.VMEM((width, gate_cols), F32),
             pltpu.VMEM((width, gate_cols), F32),
+            pltpu.VMEM((4 * width, 2 * width), F32),
             pltpu.SemaphoreType.DMA((7, hops)),
             pltpu.SemaphoreType.DMA((hops,)),
             pltpu.SemaphoreType.DMA,
         ],
         (10 * hops * paths * width * gate_cols, 32 * hops * paths * width, 52),
-        back_table, slot_row, path_cot, w_input, w_state, agg_grad,
+        core_at, back_table, slot_row, path_cot, w_input, w_state, agg_grad,
         *factors[:5], xs, factors[5],
-        in_specs=[ANY] + [VMEM] * 5 + [ANY] * 7,
-        out_specs=(VMEM, ANY, VMEM),
-    )
-    parts = exchange(grads, devices)
-    input_sums = call(
-        input_kernel, slot_rows, [pltpu.VMEM((hops * paths, width), BF16)],
+        in_specs=[SMEM, ANY] + [VMEM] * 5 + [ANY] * 7,
+        out_specs=(VMEM, ANY, VMEM, VMEM),
+    )
+    added = (mine + to_pair(other).astype(F32)).astype(BF16)
+    parts = exchange(added, chips, CHIPS)
+    half = shape((slots // 2, width), BF16)
+    my_sums, pair_sums = call(
+        functools.partial(input_kernel, groups), (half, half),
+        [pltpu.VMEM((hops * paths, width), BF16), pltpu.VMEM((slots, width), BF16)],
         (2 * hops * paths * (gate_cols + slots) * width, 2 * hops * paths * gate_cols, 24),
-        da, slot_row, w_input,
-    )
-    parts, input_sums = lax.optimization_barrier((parts, input_sums))
+        core_at, da, slot_row, w_input,
+        in_specs=[SMEM] + [VMEM] * 3,
+    )
+    got_sums = to_pair(pair_sums)
+    lists = send_rows.reshape(groups, 2, slots // (2 * groups))
+    my_list = lax.dynamic_index_in_dim(lists, core, 1, keepdims=False).reshape(1, slots // 2)
+    pair_list = lax.dynamic_index_in_dim(lists, 1 - core, 1, keepdims=False).reshape(1, slots // 2)
+    parts, my_sums, got_sums, my_list, pair_list = lax.optimization_barrier(
+        (parts, my_sums, got_sums, my_list, pair_list)
+    )
     last = call(
-        functools.partial(share_kernel, devices), shape((slots, 3 * width), BF16), [],
-        (slots * width, 10 * slots * width, 16), parts, input_sums,
-    )
-    got = exchange(last, devices)
-    wide = shape((width, gate_cols), F32)
-    grad_link, input_grad, state_grad, agg_total = call(
-        functools.partial(
-            final_kernel, 1.0 / math.sqrt(paths * devices), 1.0 / math.sqrt(links * devices)
-        ),
-        (shape((links, width), F32), wide, wide, shape((width, width), F32)),
+        functools.partial(share_kernel, chips), shape((slots // 2, 4 * width), BF16), [],
+        (slots * width, 10 * slots * width, 16), parts, my_sums, got_sums,
+    )
+    got = exchange(last, chips, CHIPS)
+    my_half = got[:, 2 * width :]
+    other_half = to_pair(my_half)
+    grad_link = call(
+        link_out_kernel, shape((links, width), F32),
         [
-            pltpu.VMEM((slots, 3 * width), BF16),
+            pltpu.VMEM((slots // 2, 4 * width), BF16),
             pltpu.VMEM((links, width), F32),
             pltpu.SemaphoreType.DMA,
             pltpu.SemaphoreType.DMA((links // 512,)),
         ],
         (2 * slots * links * width, 8 * links * width, 16),
-        got, send_row, link_cot,
-        in_specs=[ANY, VMEM, VMEM],
-        out_specs=(ANY, VMEM, VMEM, VMEM),
+        got, my_list, pair_list, link_cot,
+        in_specs=[ANY] + [VMEM] * 3,
+        out_specs=ANY,
+    )
+    wide = shape((width, gate_cols), F32)
+    input_grad, state_grad, agg_total = call(
+        functools.partial(
+            grads_kernel, 1.0 / math.sqrt(paths * devices), 1.0 / math.sqrt(links * devices)
+        ),
+        (wide, wide, shape((width, width), F32)), [pltpu.VMEM((4 * width, 2 * width), F32)],
+        (8 * width * width, 40 * width * width, 16), core_at, my_half, other_half,
+        in_specs=[SMEM, VMEM, VMEM],
     )
     return grad_path, grad_link, input_grad, state_grad, agg_total
 
 
 def solution(mesh):
+    outer, sw = mesh.devices.shape
+    by_core = Mesh(mesh.devices.reshape(outer // 2, 2, sw), AXES)
     split = P(AXES, None)
     return jax.shard_map(
         per_device,
-        mesh=mesh,
+        mesh=by_core,
         in_specs=(split, split, split, P(AXES), split, P(), P(), P(), split, split),
         out_specs=(split, split, P(), P(), P()),
         check_vma=False,

time: 158 us -> 157 us (level)
  waiting for transfers between devices: 35.7 us -> 29.1 us
  blocking collectives: 28.7 us -> 23.6 us
  starting transfers between devices: 27.5 us -> 31.6 us
  Pallas kernels: 55.7 us -> 59.8 us
  other arithmetic: 0.61 us -> 2.79 us
    all_to_all x4, waiting for transfers between devices: 35.7 us -> 26.7 us  [exchange(): got = lax.all_to_all(chunks, axes, split_axis=0, concat_axis=0, tiled=True)]
    all_to_all x1, blocking collectives: 28.7 us -> 23.6 us  [exchange(): got = lax.all_to_all(chunks, axes, split_axis=0, concat_axis=0, tiled=True)]
    pallas_call x9 -> x10, Pallas kernels: 43.6 us -> 47.7 us  [call(): pl.pallas_call(kernel, out_shape=outs, in_specs=in_specs or [VMEM] * len(...]
    ppermute x0 -> x3, starting transfers between devices: none -> 2.77 us  [to_pair(): return lax.ppermute(rows, 'core', [(0, 1), (1, 0)])]
    ppermute x0 -> x3, waiting for transfers between devices: none -> 2.39 us  [to_pair(): return lax.ppermute(rows, 'core', [(0, 1), (1, 0)])]
    reshape x0 -> x1, other arithmetic: none -> 2.18 us  [exchange(): chunks = rows.reshape(devices, lines // devices, width)]
  transfers between devices with their start and end apart: 4 -> 7, of which waited for: 4 -> 6; matrix products, arithmetic and copies ran while one was open for 1% -> 1% of each run, Pallas kernels for 14% -> 15%
where the time goes in v5:
time: 157 us; the launch traced here: 156 us
  Pallas kernels  59.8 us (38%)
  starting transfers between devices  31.6 us (20%)
  waiting for transfers between devices  29.1 us (19%)
  blocking collectives  23.6 us (15%)
  local copies, waits for them, and re-layouts  8.01 us (5%)
  other arithmetic  2.79 us (2%)
    pallas_call x10, Pallas kernels, call(): pl.pallas_call(kernel, out_shape=outs, in_specs=in_specs or [VMEM] * len(...  47.7 us
    all_to_all x4, starting transfers between devices, exchange(): got = lax.all_to_all(chunks, axes, split_axis=0, concat_axis=0, tiled=True)  28.8 us
    all_to_all x4, waiting for transfers between devices, exchange(): got = lax.all_to_all(chunks, axes, split_axis=0, concat_axis=0, tiled=True)  26.7 us
    all_to_all x1, blocking collectives, exchange(): got = lax.all_to_all(chunks, axes, split_axis=0, concat_axis=0, tiled=True)  23.6 us
    pallas_call x1, Pallas kernels, per_device(): pl.pallas_call(factors_kernel, grid=(hops,), out_shape=(short,) * 4 + (fa...  12.1 us
    unnamed x33, local copies, waits for them, and re-layouts  6.48 us
  transfers between devices with their start and end apart: 7, of which 6 were waited for; matrix products, arithmetic and copies ran while one was open for 1% of the time, Pallas kernels for 15%

profile of v5, /device:TPU:1, one launch (start us, length us, event | category | flops | bytes accessed | tf_op | source)
XLA Modules:
  0.0 155.8 jit_solution(10658791732693423816)
XLA Ops:
  0.6 0.7 copy-done.3
  1.3 1.2 copy-done.5
  2.5 2.3 %shard_map.137 = (bf16[1024,256]{1,0:T(8,128)(2,1)}, s32[1,1024]{1,0:T(1,128)S(1)}) custom-call(s32[8,128]{1,0:T(8,128)S(1)} %bitcast.22, bf16[2048,256]{1,0:T(8,128)(2,1)S(1)} %copy-done.5), custom_call_target="tpu_custom_call" | custom-call | flops 1073741824 | bytes 1048576 | tf_op jit(solution)/shard_map/pallas_call | solution.py:41
  4.8 11.5 %all-to-all-start = ((bf16[128,8,256]{2,1,0:T(8,128)(2,1)}), bf16[128,8,256]{2,1,0:T(8,128)(2,1)S(1)}, u32[]{:S(2)}, u32[]{:S(2)}) async-start(bf16[128,8,256]{2,1,0:T(8,128)(2,1)} %bitcast.2), calls=%async_computation | async-start | bytes 1048576 | tf_op jit(solution)/shard_map/all_to_all | solution.py:369
  16.6 1.3 shard_map.138.cot_ref
  17.9 0.6 bitcast_select_fusion.row_ref
  18.5 11.8 %all-to-all-done = bf16[128,8,256]{2,1,0:T(8,128)(2,1)S(1)} async-done(((bf16[128,8,256]{2,1,0:T(8,128)(2,1)}), bf16[128,8,256]{2,1,0:T(8,128)(2,1)S(1)}, u32[]{:S(2)}, u32[]{:S(2)}) %all-to-all-start) | async-done | bytes 524320 | tf_op jit(solution)/shard_map/all_to_all | solution.py:369
  30.3 0.9 copy.17.count_ref
  31.2 11.5 %shard_map.139 = (bf16[1024,256]{1,0:T(8,128)(2,1)}, bf16[8,512,256]{2,1,0:T(8,128)(2,1)}, f32[8,512,256]{2,1,0:T(8,128)}) custom-call(bf16[1024,256]{1,0:T(8,128)(2,1)} %bitcast.23, s32[512,1]{1,0:T(8,128)} %copy.17.count_ref, s32[8,512]{1,0:T(8,128)} %bitcast_select_fusion.row_ref, bf16[512,256]{1,0:T(8,128)(2,1)} %start_ref.1, bf16[256,768]{1,0:T(8,128)(2,1)} %wi_ref.7, ...), custom_call_target="tpu_custom_call" | custom-call | flops 4294967296 | bytes 8388608 | tf_op jit(solution)/shard_map/pallas_call | solution.py:41
  42.7 3.8 %all-to-all-start.1 = ((bf16[128,8,256]{2,1,0:T(8,128)(2,1)}), bf16[128,8,256]{2,1,0:T(8,128)(2,1)S(1)}, u32[]{:S(2)}, u32[]{:S(2)}) async-start(bf16[128,8,256]{2,1,0:T(8,128)(2,1)} %bitcast.24), calls=%async_computation.1 | async-start | bytes 1048576 | tf_op jit(solution)/shard_map/all_to_all | solution.py:369
  46.8 12.1 %shard_map.140 = (bf16[8,512,256]{2,1,0:T(8,128)(2,1)}, bf16[8,512,256]{2,1,0:T(8,128)(2,1)}, bf16[8,512,256]{2,1,0:T(8,128)(2,1)}, bf16[8,512,256]{2,1,0:T(8,12...) custom-call(bf16[8,512,256]{2,1,0:T(8,128)(2,1)} %get-tuple-element.50.xs_ref, ...), custom_call_target="tpu_custom_call" | custom-call | flops 3221225472 | bytes 33554432 | tf_op jit(solution)/shard_map/pallas_call | solution.py:432
  58.9 1.8 %all-to-all-done.1 = bf16[128,8,256]{2,1,0:T(8,128)(2,1)S(1)} async-done(((bf16[128,8,256]{2,1,0:T(8,128)(2,1)}), bf16[128,8,256]{2,1,0:T(8,128)(2,1)S(1)}, u32[]{:S(2)}, u32[]{:S(2)}) %all-to-all-start.1) | async-done | bytes 524320 | tf_op jit(solution)/shard_map/all_to_all | solution.py:369
  60.7 3.4 %shard_map.141 = bf16[1024,256]{1,0:T(8,128)(2,1)} custom-call(bf16[1024,256]{1,0:T(8,128)(2,1)S(1)} %bitcast.19, s32[1,1024]{1,0:T(1,128)S(1)} %get-tuple-element.45.row_ref, s32[1024,1]{1,0:T(8,128)S(1)} %copy.19.col_ref, bf16[256,256]{1,0:T(8,128)(2,1)S(1)} %copy-done.1, bf16[1024,256]{1,0:T(8,128)(2,1)S(1)} %shard_map.138.cot_ref), custom_call_target="tpu_custom_call" | custom-call | flops 536870912 | bytes 2097152 | tf_op jit(solution)/shard_map/pallas_call | solution.py:41
  64.1 8.6 %all-to-all-start.2 = ((bf16[128,8,256]{2,1,0:T(8,128)(2,1)}), bf16[128,8,256]{2,1,0:T(8,128)(2,1)}, u32[]{:S(2)}, u32[]{:S(2)}) async-start(bf16[128,8,256]{2,1,0:T(8,128)(2,1)} %bitcast.8), calls=%async_computation.2 | async-start | bytes 1048576 | tf_op jit(solution)/shard_map/all_to_all | solution.py:369
  72.8 4.1 %shard_map.142.agg_grad_ref = f32[256,256]{1,0:T(8,128)S(1)} custom-call(bf16[1024,256]{1,0:T(8,128)(2,1)S(1)} %bitcast.20, s32[1,1024]{1,0:T(1,128)S(1)} %get-tuple-element.45.row_ref, bf16[256,256]{1,0:T(8,128)(2,1)S(1)} %copy-done.1, bf16[2048,256]{1,0:T(8,128)(2,1)S(1)} %copy-done), custom_call_target="tpu_custom_call" | custom-call | flops 536870912 | bytes 3145728 | tf_op jit(solution)/shard_map/pallas_call | solution.py:41
  76.8 0.7 copy-done.10
  77.5 8.8 %all-to-all-done.2 = bf16[128,8,256]{2,1,0:T(8,128)(2,1)} async-done(((bf16[128,8,256]{2,1,0:T(8,128)(2,1)}), bf16[128,8,256]{2,1,0:T(8,128)(2,1)}, u32[]{:S(2)}, u32[]{:S(2)}) %all-to-all-start.2) | async-done | bytes 524320 | tf_op jit(solution)/shard_map/all_to_all | solution.py:369
  86.4 0.9 copy-done.11
  87.3 17.1 %shard_map.143 = (f32[512,256]{1,0:T(8,128)}, bf16[8,512,768]{2,1,0:T(8,128)(2,1)}, f32[512,512]{1,0:T(8,128)}, bf16[512,512]{1,0:T(8,128)(2,1)S(1)}) custom-call(s32[1]{0:T(128)} %bitcast.core_ref, bf16[1024,256]{1,0:T(8,128)(2,1)} %bitcast.9.table_ref, s32[8,512]{1,0:T(8,128)S(1)} %copy-done.2, bf16[512,256]{1,0:T(8,128)(2,1)S(1)} %copy-done.9, ...), custom_call_target="tpu_custom_call" | custom-call | flops 8053063680 | bytes 33554432 | tf_op jit(solution)/shard_map/pallas_call | solution.py:41
  104.4 0.5 collective-permute-start
  104.9 1.5 collective-permute-done
  106.4 2.2 %fusion = bf16[64,8,512]{2,1,0:T(8,128)(2,1)} fusion(f32[512,512]{1,0:T(8,128)} %get-tuple-element.70, bf16[512,512]{1,0:T(8,128)(2,1)S(1)} %collective-permute-done), kind=kLoop, calls=%fused_computation.1 | loop fusion | flops 786432 | bytes 2097152 | tf_op jit(solution)/shard_map/reshape | solution.py:368
  108.6 4.9 %all-to-all-start.3 = ((bf16[64,8,512]{2,1,0:T(8,128)(2,1)}), bf16[64,8,512]{2,1,0:T(8,128)(2,1)S(1)}, u32[]{:S(2)}, u32[]{:S(2)}) async-start(bf16[64,8,512]{2,1,0:T(8,128)(2,1)} %fusion), calls=%async_computation.3 | async-start | bytes 1048576 | tf_op jit(solution)/shard_map/all_to_all | solution.py:369
  113.5 2.8 %copy-done.12 = bf16[8,512,768]{2,1,0:T(8,128)(2,1)S(1)} copy-done((bf16[8,512,768]{2,1,0:T(8,128)(2,1)S(1)}, bf16[8,512,768]{2,1,0:T(8,128)(2,1)}, u32[]{:S(2)}) %copy-start.12) | copy-done | bytes 6291480
  116.3 4.0 %shard_map.144 = (bf16[512,256]{1,0:T(8,128)(2,1)S(1)}, bf16[512,256]{1,0:T(8,128)(2,1)S(1)}) custom-call(s32[1]{0:T(128)} %bitcast.core_ref, bf16[8,512,768]{2,1,0:T(8,128)(2,1)S(1)} %copy-done.12, s32[8,512]{1,0:T(8,128)S(1)} %copy-done.2, bf16[256,768]{1,0:T(8,128)(2,1)S(1)} %copy-done.8), custom_call_target="tpu_custom_call" | custom-call | flops 3758096384 | bytes 6291456 | tf_op jit(solution)/shard_map/pallas_call | solution.py:41
  120.3 0.5 collective-permute-start.1
  121.1 0.8 collective-permute-done.1.pair_ref
  121.9 4.3 %all-to-all-done.3 = bf16[64,8,512]{2,1,0:T(8,128)(2,1)S(1)} async-done(((bf16[64,8,512]{2,1,0:T(8,128)(2,1)}), bf16[64,8,512]{2,1,0:T(8,128)(2,1)S(1)}, u32[]{:S(2)}, u32[]{:S(2)}) %all-to-all-start.3) | async-done | bytes 524320 | tf_op jit(solution)/shard_map/all_to_all | solution.py:369
  126.4 23.6 %all_to_all.25 = bf16[64,8,1024]{2,1,0:T(8,128)(2,1)S(1)} all-to-all(bf16[64,8,1024]{2,1,0:T(8,128)(2,1)S(1)} %bitcast.18), channel_id=1, replica_groups=mesh['group'=16,'core'=2,'sw'=4] {'group','sw'}, dimensions={0} | all-to-all | bytes 2097152 | tf_op jit(solution)/shard_map/all_to_all | solution.py:369
  150.1 1.8 %collective-permute-start.2 = (bf16[512,512]{1,0:T(8,128)(2,1)S(1)}, bf16[512,512]{1,0:T(8,128)(2,1)S(1)}, u32[]{:S(2)}, u32[]{:S(2)}) collective-permute-start(bf16[512,512]{1,0:T(8,128)(2,1)S(1)} %slice.4.mine_ref), channel_id=1, source_target_pairs={{0,4},{4,0},{1,5},{5,1},{2,6},{6,2},{3,7},{7,3},{8,12},{12,8},{9,1... | collective-permute-start | bytes 1572872 | tf_op jit(solution)/shard_map/ppermute | solution.py:363
  151.9 2.4 %shard_map.146 = f32[2048,256]{1,0:T(8,128)} custom-call(bf16[512,1024]{1,0:T(8,128)(2,1)S(1)} %bitcast.17, s32[1,512]{1,0:T(1,128)S(1)} %reshape.69.mine_ref, s32[1,512]{1,0:T(1,128)S(1)} %reshape.70.pair_ref, bf16[2048,256]{1,0:T(8,128)(2,1)S(1)} %copy-done), custom_call_target="tpu_custom_call" | custom-call | flops 1073741824 | bytes 4194304 | tf_op jit(solution)/shard_map/pallas_call | solution.py:41
  154.4 1.4 shard_map.147
  (37 shorter events, 1.0 us)
Async XLA Ops:
  0.6 0.7 copy-start.3
  1.3 1.2 copy-start.5
  2.5 13.8 %copy-start.4 = (s32[128,8]{0,1:T(8,128)S(1)}, s32[128,8]{0,1:T(8,128)}, u32[]{:S(2)}) copy-start(s32[128,8]{0,1:T(8,128)} %param.14) | copy-start | bytes 12292
  2.5 14.0 %copy-start = (bf16[2048,256]{1,0:T(8,128)(2,1)S(1)}, bf16[2048,256]{1,0:T(8,128)(2,1)}, u32[]{:S(2)}) copy-start(bf16[2048,256]{1,0:T(8,128)(2,1)} %cot_ref.5) | copy-start | bytes 3145732
  4.8 25.5 %all-to-all-start = ((bf16[128,8,256]{2,1,0:T(8,128)(2,1)}), bf16[128,8,256]{2,1,0:T(8,128)(2,1)S(1)}, u32[]{:S(2)}, u32[]{:S(2)}) async-start(bf16[128,8,256]{2,1,0:T(8,128)(2,1)} %bitcast.2), calls=%async_computation | async-start | bytes 1048576 | tf_op jit(solution)/shard_map/all_to_all | solution.py:369
  16.3 1.5 copy-start.14
  16.3 1.5 copy-start.15
  30.3 0.9 copy-start.13
  42.7 17.9 %all-to-all-start.1 = ((bf16[128,8,256]{2,1,0:T(8,128)(2,1)}), bf16[128,8,256]{2,1,0:T(8,128)(2,1)S(1)}, u32[]{:S(2)}, u32[]{:S(2)}) async-start(bf16[128,8,256]{2,1,0:T(8,128)(2,1)} %bitcast.24), calls=%async_computation.1 | async-start | bytes 1048576 | tf_op jit(solution)/shard_map/all_to_all | solution.py:369
  46.8 13.9 %copy-start.1 = (bf16[256,256]{1,0:T(8,128)(2,1)S(1)}, bf16[256,256]{1,0:T(8,128)(2,1)}, u32[]{:S(2)}) copy-start(bf16[256,256]{1,0:T(8,128)(2,1)} %w_ref.3) | copy-start | bytes 393220
  60.7 25.7 %copy-start.2 = (s32[8,512]{1,0:T(8,128)S(1)}, s32[8,512]{1,0:T(8,128)}, u32[]{:S(2)}) copy-start(s32[8,512]{1,0:T(8,128)} %bitcast_select_fusion.row_ref) | copy-start | bytes 49156
  60.7 25.7 %copy-start.6 = (bf16[256,768]{1,0:T(8,128)(2,1)S(1)}, bf16[256,768]{1,0:T(8,128)(2,1)}, u32[]{:S(2)}) copy-start(bf16[256,768]{1,0:T(8,128)(2,1)} %ws_ref.5) | copy-start | bytes 1179652
  60.7 25.7 %copy-start.9 = (bf16[512,256]{1,0:T(8,128)(2,1)S(1)}, bf16[512,256]{1,0:T(8,128)(2,1)}, u32[]{:S(2)}) copy-start(bf16[512,256]{1,0:T(8,128)(2,1)} %cot_ref.4) | copy-start | bytes 786436
  64.1 22.3 %copy-start.7 = (bf16[256,768]{1,0:T(8,128)(2,1)S(1)}, bf16[256,768]{1,0:T(8,128)(2,1)}, u32[]{:S(2)}) copy-start(bf16[256,768]{1,0:T(8,128)(2,1)} %wi_ref.7) | copy-start | bytes 1179652
  64.1 22.3 %all-to-all-start.2 = ((bf16[128,8,256]{2,1,0:T(8,128)(2,1)}), bf16[128,8,256]{2,1,0:T(8,128)(2,1)}, u32[]{:S(2)}, u32[]{:S(2)}) async-start(bf16[128,8,256]{2,1,0:T(8,128)(2,1)} %bitcast.8), calls=%async_computation.2 | async-start | bytes 1048576 | tf_op jit(solution)/shard_map/all_to_all | solution.py:369
  76.8 0.7 copy-start.10
  86.4 1.0 copy-start.11
  104.4 9.1 %copy-start.8 = (bf16[256,768]{1,0:T(8,128)(2,1)S(1)}, bf16[256,768]{1,0:T(8,128)(2,1)}, u32[]{:S(2)}) copy-start(bf16[256,768]{1,0:T(8,128)(2,1)} %wi_ref.7) | copy-start | bytes 1179652
  104.4 2.0 %collective-permute-start = (bf16[512,512]{1,0:T(8,128)(2,1)S(1)}, bf16[512,512]{1,0:T(8,128)(2,1)S(1)}, u32[]{:S(2)}, u32[]{:S(2)}) collective-permute-start(bf16[512,512]{1,0:T(8,128)(2,1)S(1)} %get-tuple-element.71), channel_id=1, source_target_pairs={{0,4},{4,0},{1,5},{5,1},{2,6},{6,2},{3,7},{7,3},{8,12},{12,8},{9,1... | collective-permute-start | bytes 1572872 | tf_op jit(solution)/shard_map/ppermute | solution.py:363
  108.6 17.6 %all-to-all-start.3 = ((bf16[64,8,512]{2,1,0:T(8,128)(2,1)}), bf16[64,8,512]{2,1,0:T(8,128)(2,1)S(1)}, u32[]{:S(2)}, u32[]{:S(2)}) async-start(bf16[64,8,512]{2,1,0:T(8,128)(2,1)} %fusion), calls=%async_computation.3 | async-start | bytes 1048576 | tf_op jit(solution)/shard_map/all_to_all | solution.py:369
  113.5 2.8 %copy-start.12 = (bf16[8,512,768]{2,1,0:T(8,128)(2,1)S(1)}, bf16[8,512,768]{2,1,0:T(8,128)(2,1)}, u32[]{:S(2)}) copy-start(bf16[8,512,768]{2,1,0:T(8,128)(2,1)} %get-tuple-element.72.da_ref) | copy-start | bytes 18874372
  120.3 1.6 %collective-permute-start.1 = (bf16[512,256]{1,0:T(8,128)(2,1)S(1)}, bf16[512,256]{1,0:T(8,128)(2,1)S(1)}, u32[]{:S(2)}, u32[]{:S(2)}) collective-permute-start(bf16[512,256]{1,0:T(8,128)(2,1)S(1)} %get-tuple-element.74), channel_id=1, source_target_pairs={{0,4},{4,0},{1,5},{5,1},{2,6},{6,2},{3,7},{7,3},{8,12},{12,8},{9,1... | collective-permute-start | bytes 786440 | tf_op jit(solution)/shard_map/ppermute | solution.py:363
  150.1 4.3 %collective-permute-start.2 = (bf16[512,512]{1,0:T(8,128)(2,1)S(1)}, bf16[512,512]{1,0:T(8,128)(2,1)S(1)}, u32[]{:S(2)}, u32[]{:S(2)}) collective-permute-start(bf16[512,512]{1,0:T(8,128)(2,1)S(1)} %slice.4.mine_ref), channel_id=1, source_target_pairs={{0,4},{4,0},{1,5},{5,1},{2,6},{6,2},{3,7},{7,3},{8,12},{12,8},{9,1... | collective-permute-start | bytes 1572872 | tf_op jit(solution)/shard_map/ppermute | solution.py:363

commit v6 on v5

--- a/solution.py
+++ b/solution.py
@@ -219,10 +219,10 @@
 
 
 def backward_kernel(
-    core_ref, table_ref, row_ref, cot_ref, wi_ref, ws_ref, agg_grad_ref,
+    core_ref, table_ref, row_ref, cot_ref, turned_ref, agg_grad_ref,
     fr_ref, fu_ref, fn_ref, fm_ref, fc_ref, xs_ref, cb_ref,
     grad_ref, da_ref, mine_ref, other_ref,
-    table_s, f_s, fc_s, x_s, c_s, m_s, da_s, db_s, gi_s, gs_s, grads_s, sem, da_sem, table_sem,
+    table_s, f_s, fc_s, x_s, c_s, m_s, da_s, db_s, grads_s, sem, da_sem, table_sem,
 ):
     _, hops, paths, width = f_s.shape
     slots = table_ref.shape[0]
@@ -268,21 +268,19 @@
             db_s[t, at, :width] = dr
             db_s[t, at, width : 2 * width] = du
             db_s[t, at, 2 * width :] = (d * f_s[3, t, at, :]).astype(BF16)
-            back = mm_t(db_s[t, at, :], ws_ref[...]).astype(BF16).astype(F32)
+            back = mm(db_s[t, at, :], turned_ref[...]).astype(BF16).astype(F32)
             grad_ref[at, :] = d * fc_s[t, at, :] + back
         save(t).start()
-    gi_s[...] = t_mm(flat(x_s), flat(da_s))
-    gs_s[...] = t_mm(flat(c_s), flat(db_s))
     two = 2 * width
-    grads_s[:width, :] = gi_s[:, :two]
-    grads_s[width:two, :] = gs_s[:, :two]
-    grads_s[two : 3 * width, :width] = gi_s[:, two:]
-    grads_s[two : 3 * width, width:] = gs_s[:, two:]
-    grads_s[3 * width :, :width] = agg_grad_ref[...]
-    grads_s[3 * width :, width:] = jnp.zeros_like(agg_grad_ref)
+    for k, (left, right) in enumerate(((x_s, da_s), (c_s, db_s))):
+        grad = t_mm(flat(left), flat(right)).astype(BF16)
+        grads_s[k * width : (k + 1) * width, :] = grad[:, :two]
+        grads_s[two : 3 * width, k * width : (k + 1) * width] = grad[:, two:]
+    grads_s[3 * width :, :width] = agg_grad_ref[...].astype(BF16)
+    grads_s[3 * width :, width:] = jnp.zeros_like(agg_grad_ref).astype(BF16)
     core = core_ref[0]
     mine_ref[...] = grads_s[half_of(core, two), :]
-    other_ref[...] = grads_s[half_of(1 - core, two), :].astype(BF16)
+    other_ref[...] = grads_s[half_of(1 - core, two), :]
     for t in order:
         save(t).wait()
 
@@ -296,10 +294,10 @@
     return ref[...].reshape(hops * paths, width)
 
 
-def input_kernel(groups, core_ref, da_ref, row_ref, wi_ref, mine_ref, other_ref, dx_s, sums_s):
+def input_kernel(groups, core_ref, da_ref, row_ref, turned_ref, mine_ref, other_ref, dx_s, sums_s):
     hops, paths, _ = da_ref.shape
     for t in range(hops):
-        dx_s[t * paths : (t + 1) * paths, :] = mm_t(da_ref[t], wi_ref[...]).astype(BF16)
+        dx_s[t * paths : (t + 1) * paths, :] = mm(da_ref[t], turned_ref[...]).astype(BF16)
     add_up(row_ref, dx_s, sums_s)
     run = mine_ref.shape[0] // groups
     core = core_ref[0]
@@ -307,6 +305,10 @@
         at = slice(g * run, (g + 1) * run)
         mine_ref[at, :] = sums_s[pl.ds(pl.multiple_of((2 * g + core) * run, run), run), :]
         other_ref[at, :] = sums_s[pl.ds(pl.multiple_of((2 * g + 1 - core) * run, run), run), :]
+
+
+def pair_kernel(mine_ref, other_ref, out_ref):
+    out_ref[...] = (mine_ref[...].astype(F32) + other_ref[...].astype(F32)).astype(BF16)
 
 
 def share_kernel(chips, parts_ref, mine_ref, pair_ref, out_ref):
@@ -401,8 +403,12 @@
         pick_again_kernel, slot_rows, [],
         (2 * slots * links * width, 2 * links * width, 16), send_row, link_cot,
     )
-    table, cot_rows, send_col, count, slot_row = lax.optimization_barrier(
-        (table, cot_rows, send_col, count, slot_row)
+    input_turned = w_input.T
+    state_turned = w_state.T
+    table, cot_rows, send_col, count, slot_row, input_turned, state_turned = (
+        lax.optimization_barrier(
+            (table, cot_rows, send_col, count, slot_row, input_turned, state_turned)
+        )
     )
     sums, xs, cs = call(
         forward_kernel,
@@ -457,7 +463,7 @@
     back_table = exchange(back, devices)
     agg_grad = call(
         link_grad_kernel, shape((width, width), F32), [],
-        (4 * links * width * width, 6 * links * width, 16), arrived, send_row, w_agg, link_cot,
+        (4 * links * width * width, 6 * links * width, 58), arrived, send_row, w_agg, link_cot,
     )
     back_table, agg_grad = lax.optimization_barrier((back_table, agg_grad))
 
@@ -466,7 +472,7 @@
         (
             shape((paths, width), F32),
             shape((hops, paths, gate_cols), BF16),
-            shape((2 * width, 2 * width), F32),
+            shape((2 * width, 2 * width), BF16),
             shape((2 * width, 2 * width), BF16),
         ),
         [
@@ -478,27 +484,28 @@
             pltpu.VMEM((hops, paths, width), F32),
             pltpu.VMEM((hops, paths, gate_cols), BF16),
             pltpu.VMEM((hops, paths, gate_cols), BF16),
-            pltpu.VMEM((width, gate_cols), F32),
-            pltpu.VMEM((width, gate_cols), F32),
-            pltpu.VMEM((4 * width, 2 * width), F32),
+            pltpu.VMEM((4 * width, 2 * width), BF16),
             pltpu.SemaphoreType.DMA((7, hops)),
             pltpu.SemaphoreType.DMA((hops,)),
             pltpu.SemaphoreType.DMA,
         ],
         (10 * hops * paths * width * gate_cols, 32 * hops * paths * width, 52),
-        core_at, back_table, slot_row, path_cot, w_input, w_state, agg_grad,
+        core_at, back_table, slot_row, path_cot, state_turned, agg_grad,
         *factors[:5], xs, factors[5],
-        in_specs=[SMEM, ANY] + [VMEM] * 5 + [ANY] * 7,
+        in_specs=[SMEM, ANY] + [VMEM] * 4 + [ANY] * 7,
         out_specs=(VMEM, ANY, VMEM, VMEM),
     )
-    added = (mine + to_pair(other).astype(F32)).astype(BF16)
+    added = call(
+        pair_kernel, shape((slots // 2, 2 * width), BF16), [],
+        (slots * width, 4 * slots * width, 8), mine, to_pair(other),
+    )
     parts = exchange(added, chips, CHIPS)
     half = shape((slots // 2, width), BF16)
     my_sums, pair_sums = call(
         functools.partial(input_kernel, groups), (half, half),
         [pltpu.VMEM((hops * paths, width), BF16), pltpu.VMEM((slots, width), BF16)],
         (2 * hops * paths * (gate_cols + slots) * width, 2 * hops * paths * gate_cols, 24),
-        core_at, da, slot_row, w_input,
+        core_at, da, slot_row, input_turned,
         in_specs=[SMEM] + [VMEM] * 3,
     )
     got_sums = to_pair(pair_sums)

time: 157 us -> 155 us (0.987)
  Pallas kernels: 59.8 us -> 62 us
  other arithmetic: 2.79 us -> 0.61 us
    pallas_call x10 -> x11, Pallas kernels: 47.7 us -> 49.9 us  [call(): pl.pallas_call(kernel, out_shape=outs, in_specs=in_specs or [VMEM] * len(...]
    reshape x1 -> x0, other arithmetic: 2.18 us -> none  [exchange(): chunks = rows.reshape(devices, lines // devices, width)]
    unnamed x33 -> x39, local copies, waits for them, and re-layouts: 6.48 us -> 6.93 us
  transfers between devices with their start and end apart: 7 -> 7, of which waited for: 6 -> 6; matrix products, arithmetic and copies ran while one was open for 1% -> 1% of each run, Pallas kernels for 15% -> 17%
where the time goes in v6:
time: 155 us
  Pallas kernels  62 us (40%)
  starting transfers between devices  31.1 us (20%)
  waiting for transfers between devices  27.7 us (18%)
  blocking collectives  23.7 us (15%)
  local copies, waits for them, and re-layouts  8.46 us (5%)
    pallas_call x11, Pallas kernels, call(): pl.pallas_call(kernel, out_shape=outs, in_specs=in_specs or [VMEM] * len(...  49.9 us
    all_to_all x4, starting transfers between devices, exchange(): got = lax.all_to_all(chunks, axes, split_axis=0, concat_axis=0, tiled=True)  28.4 us
    all_to_all x4, waiting for transfers between devices, exchange(): got = lax.all_to_all(chunks, axes, split_axis=0, concat_axis=0, tiled=True)  25.3 us
    all_to_all x1, blocking collectives, exchange(): got = lax.all_to_all(chunks, axes, split_axis=0, concat_axis=0, tiled=True)  23.7 us
    pallas_call x1, Pallas kernels, per_device(): pl.pallas_call(factors_kernel, grid=(hops,), out_shape=(short,) * 4 + (fa...  12.1 us
    unnamed x39, local copies, waits for them, and re-layouts  6.93 us
  transfers between devices with their start and end apart: 7, of which 6 were waited for; matrix products, arithmetic and copies ran while one was open for 1% of the time, Pallas kernels for 17%

profile of v6, /device:TPU:1, one launch (start us, length us, event | category | flops | bytes accessed | tf_op | source)
XLA Modules:
  0.0 154.6 jit_solution(11599998266753748870)
XLA Ops:
  0.6 0.7 copy-done.6
  1.3 1.2 copy-done.8
  2.6 2.3 %shard_map.137 = (bf16[1024,256]{1,0:T(8,128)(2,1)}, s32[1,1024]{1,0:T(1,128)S(1)}) custom-call(s32[8,128]{1,0:T(8,128)S(1)} %bitcast.25, bf16[2048,256]{1,0:T(8,128)(2,1)S(1)} %copy-done.8), custom_call_target="tpu_custom_call" | custom-call | flops 1073741824 | bytes 1048576 | tf_op jit(solution)/shard_map/pallas_call | solution.py:41
  4.8 11.5 %all-to-all-start = ((bf16[128,8,256]{2,1,0:T(8,128)(2,1)}), bf16[128,8,256]{2,1,0:T(8,128)(2,1)S(1)}, u32[]{:S(2)}, u32[]{:S(2)}) async-start(bf16[128,8,256]{2,1,0:T(8,128)(2,1)} %bitcast.2), calls=%async_computation | async-start | bytes 1048576 | tf_op jit(solution)/shard_map/all_to_all | solution.py:371
  16.9 1.3 shard_map.138.cot_ref
  18.3 0.6 bitcast_select_fusion.row_ref
  18.9 11.4 %all-to-all-done = bf16[128,8,256]{2,1,0:T(8,128)(2,1)S(1)} async-done(((bf16[128,8,256]{2,1,0:T(8,128)(2,1)}), bf16[128,8,256]{2,1,0:T(8,128)(2,1)S(1)}, u32[]{:S(2)}, u32[]{:S(2)}) %all-to-all-start) | async-done | bytes 524320 | tf_op jit(solution)/shard_map/all_to_all | solution.py:371
  30.3 0.9 copy.21.count_ref
  31.2 11.6 %shard_map.139 = (bf16[1024,256]{1,0:T(8,128)(2,1)}, bf16[8,512,256]{2,1,0:T(8,128)(2,1)}, f32[8,512,256]{2,1,0:T(8,128)}) custom-call(bf16[1024,256]{1,0:T(8,128)(2,1)} %bitcast.27, s32[512,1]{1,0:T(8,128)} %copy.21.count_ref, s32[8,512]{1,0:T(8,128)} %bitcast_select_fusion.row_ref, bf16[512,256]{1,0:T(8,128)(2,1)} %start_ref.1, bf16[256,768]{1,0:T(8,128)(2,1)} %wi_ref.3, ...), custom_call_target="tpu_custom_call" | custom-call | flops 4294967296 | bytes 8388608 | tf_op jit(solution)/shard_map/pallas_call | solution.py:41
  42.8 3.8 %all-to-all-start.1 = ((bf16[128,8,256]{2,1,0:T(8,128)(2,1)}), bf16[128,8,256]{2,1,0:T(8,128)(2,1)S(1)}, u32[]{:S(2)}, u32[]{:S(2)}) async-start(bf16[128,8,256]{2,1,0:T(8,128)(2,1)} %bitcast.28), calls=%async_computation.1 | async-start | bytes 1048576 | tf_op jit(solution)/shard_map/all_to_all | solution.py:371
  46.8 12.1 %shard_map.140 = (bf16[8,512,256]{2,1,0:T(8,128)(2,1)}, bf16[8,512,256]{2,1,0:T(8,128)(2,1)}, bf16[8,512,256]{2,1,0:T(8,128)(2,1)}, bf16[8,512,256]{2,1,0:T(8,12...) custom-call(bf16[8,512,256]{2,1,0:T(8,128)(2,1)} %get-tuple-element.52.xs_ref, ...), custom_call_target="tpu_custom_call" | custom-call | flops 3221225472 | bytes 33554432 | tf_op jit(solution)/shard_map/pallas_call | solution.py:438
  58.9 1.8 %all-to-all-done.1 = bf16[128,8,256]{2,1,0:T(8,128)(2,1)S(1)} async-done(((bf16[128,8,256]{2,1,0:T(8,128)(2,1)}), bf16[128,8,256]{2,1,0:T(8,128)(2,1)S(1)}, u32[]{:S(2)}, u32[]{:S(2)}) %all-to-all-start.1) | async-done | bytes 524320 | tf_op jit(solution)/shard_map/all_to_all | solution.py:371
  60.7 3.4 %shard_map.141 = bf16[1024,256]{1,0:T(8,128)(2,1)} custom-call(bf16[1024,256]{1,0:T(8,128)(2,1)S(1)} %bitcast.20, s32[1,1024]{1,0:T(1,128)S(1)} %get-tuple-element.47.row_ref, s32[1024,1]{1,0:T(8,128)S(1)} %copy.23.col_ref, bf16[256,256]{1,0:T(8,128)(2,1)S(1)} %copy-done.3, bf16[1024,256]{1,0:T(8,128)(2,1)S(1)} %shard_map.138.cot_ref), custom_call_target="tpu_custom_call" | custom-call | flops 536870912 | bytes 2097152 | tf_op jit(solution)/shard_map/pallas_call | solution.py:41
  64.1 8.2 %all-to-all-start.2 = ((bf16[128,8,256]{2,1,0:T(8,128)(2,1)}), bf16[128,8,256]{2,1,0:T(8,128)(2,1)S(1)}, u32[]{:S(2)}, u32[]{:S(2)}) async-start(bf16[128,8,256]{2,1,0:T(8,128)(2,1)} %bitcast.10), calls=%async_computation.2 | async-start | bytes 1048576 | tf_op jit(solution)/shard_map/all_to_all | solution.py:371
  72.3 6.2 %shard_map.142.agg_grad_ref = f32[256,256]{1,0:T(8,128)} custom-call(bf16[1024,256]{1,0:T(8,128)(2,1)} %bitcast.21, s32[1,1024]{1,0:T(1,128)} %copy-done.5, bf16[256,256]{1,0:T(8,128)(2,1)} %w_ref.3, bf16[2048,256]{1,0:T(8,128)(2,1)} %cot_ref.5), custom_call_target="tpu_custom_call" | custom-call | flops 536870912 | bytes 3145728 | tf_op jit(solution)/shard_map/pallas_call | solution.py:41
  78.5 7.8 %all-to-all-done.2 = bf16[128,8,256]{2,1,0:T(8,128)(2,1)S(1)} async-done(((bf16[128,8,256]{2,1,0:T(8,128)(2,1)}), bf16[128,8,256]{2,1,0:T(8,128)(2,1)S(1)}, u32[]{:S(2)}, u32[]{:S(2)}) %all-to-all-start.2) | async-done | bytes 524320 | tf_op jit(solution)/shard_map/all_to_all | solution.py:371
  86.3 0.8 copy-done.12
  87.1 0.9 copy-done.10
  88.0 16.3 %shard_map.143 = (f32[512,256]{1,0:T(8,128)}, bf16[8,512,768]{2,1,0:T(8,128)(2,1)}, bf16[512,512]{1,0:T(8,128)(2,1)S(1)}, bf16[512,512]{1,0:T(8,128)(2,1)S(1)}) custom-call(s32[1]{0:T(128)} %bitcast.core_ref, bf16[1024,256]{1,0:T(8,128)(2,1)} %bitcast.26, s32[8,512]{1,0:T(8,128)S(1)} %copy-done.4, bf16[512,256]{1,0:T(8,128)(2,1)S(1)} %copy-done.9, ...), custom_call_target="tpu_custom_call" | custom-call | flops 8053063680 | bytes 33554432 | tf_op jit(solution)/shard_map/pallas_call | solution.py:41
  104.3 0.5 collective-permute-start
  104.8 1.5 collective-permute-done.other_ref
  106.3 0.9 shard_map.144
  107.3 4.9 %all-to-all-start.3 = ((bf16[64,8,512]{2,1,0:T(8,128)(2,1)}), bf16[64,8,512]{2,1,0:T(8,128)(2,1)S(1)}, u32[]{:S(2)}, u32[]{:S(2)}) async-start(bf16[64,8,512]{2,1,0:T(8,128)(2,1)} %bitcast.12), calls=%async_computation.3 | async-start | bytes 1048576 | tf_op jit(solution)/shard_map/all_to_all | solution.py:371
  112.1 2.8 %copy-done.11 = bf16[8,512,768]{2,1,0:T(8,128)(2,1)S(1)} copy-done((bf16[8,512,768]{2,1,0:T(8,128)(2,1)S(1)}, bf16[8,512,768]{2,1,0:T(8,128)(2,1)}, u32[]{:S(2)}) %copy-start.11) | copy-done | bytes 6291480
  114.9 4.0 %shard_map.145 = (bf16[512,256]{1,0:T(8,128)(2,1)S(1)}, bf16[512,256]{1,0:T(8,128)(2,1)S(1)}) custom-call(s32[1]{0:T(128)} %bitcast.core_ref, bf16[8,512,768]{2,1,0:T(8,128)(2,1)S(1)} %copy-done.11, s32[8,512]{1,0:T(8,128)S(1)} %copy-done.4, bf16[768,256]{1,0:T(8,128)(2,1)S(1)} %bitcast.23), custom_call_target="tpu_custom_call" | custom-call | flops 3758096384 | bytes 6291456 | tf_op jit(solution)/shard_map/pallas_call | solution.py:41
  118.9 0.5 collective-permute-start.1
  119.7 0.8 collective-permute-done.1.pair_ref
  120.5 4.4 %all-to-all-done.3 = bf16[64,8,512]{2,1,0:T(8,128)(2,1)S(1)} async-done(((bf16[64,8,512]{2,1,0:T(8,128)(2,1)}), bf16[64,8,512]{2,1,0:T(8,128)(2,1)S(1)}, u32[]{:S(2)}, u32[]{:S(2)}) %all-to-all-start.3) | async-done | bytes 524320 | tf_op jit(solution)/shard_map/all_to_all | solution.py:371
  125.1 23.7 %all_to_all.25 = bf16[64,8,1024]{2,1,0:T(8,128)(2,1)S(1)} all-to-all(bf16[64,8,1024]{2,1,0:T(8,128)(2,1)S(1)} %bitcast.19), channel_id=1, replica_groups=mesh['group'=16,'core'=2,'sw'=4] {'group','sw'}, dimensions={0} | all-to-all | bytes 2097152 | tf_op jit(solution)/shard_map/all_to_all | solution.py:371
  148.8 1.8 %collective-permute-start.2 = (bf16[512,512]{1,0:T(8,128)(2,1)S(1)}, bf16[512,512]{1,0:T(8,128)(2,1)S(1)}, u32[]{:S(2)}, u32[]{:S(2)}) collective-permute-start(bf16[512,512]{1,0:T(8,128)(2,1)S(1)} %slice.4.mine_ref), channel_id=1, source_target_pairs={{0,4},{4,0},{1,5},{5,1},{2,6},{6,2},{3,7},{7,3},{8,12},{12,8},{9,1... | collective-permute-start | bytes 1572872 | tf_op jit(solution)/shard_map/ppermute | solution.py:365
  150.7 2.4 %shard_map.147 = f32[2048,256]{1,0:T(8,128)} custom-call(bf16[512,1024]{1,0:T(8,128)(2,1)S(1)} %bitcast.18, s32[1,512]{1,0:T(1,128)S(1)} %reshape.69.mine_ref, s32[1,512]{1,0:T(1,128)S(1)} %reshape.70.pair_ref, bf16[2048,256]{1,0:T(8,128)(2,1)S(1)} %copy-done.2), custom_call_target="tpu_custom_call" | custom-call | flops 1073741824 | bytes 4194304 | tf_op jit(solution)/shard_map/pallas_call | solution.py:41
  153.1 1.4 shard_map.148
  (43 shorter events, 1.4 us)
Async XLA Ops:
  0.6 0.7 copy-start.6
  1.3 1.2 copy-start.8
  2.5 13.8 %copy-start.7 = (s32[128,8]{0,1:T(8,128)S(1)}, s32[128,8]{0,1:T(8,128)}, u32[]{:S(2)}) copy-start(s32[128,8]{0,1:T(8,128)} %param.14) | copy-start | bytes 12292
  2.5 14.0 %copy-start.14 = (bf16[256,768]{1,0:T(8,128)(2,1)S(1)}, bf16[256,768]{1,0:T(8,128)(2,1)}, u32[]{:S(2)}) copy-start(bf16[256,768]{1,0:T(8,128)(2,1)} %wi_ref.3) | copy-start | bytes 1179652
  2.5 14.2 %copy-start.15 = (bf16[256,768]{1,0:T(8,128)(2,1)S(1)}, bf16[256,768]{1,0:T(8,128)(2,1)}, u32[]{:S(2)}) copy-start(bf16[256,768]{1,0:T(8,128)(2,1)} %ws_ref.3) | copy-start | bytes 1179652
  4.8 55.9 %copy-start.5 = (s32[1,1024]{1,0:T(1,128)}, s32[1,1024]{1,0:T(1,128)S(1)}, u32[]{:S(2)}) copy-start(s32[1,1024]{1,0:T(1,128)S(1)} %get-tuple-element.47.row_ref) | copy-start | bytes 12292
  4.8 12.1 %copy-start.1 = (bf16[2048,256]{1,0:T(8,128)(2,1)S(1)}, bf16[2048,256]{1,0:T(8,128)(2,1)}, u32[]{:S(2)}) copy-start(bf16[2048,256]{1,0:T(8,128)(2,1)} %cot_ref.5) | copy-start | bytes 3145732
  4.8 25.5 %all-to-all-start = ((bf16[128,8,256]{2,1,0:T(8,128)(2,1)}), bf16[128,8,256]{2,1,0:T(8,128)(2,1)S(1)}, u32[]{:S(2)}, u32[]{:S(2)}) async-start(bf16[128,8,256]{2,1,0:T(8,128)(2,1)} %bitcast.2), calls=%async_computation | async-start | bytes 1048576 | tf_op jit(solution)/shard_map/all_to_all | solution.py:371
  16.9 1.4 copy-start.16
  16.9 1.4 copy-start.17
  30.3 0.9 copy-start.13
  42.8 17.9 %all-to-all-start.1 = ((bf16[128,8,256]{2,1,0:T(8,128)(2,1)}), bf16[128,8,256]{2,1,0:T(8,128)(2,1)S(1)}, u32[]{:S(2)}, u32[]{:S(2)}) async-start(bf16[128,8,256]{2,1,0:T(8,128)(2,1)} %bitcast.28), calls=%async_computation.1 | async-start | bytes 1048576 | tf_op jit(solution)/shard_map/all_to_all | solution.py:371
  46.8 13.9 %copy-start.3 = (bf16[256,256]{1,0:T(8,128)(2,1)S(1)}, bf16[256,256]{1,0:T(8,128)(2,1)}, u32[]{:S(2)}) copy-start(bf16[256,256]{1,0:T(8,128)(2,1)} %w_ref.3) | copy-start | bytes 393220
  60.7 11.6 %copy-start = (bf16[128,8,256]{2,1,0:T(8,128)(2,1)}, bf16[128,8,256]{2,1,0:T(8,128)(2,1)S(1)}, u32[]{:S(2)}) copy-start(bf16[128,8,256]{2,1,0:T(8,128)(2,1)S(1)} %all-to-all-done.1) | copy-start | bytes 1572868
  60.7 26.4 %copy-start.4 = (s32[8,512]{1,0:T(8,128)S(1)}, s32[8,512]{1,0:T(8,128)}, u32[]{:S(2)}) copy-start(s32[8,512]{1,0:T(8,128)} %bitcast_select_fusion.row_ref) | copy-start | bytes 49156
  60.7 26.4 %copy-start.9 = (bf16[512,256]{1,0:T(8,128)(2,1)S(1)}, bf16[512,256]{1,0:T(8,128)(2,1)}, u32[]{:S(2)}) copy-start(bf16[512,256]{1,0:T(8,128)(2,1)} %cot_ref.4) | copy-start | bytes 786436
  64.1 22.2 %all-to-all-start.2 = ((bf16[128,8,256]{2,1,0:T(8,128)(2,1)}), bf16[128,8,256]{2,1,0:T(8,128)(2,1)S(1)}, u32[]{:S(2)}, u32[]{:S(2)}) async-start(bf16[128,8,256]{2,1,0:T(8,128)(2,1)} %bitcast.10), calls=%async_computation.2 | async-start | bytes 1048576 | tf_op jit(solution)/shard_map/all_to_all | solution.py:371
  86.3 0.8 copy-start.12
  87.1 1.0 copy-start.10
  104.3 2.0 %collective-permute-start = (bf16[512,512]{1,0:T(8,128)(2,1)S(1)}, bf16[512,512]{1,0:T(8,128)(2,1)S(1)}, u32[]{:S(2)}, u32[]{:S(2)}) collective-permute-start(bf16[512,512]{1,0:T(8,128)(2,1)S(1)} %get-tuple-element.74), channel_id=1, source_target_pairs={{0,4},{4,0},{1,5},{5,1},{2,6},{6,2},{3,7},{7,3},{8,12},{12,8},{9,1... | collective-permute-start | bytes 1572872 | tf_op jit(solution)/shard_map/ppermute | solution.py:365
  107.3 17.6 %all-to-all-start.3 = ((bf16[64,8,512]{2,1,0:T(8,128)(2,1)}), bf16[64,8,512]{2,1,0:T(8,128)(2,1)S(1)}, u32[]{:S(2)}, u32[]{:S(2)}) async-start(bf16[64,8,512]{2,1,0:T(8,128)(2,1)} %bitcast.12), calls=%async_computation.3 | async-start | bytes 1048576 | tf_op jit(solution)/shard_map/all_to_all | solution.py:371
  112.1 2.8 %copy-start.11 = (bf16[8,512,768]{2,1,0:T(8,128)(2,1)S(1)}, bf16[8,512,768]{2,1,0:T(8,128)(2,1)}, u32[]{:S(2)}) copy-start(bf16[8,512,768]{2,1,0:T(8,128)(2,1)} %get-tuple-element.75.da_ref) | copy-start | bytes 18874372
  118.9 1.6 %collective-permute-start.1 = (bf16[512,256]{1,0:T(8,128)(2,1)S(1)}, bf16[512,256]{1,0:T(8,128)(2,1)S(1)}, u32[]{:S(2)}, u32[]{:S(2)}) collective-permute-start(bf16[512,256]{1,0:T(8,128)(2,1)S(1)} %get-tuple-element.78), channel_id=1, source_target_pairs={{0,4},{4,0},{1,5},{5,1},{2,6},{6,2},{3,7},{7,3},{8,12},{12,8},{9,1... | collective-permute-start | bytes 786440 | tf_op jit(solution)/shard_map/ppermute | solution.py:365
  125.1 25.6 %copy-start.2 = (bf16[2048,256]{1,0:T(8,128)(2,1)S(1)}, bf16[2048,256]{1,0:T(8,128)(2,1)}, u32[]{:S(2)}) copy-start(bf16[2048,256]{1,0:T(8,128)(2,1)} %cot_ref.5) | copy-start | bytes 3145732
  148.8 4.3 %collective-permute-start.2 = (bf16[512,512]{1,0:T(8,128)(2,1)S(1)}, bf16[512,512]{1,0:T(8,128)(2,1)S(1)}, u32[]{:S(2)}, u32[]{:S(2)}) collective-permute-start(bf16[512,512]{1,0:T(8,128)(2,1)S(1)} %slice.4.mine_ref), channel_id=1, source_target_pairs={{0,4},{4,0},{1,5},{5,1},{2,6},{6,2},{3,7},{7,3},{8,12},{12,8},{9,1... | collective-permute-start | bytes 1572872 | tf_op jit(solution)/shard_map/ppermute | solution.py:365

commit v7 on v6

--- a/solution.py
+++ b/solution.py
@@ -219,10 +219,10 @@
 
 
 def backward_kernel(
-    core_ref, table_ref, row_ref, cot_ref, turned_ref, agg_grad_ref,
+    table_ref, row_ref, cot_ref, wi_ref, ws_ref, agg_grad_ref,
     fr_ref, fu_ref, fn_ref, fm_ref, fc_ref, xs_ref, cb_ref,
-    grad_ref, da_ref, mine_ref, other_ref,
-    table_s, f_s, fc_s, x_s, c_s, m_s, da_s, db_s, grads_s, sem, da_sem, table_sem,
+    grad_ref, da_ref, grads_ref,
+    table_s, f_s, fc_s, x_s, c_s, m_s, da_s, db_s, gi_s, gs_s, sem, da_sem, table_sem,
 ):
     _, hops, paths, width = f_s.shape
     slots = table_ref.shape[0]
@@ -268,21 +268,27 @@
             db_s[t, at, :width] = dr
             db_s[t, at, width : 2 * width] = du
             db_s[t, at, 2 * width :] = (d * f_s[3, t, at, :]).astype(BF16)
-            back = mm(db_s[t, at, :], turned_ref[...]).astype(BF16).astype(F32)
+            back = mm_t(db_s[t, at, :], ws_ref[...]).astype(BF16).astype(F32)
             grad_ref[at, :] = d * fc_s[t, at, :] + back
         save(t).start()
+    gi_s[...] = t_mm(flat(x_s), flat(da_s))
+    gs_s[...] = t_mm(flat(c_s), flat(db_s))
     two = 2 * width
-    for k, (left, right) in enumerate(((x_s, da_s), (c_s, db_s))):
-        grad = t_mm(flat(left), flat(right)).astype(BF16)
-        grads_s[k * width : (k + 1) * width, :] = grad[:, :two]
-        grads_s[two : 3 * width, k * width : (k + 1) * width] = grad[:, two:]
-    grads_s[3 * width :, :width] = agg_grad_ref[...].astype(BF16)
-    grads_s[3 * width :, width:] = jnp.zeros_like(agg_grad_ref).astype(BF16)
-    core = core_ref[0]
-    mine_ref[...] = grads_s[half_of(core, two), :]
-    other_ref[...] = grads_s[half_of(1 - core, two), :]
+    grads_ref[:width, :] = gi_s[:, :two].astype(BF16)
+    grads_ref[width:two, :] = gs_s[:, :two].astype(BF16)
+    grads_ref[two : 3 * width, :width] = gi_s[:, two:].astype(BF16)
+    grads_ref[two : 3 * width, width:] = gs_s[:, two:].astype(BF16)
+    grads_ref[3 * width :, :width] = agg_grad_ref[...].astype(BF16)
+    grads_ref[3 * width :, width:] = jnp.zeros_like(agg_grad_ref).astype(BF16)
     for t in order:
         save(t).wait()
+
+
+def split_kernel(core_ref, grads_ref, mine_ref, other_ref):
+    half = mine_ref.shape[0]
+    core = core_ref[0]
+    mine_ref[...] = grads_ref[half_of(core, half), :]
+    other_ref[...] = grads_ref[half_of(1 - core, half), :]
 
 
 def half_of(core, lines):
@@ -404,11 +410,8 @@
         (2 * slots * links * width, 2 * links * width, 16), send_row, link_cot,
     )
     input_turned = w_input.T
-    state_turned = w_state.T
-    table, cot_rows, send_col, count, slot_row, input_turned, state_turned = (
-        lax.optimization_barrier(
-            (table, cot_rows, send_col, count, slot_row, input_turned, state_turned)
-        )
+    table, cot_rows, send_col, count, slot_row, input_turned = lax.optimization_barrier(
+        (table, cot_rows, send_col, count, slot_row, input_turned)
     )
     sums, xs, cs = call(
         forward_kernel,
@@ -467,13 +470,12 @@
     )
     back_table, agg_grad = lax.optimization_barrier((back_table, agg_grad))
 
-    grad_path, da, mine, other = call(
+    grad_path, da, grads = call(
         backward_kernel,
         (
             shape((paths, width), F32),
             shape((hops, paths, gate_cols), BF16),
-            shape((2 * width, 2 * width), BF16),
-            shape((2 * width, 2 * width), BF16),
+            shape((4 * width, 2 * width), BF16),
         ),
         [
             pltpu.VMEM((slots, width), BF16),
@@ -484,16 +486,22 @@
             pltpu.VMEM((hops, paths, width), F32),
             pltpu.VMEM((hops, paths, gate_cols), BF16),
             pltpu.VMEM((hops, paths, gate_cols), BF16),
-            pltpu.VMEM((4 * width, 2 * width), BF16),
+            pltpu.VMEM((width, gate_cols), F32),
+            pltpu.VMEM((width, gate_cols), F32),
             pltpu.SemaphoreType.DMA((7, hops)),
             pltpu.SemaphoreType.DMA((hops,)),
             pltpu.SemaphoreType.DMA,
         ],
         (10 * hops * paths * width * gate_cols, 32 * hops * paths * width, 52),
-        core_at, back_table, slot_row, path_cot, state_turned, agg_grad,
+        back_table, slot_row, path_cot, w_input, w_state, agg_grad,
         *factors[:5], xs, factors[5],
-        in_specs=[SMEM, ANY] + [VMEM] * 4 + [ANY] * 7,
-        out_specs=(VMEM, ANY, VMEM, VMEM),
+        in_specs=[ANY] + [VMEM] * 5 + [ANY] * 7,
+        out_specs=(VMEM, ANY, VMEM),
+    )
+    grad_half = shape((2 * width, 2 * width), BF16)
+    mine, other = call(
+        split_kernel, (grad_half, grad_half), [], (slots * width, 4 * slots * width, 8),
+        core_at, grads, in_specs=[SMEM, VMEM],
     )
     added = call(
         pair_kernel, shape((slots // 2, 2 * width), BF16), [],

time: 155 us -> 153 us (0.987)
  Pallas kernels: 62 us -> 58.8 us
    pallas_call x11 -> x12, Pallas kernels: 49.9 us -> 46.7 us  [call(): pl.pallas_call(kernel, out_shape=outs, in_specs=in_specs or [VMEM] * len(...]
    unnamed x39 -> x40, local copies, waits for them, and re-layouts: 6.93 us -> 7.19 us
where the time goes in v7:
time: 153 us; the launch traced here: 152 us
  Pallas kernels  58.8 us (38%)
  starting transfers between devices  31.2 us (20%)
  waiting for transfers between devices  27.8 us (18%)
  blocking collectives  23.7 us (15%)
  local copies, waits for them, and re-layouts  8.71 us (6%)
    pallas_call x12, Pallas kernels, call(): pl.pallas_call(kernel, out_shape=outs, in_specs=in_specs or [VMEM] * len(...  46.7 us
    all_to_all x4, starting transfers between devices, exchange(): got = lax.all_to_all(chunks, axes, split_axis=0, concat_axis=0, tiled=True)  28.4 us
    all_to_all x4, waiting for transfers between devices, exchange(): got = lax.all_to_all(chunks, axes, split_axis=0, concat_axis=0, tiled=True)  25.5 us
    all_to_all x1, blocking collectives, exchange(): got = lax.all_to_all(chunks, axes, split_axis=0, concat_axis=0, tiled=True)  23.7 us
    pallas_call x1, Pallas kernels, per_device(): pl.pallas_call(factors_kernel, grid=(hops,), out_shape=(short,) * 4 + (fa...  12.1 us
    unnamed x40, local copies, waits for them, and re-layouts  7.19 us
  transfers between devices with their start and end apart: 7, of which 6 were waited for; matrix products, arithmetic and copies ran while one was open for 1% of the time, Pallas kernels for 17%

profile of v7, /device:TPU:1, one launch (start us, length us, event | category | flops | bytes accessed | tf_op | source)
XLA Modules:
  0.0 151.8 jit_solution(16712953675383883812)
XLA Ops:
  0.6 0.7 copy-done.9
  1.3 1.2 copy-done.11
  2.6 2.3 %shard_map.137 = (bf16[1024,256]{1,0:T(8,128)(2,1)}, s32[1,1024]{1,0:T(1,128)S(1)}) custom-call(s32[8,128]{1,0:T(8,128)S(1)} %bitcast.24, bf16[2048,256]{1,0:T(8,128)(2,1)S(1)} %copy-done.11), custom_call_target="tpu_custom_call" | custom-call | flops 1073741824 | bytes 1048576 | tf_op jit(solution)/shard_map/pallas_call | solution.py:41
  4.8 11.5 %all-to-all-start = ((bf16[128,8,256]{2,1,0:T(8,128)(2,1)}), bf16[128,8,256]{2,1,0:T(8,128)(2,1)S(1)}, u32[]{:S(2)}, u32[]{:S(2)}) async-start(bf16[128,8,256]{2,1,0:T(8,128)(2,1)} %bitcast.1), calls=%async_computation | async-start | bytes 1048576 | tf_op jit(solution)/shard_map/all_to_all | solution.py:377
  16.8 1.3 shard_map.138.cot_ref
  18.1 0.6 bitcast_select_fusion.row_ref
  18.7 11.6 %all-to-all-done = bf16[128,8,256]{2,1,0:T(8,128)(2,1)S(1)} async-done(((bf16[128,8,256]{2,1,0:T(8,128)(2,1)}), bf16[128,8,256]{2,1,0:T(8,128)(2,1)S(1)}, u32[]{:S(2)}, u32[]{:S(2)}) %all-to-all-start) | async-done | bytes 524320 | tf_op jit(solution)/shard_map/all_to_all | solution.py:377
  30.3 0.9 copy.19.count_ref
  31.2 11.5 %shard_map.139 = (bf16[1024,256]{1,0:T(8,128)(2,1)}, bf16[8,512,256]{2,1,0:T(8,128)(2,1)}, f32[8,512,256]{2,1,0:T(8,128)}) custom-call(bf16[1024,256]{1,0:T(8,128)(2,1)} %bitcast.25, s32[512,1]{1,0:T(8,128)} %copy.19.count_ref, s32[8,512]{1,0:T(8,128)} %bitcast_select_fusion.row_ref, bf16[512,256]{1,0:T(8,128)(2,1)} %start_ref.1, bf16[256,768]{1,0:T(8,128)(2,1)} %wi_ref.5, ...), custom_call_target="tpu_custom_call" | custom-call | flops 4294967296 | bytes 8388608 | tf_op jit(solution)/shard_map/pallas_call | solution.py:41
  42.7 3.8 %all-to-all-start.1 = ((bf16[128,8,256]{2,1,0:T(8,128)(2,1)}), bf16[128,8,256]{2,1,0:T(8,128)(2,1)S(1)}, u32[]{:S(2)}, u32[]{:S(2)}) async-start(bf16[128,8,256]{2,1,0:T(8,128)(2,1)} %bitcast.26), calls=%async_computation.1 | async-start | bytes 1048576 | tf_op jit(solution)/shard_map/all_to_all | solution.py:377
  46.8 12.1 %shard_map.140 = (bf16[8,512,256]{2,1,0:T(8,128)(2,1)}, bf16[8,512,256]{2,1,0:T(8,128)(2,1)}, bf16[8,512,256]{2,1,0:T(8,128)(2,1)}, bf16[8,512,256]{2,1,0:T(8,12...) custom-call(bf16[8,512,256]{2,1,0:T(8,128)(2,1)} %get-tuple-element.52.xs_ref, ...), custom_call_target="tpu_custom_call" | custom-call | flops 3221225472 | bytes 33554432 | tf_op jit(solution)/shard_map/pallas_call | solution.py:441
  59.0 1.7 %all-to-all-done.1 = bf16[128,8,256]{2,1,0:T(8,128)(2,1)S(1)} async-done(((bf16[128,8,256]{2,1,0:T(8,128)(2,1)}), bf16[128,8,256]{2,1,0:T(8,128)(2,1)S(1)}, u32[]{:S(2)}, u32[]{:S(2)}) %all-to-all-start.1) | async-done | bytes 524320 | tf_op jit(solution)/shard_map/all_to_all | solution.py:377
  60.7 3.4 %shard_map.141 = bf16[1024,256]{1,0:T(8,128)(2,1)} custom-call(bf16[1024,256]{1,0:T(8,128)(2,1)S(1)} %bitcast.19, s32[1,1024]{1,0:T(1,128)S(1)} %get-tuple-element.47.row_ref, s32[1024,1]{1,0:T(8,128)S(1)} %copy.21.col_ref, bf16[256,256]{1,0:T(8,128)(2,1)S(1)} %copy-done.6, bf16[1024,256]{1,0:T(8,128)(2,1)S(1)} %shard_map.138.cot_ref), custom_call_target="tpu_custom_call" | custom-call | flops 536870912 | bytes 2097152 | tf_op jit(solution)/shard_map/pallas_call | solution.py:41
  64.1 8.2 %all-to-all-start.2 = ((bf16[128,8,256]{2,1,0:T(8,128)(2,1)}), bf16[128,8,256]{2,1,0:T(8,128)(2,1)S(1)}, u32[]{:S(2)}, u32[]{:S(2)}) async-start(bf16[128,8,256]{2,1,0:T(8,128)(2,1)} %bitcast.8), calls=%async_computation.2 | async-start | bytes 1048576 | tf_op jit(solution)/shard_map/all_to_all | solution.py:377
  72.4 6.2 %shard_map.142.agg_grad_ref = f32[256,256]{1,0:T(8,128)} custom-call(bf16[1024,256]{1,0:T(8,128)(2,1)} %bitcast.20, s32[1,1024]{1,0:T(1,128)} %copy-done.8, bf16[256,256]{1,0:T(8,128)(2,1)} %w_ref.3, bf16[2048,256]{1,0:T(8,128)(2,1)} %cot_ref.5), custom_call_target="tpu_custom_call" | custom-call | flops 536870912 | bytes 3145728 | tf_op jit(solution)/shard_map/pallas_call | solution.py:41
  78.6 7.8 %all-to-all-done.2 = bf16[128,8,256]{2,1,0:T(8,128)(2,1)S(1)} async-done(((bf16[128,8,256]{2,1,0:T(8,128)(2,1)}), bf16[128,8,256]{2,1,0:T(8,128)(2,1)S(1)}, u32[]{:S(2)}, u32[]{:S(2)}) %all-to-all-start.2) | async-done | bytes 524320 | tf_op jit(solution)/shard_map/all_to_all | solution.py:377
  86.4 0.9 copy-done.14
  87.3 13.0 %shard_map.143 = (f32[512,256]{1,0:T(8,128)}, bf16[8,512,768]{2,1,0:T(8,128)(2,1)}, bf16[1024,512]{1,0:T(8,128)(2,1)}) custom-call(bf16[1024,256]{1,0:T(8,128)(2,1)S(1)} %bitcast.22, s32[8,512]{1,0:T(8,128)S(1)} %copy-done.7, bf16[512,256]{1,0:T(8,128)(2,1)S(1)} %copy-done.13, bf16[256,768]{1,0:T(8,128)(2,1)S(1)} %copy-done.5, ...), custom_call_target="tpu_custom_call" | custom-call | flops 8053063680 | bytes 33554432 | tf_op jit(solution)/shard_map/pallas_call | solution.py:41
  100.3 1.2 copy-done.3
  101.6 0.5 collective-permute-start
  102.1 1.5 %collective-permute-done.other_ref = bf16[512,512]{1,0:T(8,128)(2,1)S(1)} collective-permute-done((bf16[512,512]{1,0:T(8,128)(2,1)S(1)}, bf16[512,512]{1,0:T(8,128)(2,1)S(1)}, u32[]{:S(2)}, u32[]{:S(2)}) %collective-permute-start) | collective-permute-done | bytes 524320 | tf_op jit(solution)/shard_map/ppermute | solution.py:371
  103.6 0.9 shard_map.145
  104.5 4.9 %all-to-all-start.3 = ((bf16[64,8,512]{2,1,0:T(8,128)(2,1)}), bf16[64,8,512]{2,1,0:T(8,128)(2,1)S(1)}, u32[]{:S(2)}, u32[]{:S(2)}) async-start(bf16[64,8,512]{2,1,0:T(8,128)(2,1)} %bitcast.11), calls=%async_computation.3 | async-start | bytes 1048576 | tf_op jit(solution)/shard_map/all_to_all | solution.py:377
  109.4 2.8 %copy-done.15 = bf16[8,512,768]{2,1,0:T(8,128)(2,1)S(1)} copy-done((bf16[8,512,768]{2,1,0:T(8,128)(2,1)S(1)}, bf16[8,512,768]{2,1,0:T(8,128)(2,1)}, u32[]{:S(2)}) %copy-start.15) | copy-done | bytes 6291480
  112.2 4.0 %shard_map.146 = (bf16[512,256]{1,0:T(8,128)(2,1)S(1)}, bf16[512,256]{1,0:T(8,128)(2,1)S(1)}) custom-call(s32[1]{0:T(128)} %bitcast.10.core_ref, bf16[8,512,768]{2,1,0:T(8,128)(2,1)S(1)} %copy-done.15, s32[8,512]{1,0:T(8,128)S(1)} %copy-done.7, bf16[768,256]{1,0:T(8,128)(2,1)S(1)} %bitcast.23), custom_call_target="tpu_custom_call" | custom-call | flops 3758096384 | bytes 6291456 | tf_op jit(solution)/shard_map/pallas_call | solution.py:41
  116.1 0.5 collective-permute-start.1
  116.9 0.8 collective-permute-done.1.pair_ref
  117.8 4.4 %all-to-all-done.3 = bf16[64,8,512]{2,1,0:T(8,128)(2,1)S(1)} async-done(((bf16[64,8,512]{2,1,0:T(8,128)(2,1)}), bf16[64,8,512]{2,1,0:T(8,128)(2,1)S(1)}, u32[]{:S(2)}, u32[]{:S(2)}) %all-to-all-start.3) | async-done | bytes 524320 | tf_op jit(solution)/shard_map/all_to_all | solution.py:377
  122.4 23.7 %all_to_all.25 = bf16[64,8,1024]{2,1,0:T(8,128)(2,1)S(1)} all-to-all(bf16[64,8,1024]{2,1,0:T(8,128)(2,1)S(1)} %bitcast.18), channel_id=1, replica_groups=mesh['group'=16,'core'=2,'sw'=4] {'group','sw'}, dimensions={0} | all-to-all | bytes 2097152 | tf_op jit(solution)/shard_map/all_to_all | solution.py:377
  146.1 1.8 %collective-permute-start.2 = (bf16[512,512]{1,0:T(8,128)(2,1)S(1)}, bf16[512,512]{1,0:T(8,128)(2,1)S(1)}, u32[]{:S(2)}, u32[]{:S(2)}) collective-permute-start(bf16[512,512]{1,0:T(8,128)(2,1)S(1)} %slice.4.mine_ref), channel_id=1, source_target_pairs={{0,4},{4,0},{1,5},{5,1},{2,6},{6,2},{3,7},{7,3},{8,12},{12,8},{9,1... | collective-permute-start | bytes 1572872 | tf_op jit(solution)/shard_map/ppermute | solution.py:371
  147.9 2.4 %shard_map.148 = f32[2048,256]{1,0:T(8,128)} custom-call(bf16[512,1024]{1,0:T(8,128)(2,1)S(1)} %bitcast.17, s32[1,512]{1,0:T(1,128)S(1)} %reshape.69.mine_ref, s32[1,512]{1,0:T(1,128)S(1)} %reshape.70.pair_ref, bf16[2048,256]{1,0:T(8,128)(2,1)S(1)} %copy-done.2), custom_call_target="tpu_custom_call" | custom-call | flops 1073741824 | bytes 4194304 | tf_op jit(solution)/shard_map/pallas_call | solution.py:41
  150.4 1.4 shard_map.149
  (45 shorter events, 1.3 us)
Async XLA Ops:
  0.6 0.7 copy-start.9
  1.3 1.2 copy-start.11
  2.5 13.8 %copy-start.10 = (s32[128,8]{0,1:T(8,128)S(1)}, s32[128,8]{0,1:T(8,128)}, u32[]{:S(2)}) copy-start(s32[128,8]{0,1:T(8,128)} %param.14) | copy-start | bytes 12292
  2.5 14.0 %copy-start.4 = (bf16[256,768]{1,0:T(8,128)(2,1)S(1)}, bf16[256,768]{1,0:T(8,128)(2,1)}, u32[]{:S(2)}) copy-start(bf16[256,768]{1,0:T(8,128)(2,1)} %wi_ref.5) | copy-start | bytes 1179652
  2.5 14.2 %copy-start.1 = (bf16[2048,256]{1,0:T(8,128)(2,1)S(1)}, bf16[2048,256]{1,0:T(8,128)(2,1)}, u32[]{:S(2)}) copy-start(bf16[2048,256]{1,0:T(8,128)(2,1)} %cot_ref.5) | copy-start | bytes 3145732
  4.8 55.9 %copy-start.8 = (s32[1,1024]{1,0:T(1,128)}, s32[1,1024]{1,0:T(1,128)S(1)}, u32[]{:S(2)}) copy-start(s32[1,1024]{1,0:T(1,128)S(1)} %get-tuple-element.47.row_ref) | copy-start | bytes 12292
  4.8 25.5 %all-to-all-start = ((bf16[128,8,256]{2,1,0:T(8,128)(2,1)}), bf16[128,8,256]{2,1,0:T(8,128)(2,1)S(1)}, u32[]{:S(2)}, u32[]{:S(2)}) async-start(bf16[128,8,256]{2,1,0:T(8,128)(2,1)} %bitcast.1), calls=%async_computation | async-start | bytes 1048576 | tf_op jit(solution)/shard_map/all_to_all | solution.py:377
  16.7 1.4 copy-start.17
  16.7 1.4 copy-start.18
  30.3 0.9 copy-start.16
  42.7 17.9 %all-to-all-start.1 = ((bf16[128,8,256]{2,1,0:T(8,128)(2,1)}), bf16[128,8,256]{2,1,0:T(8,128)(2,1)S(1)}, u32[]{:S(2)}, u32[]{:S(2)}) async-start(bf16[128,8,256]{2,1,0:T(8,128)(2,1)} %bitcast.26), calls=%async_computation.1 | async-start | bytes 1048576 | tf_op jit(solution)/shard_map/all_to_all | solution.py:377
  46.8 13.9 %copy-start.6 = (bf16[256,256]{1,0:T(8,128)(2,1)S(1)}, bf16[256,256]{1,0:T(8,128)(2,1)}, u32[]{:S(2)}) copy-start(bf16[256,256]{1,0:T(8,128)(2,1)} %w_ref.3) | copy-start | bytes 393220
  60.7 11.7 %copy-start = (bf16[128,8,256]{2,1,0:T(8,128)(2,1)}, bf16[128,8,256]{2,1,0:T(8,128)(2,1)S(1)}, u32[]{:S(2)}) copy-start(bf16[128,8,256]{2,1,0:T(8,128)(2,1)S(1)} %all-to-all-done.1) | copy-start | bytes 1572868
  60.7 25.7 %copy-start.5 = (bf16[256,768]{1,0:T(8,128)(2,1)S(1)}, bf16[256,768]{1,0:T(8,128)(2,1)}, u32[]{:S(2)}) copy-start(bf16[256,768]{1,0:T(8,128)(2,1)} %wi_ref.5) | copy-start | bytes 1179652
  60.7 25.7 %copy-start.7 = (s32[8,512]{1,0:T(8,128)S(1)}, s32[8,512]{1,0:T(8,128)}, u32[]{:S(2)}) copy-start(s32[8,512]{1,0:T(8,128)} %bitcast_select_fusion.row_ref) | copy-start | bytes 49156
  60.7 25.6 %copy-start.12 = (bf16[256,768]{1,0:T(8,128)(2,1)S(1)}, bf16[256,768]{1,0:T(8,128)(2,1)}, u32[]{:S(2)}) copy-start(bf16[256,768]{1,0:T(8,128)(2,1)} %ws_ref.5) | copy-start | bytes 1179652
  60.7 25.6 %copy-start.13 = (bf16[512,256]{1,0:T(8,128)(2,1)S(1)}, bf16[512,256]{1,0:T(8,128)(2,1)}, u32[]{:S(2)}) copy-start(bf16[512,256]{1,0:T(8,128)(2,1)} %cot_ref.4) | copy-start | bytes 786436
  64.1 22.2 %all-to-all-start.2 = ((bf16[128,8,256]{2,1,0:T(8,128)(2,1)}), bf16[128,8,256]{2,1,0:T(8,128)(2,1)S(1)}, u32[]{:S(2)}, u32[]{:S(2)}) async-start(bf16[128,8,256]{2,1,0:T(8,128)(2,1)} %bitcast.8), calls=%async_computation.2 | async-start | bytes 1048576 | tf_op jit(solution)/shard_map/all_to_all | solution.py:377
  86.4 1.0 copy-start.14
  100.3 1.2 copy-start.3
  101.6 2.0 %collective-permute-start = (bf16[512,512]{1,0:T(8,128)(2,1)S(1)}, bf16[512,512]{1,0:T(8,128)(2,1)S(1)}, u32[]{:S(2)}, u32[]{:S(2)}) collective-permute-start(bf16[512,512]{1,0:T(8,128)(2,1)S(1)} %get-tuple-element.74), channel_id=1, source_target_pairs={{0,4},{4,0},{1,5},{5,1},{2,6},{6,2},{3,7},{7,3},{8,12},{12,8},{9,1... | collective-permute-start | bytes 1572872 | tf_op jit(solution)/shard_map/ppermute | solution.py:371
  104.5 17.6 %all-to-all-start.3 = ((bf16[64,8,512]{2,1,0:T(8,128)(2,1)}), bf16[64,8,512]{2,1,0:T(8,128)(2,1)S(1)}, u32[]{:S(2)}, u32[]{:S(2)}) async-start(bf16[64,8,512]{2,1,0:T(8,128)(2,1)} %bitcast.11), calls=%async_computation.3 | async-start | bytes 1048576 | tf_op jit(solution)/shard_map/all_to_all | solution.py:377
  109.4 2.8 %copy-start.15 = (bf16[8,512,768]{2,1,0:T(8,128)(2,1)S(1)}, bf16[8,512,768]{2,1,0:T(8,128)(2,1)}, u32[]{:S(2)}) copy-start(bf16[8,512,768]{2,1,0:T(8,128)(2,1)} %get-tuple-element.75.da_ref) | copy-start | bytes 18874372
  116.1 1.6 %collective-permute-start.1 = (bf16[512,256]{1,0:T(8,128)(2,1)S(1)}, bf16[512,256]{1,0:T(8,128)(2,1)S(1)}, u32[]{:S(2)}, u32[]{:S(2)}) collective-permute-start(bf16[512,256]{1,0:T(8,128)(2,1)S(1)} %get-tuple-element.78), channel_id=1, source_target_pairs={{0,4},{4,0},{1,5},{5,1},{2,6},{6,2},{3,7},{7,3},{8,12},{12,8},{9,1... | collective-permute-start | bytes 786440 | tf_op jit(solution)/shard_map/ppermute | solution.py:371
  122.3 25.6 %copy-start.2 = (bf16[2048,256]{1,0:T(8,128)(2,1)S(1)}, bf16[2048,256]{1,0:T(8,128)(2,1)}, u32[]{:S(2)}) copy-start(bf16[2048,256]{1,0:T(8,128)(2,1)} %cot_ref.5) | copy-start | bytes 3145732
  146.1 4.3 %collective-permute-start.2 = (bf16[512,512]{1,0:T(8,128)(2,1)S(1)}, bf16[512,512]{1,0:T(8,128)(2,1)S(1)}, u32[]{:S(2)}, u32[]{:S(2)}) collective-permute-start(bf16[512,512]{1,0:T(8,128)(2,1)S(1)} %slice.4.mine_ref), channel_id=1, source_target_pairs={{0,4},{4,0},{1,5},{5,1},{2,6},{6,2},{3,7},{7,3},{8,12},{12,8},{9,1... | collective-permute-start | bytes 1572872 | tf_op jit(solution)/shard_map/ppermute | solution.py:371
